TPU v7x, 512 devices: a whole 4x4x16 slice. The times are simulated.
512 devices in a mesh: dp: 128 (over y, z, core), mp: 4 (over x).
Axes of the slice: x: 4, y: 4, z: 16, core: 2. Of those that a mesh axis runs over, the one named last changes fastest.
Arguments:
- train_grads: bfloat16 [512, 64, 14336], P('dp', None, 'mp'), may hold values from -6 to 6
- train_acts: bfloat16 [512, 64, 4096], P('dp', None, 'mp'), may hold values from -6 to 6
- query_grads: bfloat16 [128, 64, 14336], P('dp', None, 'mp'), may hold values from -6 to 6
- query_acts: bfloat16 [128, 64, 4096], P('dp', None, 'mp'), may hold values from -6 to 6
- out_factor: bfloat16 [64, 14336], P(None, 'mp'), may hold values from -0.046875 to 0.046875
- in_factor: bfloat16 [64, 4096], P(None, 'mp'), may hold values from -0.09375 to 0.09375
- train_lengths: int32 [512], P('dp'), may hold values from 16 to 64
- query_lengths: int32 [128], P('dp'), may hold values from 16 to 64
Outputs:
- scores: float32 [512, 128], P('dp', 'mp')
Inputs may be any that keep to these rules, and one draw needn't show every extreme that they name: `train_lengths`: the number of real tokens of each training example; they are its first positions. `query_lengths`: the number of real tokens of each query example; they are its first positions.
All inputs are finite; a program needn't handle non-finite values.
Results may differ from a plain program's by a relative error of at most 0.0003.
Values sent between devices are 32-bit elements; how exact they have to be, the bound alone decides.
No kernel may reach another device: no remote copies, remote signals or barrier semaphores. Data moves between devices by JAX's collectives and lax.ppermute only.
A program may use at most 128 MiB of HBM per device.

v0:
```python
import jax
import jax.numpy as jnp
from jax import lax
from jax.sharding import PartitionSpec as P

damping = 2.0


def project_rows(grads, activations, out_factor, in_factor):
    examples = grads.shape[0]
    positions = grads.shape[1]
    projected_out = jnp.einsum(
        "tf,rf->tr",
        grads.reshape(examples * positions, grads.shape[2]),
        out_factor,
        preferred_element_type=jnp.float32,
    )
    projected_in = jnp.einsum(
        "td,rd->tr",
        activations.reshape(examples * positions, activations.shape[2]),
        in_factor,
        preferred_element_type=jnp.float32,
    )
    return (
        projected_out.reshape(examples, positions, -1),
        projected_in.reshape(examples, positions, -1),
    )


def token_weights(lengths, positions, average):
    position = jnp.arange(positions, dtype=jnp.int32)
    weights = (position[None, :] < lengths[:, None]).astype(jnp.float32)
    if average:
        weights = weights / lengths[:, None].astype(jnp.float32)
    return weights


def outer_sum(projected_out, projected_in, weights):
    sketch = jnp.einsum(
        "eti,etj->eij",
        projected_out * weights[:, :, None],
        projected_in,
        precision=lax.Precision.HIGHEST,
    )
    return sketch.reshape(sketch.shape[0], -1)


def full_products(all_train, all_query, model_index, block):
    gram = jnp.dot(
        all_train, all_train.T, precision=lax.Precision.HIGHEST, preferred_element_type=jnp.float32
    )
    query_block = lax.dynamic_slice_in_dim(all_query, model_index * block, block, 0)
    cross = jnp.dot(
        all_train,
        query_block.T,
        precision=lax.Precision.HIGHEST,
        preferred_element_type=jnp.float32,
    )
    return (gram, cross)


def shards(
    train_grads,
    train_acts,
    query_grads,
    query_acts,
    out_factor,
    in_factor,
    train_lengths,
    query_lengths,
):
    positions = train_grads.shape[1]
    rank_out = out_factor.shape[0]
    train_weights = token_weights(train_lengths, positions, True)
    query_weights = token_weights(query_lengths, positions, False)
    train_out, train_in = project_rows(train_grads, train_acts, out_factor, in_factor)
    query_out, query_in = project_rows(query_grads, query_acts, out_factor, in_factor)
    train_examples = train_out.shape[0]
    query_examples = query_out.shape[0]
    train_both = jnp.concatenate([train_out, train_in], axis=2).reshape(train_examples, -1)
    query_both = jnp.concatenate([query_out, query_in], axis=2).reshape(query_examples, -1)
    train_both, query_both = lax.psum((train_both, query_both), "mp")
    train_both = train_both.reshape(train_examples, positions, -1)
    query_both = query_both.reshape(query_examples, positions, -1)
    train_sketch = outer_sum(
        train_both[:, :, :rank_out], train_both[:, :, rank_out:], train_weights
    )
    query_sketch = outer_sum(
        query_both[:, :, :rank_out], query_both[:, :, rank_out:], query_weights
    )
    model_parts = lax.axis_size("mp")
    model_index = lax.axis_index("mp")
    data_parts = lax.axis_size("dp")
    data_index = lax.axis_index("dp")
    block = query_examples * data_parts // model_parts
    all_train, all_query = (
        lax.all_gather(train_sketch, "dp", axis=0, tiled=True),
        lax.all_gather(query_sketch, "dp", axis=0, tiled=True),
    )
    gram, cross = full_products(all_train, all_query, model_index, block)
    damped = gram + damping * jnp.eye(gram.shape[0], dtype=jnp.float32)
    factor = jnp.linalg.cholesky(damped)
    solved = jax.scipy.linalg.cho_solve((factor, True), cross)
    return lax.dynamic_slice_in_dim(solved, data_index * train_examples, train_examples, 0)


def solution(mesh):
    return jax.shard_map(
        shards,
        mesh=mesh,
        in_specs=(
            P("dp", None, "mp"),
            P("dp", None, "mp"),
            P("dp", None, "mp"),
            P("dp", None, "mp"),
            P(None, "mp"),
            P(None, "mp"),
            P("dp"),
            P("dp"),
        ),
        out_specs=P("dp", "mp"),
        check_vma=False,
    )
```

profile of v0, /device:TPU:1, one launch (start us, length us, event | category | flops | bytes accessed | tf_op | source)
XLA Modules:
  0.0 528.0 jit_solution(11955485615938561649)
XLA Ops:
  7.4 1.5 fusion.21
  9.1 1.6 fusion.6
  10.7 0.8 pad_maximum_fusion
  11.5 1.1 convolution_bitcast_fusion
  12.7 1.4 convolution_bitcast_fusion.1
  14.2 14.5 %psum.15 = f32[1,64,128]{2,1,0:T(8,128)S(1)} all-reduce(f32[1,64,128]{2,1,0:T(8,128)S(1)} %pad_maximum_fusion.1), channel_id=1, replica_groups=mesh['dp'=128,'mp'=4] {'mp'}, use_global_device_ids=true, to_apply=%region_9.10 | all-reduce | flops 8192 | bytes 65536 | tf_op jit(solution)/shard_map/psum | solution.py:82
  29.6 0.7 reshape.184
  30.4 0.7 convert_element_type.22
  31.0 0.7 convert_divide_fusion
  31.8 39.7 %all-reduce.3.cloned.1.call-done = f32[4,64,128]{2,1,0:T(8,128)} async-done(((f32[4,64,128]{2,1,0:T(8,128)}), f32[4,64,128]{2,1,0:T(8,128)}) %all-reduce.3.cloned.1.call-update) | async-done | bytes 131088 | tf_op jit(solution)/shard_map/psum | solution.py:82
  71.5 1.5 fusion.18
  72.9 0.7 reshape.182
  73.7 103.9 %all-gather.7.cloned.1.call-done = f32[128,1,4096]{2,1,0:T(1,128)} async-done(((f32[1,1,4096]{2,1,0:T(1,128)}), f32[128,1,4096]{2,1,0:T(1,128)}) %all-gather.7.cloned.1.call-update) | async-done | bytes 2097168 | tf_op jit(solution)/shard_map/all_gather | solution.py:98
  177.6 1.1 constant_dynamic-slice_fusion.1
  178.7 146.8 %all-gather.5.cloned.1.call-done = f32[128,4,4096]{2,1,0:T(4,128)} async-done(((f32[1,4,4096]{2,1,0:T(4,128)}), f32[128,4,4096]{2,1,0:T(4,128)}) %all-gather.5.cloned.1.call-update) | async-done | bytes 8388624 | tf_op jit(solution)/shard_map/all_gather | solution.py:97
  325.4 10.0 %reshape.183 = f32[512,4096]{1,0:T(8,128)} reshape(f32[128,4,4096]{2,1,0:T(4,128)} %all-gather.5.cloned.1.call-done) | data formatting | bytes 16777216
  335.4 16.9 %fusion.68 = f32[512,512]{1,0:T(8,128)S(1)} fusion(f32[512,4096]{1,0:T(8,128)} %reshape.183), kind=kOutput, calls=%fused_computation.122 | convolution fusion | flops 12884901888 | bytes 9437184 | tf_op jit(solution)/shard_map/dot_general | solution.py:49
  352.3 1.4 copy.13
  353.7 1.4 fusion.1
  355.1 1.1 copy-done.2
  356.2 11.7 %cholesky.103 = f32[128,128]{1,0:T(8,128)S(1)} custom-call(f32[128,128]{1,0:T(8,128)S(1)} %cholesky.263), custom_call_target="Cholesky" | custom-call | tf_op jit(solution)/shard_map/jit(cholesky)/cholesky | solution.py:102
  368.0 9.8 %custom-call.34 = f32[1,128,128]{1,2,0:T(8,128)S(1)} custom-call(f32[1,128,128]{2,1,0:T(8,128)S(1)} %get-tuple-element.32), custom_call_target="InvertDiagBlocksLowerTriangular" | custom-call | tf_op jit(solution)/shard_map/jit(cholesky)/cholesky | solution.py:102
  377.9 1.2 constant_dynamic-update-slice_fusion
  379.1 1.3 convolution_subtract_fusion
  380.4 0.7 copy-done.4
  381.1 11.7 %cholesky.215 = f32[128,128]{1,0:T(8,128)S(1)} custom-call(f32[128,128]{1,0:T(8,128)S(1)} %cholesky.267), custom_call_target="Cholesky" | custom-call | tf_op jit(solution)/shard_map/jit(cholesky)/cholesky | solution.py:102
  392.8 9.9 %custom-call.35 = f32[1,128,128]{1,2,0:T(8,128)S(1)} custom-call(f32[1,128,128]{2,1,0:T(8,128)S(1)} %get-tuple-element.29), custom_call_target="InvertDiagBlocksLowerTriangular" | custom-call | tf_op jit(solution)/shard_map/jit(cholesky)/cholesky | solution.py:102
  402.8 1.2 convolution_dynamic-update-slice_fusion
  404.0 1.3 convolution_subtract_fusion.1
  405.2 0.6 cholesky.272
  405.9 13.2 %cholesky.236 = f32[128,128]{1,0:T(8,128)} custom-call(f32[128,128]{1,0:T(8,128)} %cholesky.272), custom_call_target="Cholesky" | custom-call | tf_op jit(solution)/shard_map/jit(cholesky)/cholesky | solution.py:102
  419.0 1.5 select_reduce_fusion.1
  420.5 0.7 compare_reduce_fusion.1
  421.2 11.3 %custom-call.36 = f32[1,128,128]{1,2,0:T(8,128)} custom-call(f32[1,128,128]{2,1,0:T(8,128)} %get-tuple-element.26), custom_call_target="InvertDiagBlocksLowerTriangular" | custom-call | tf_op jit(solution)/shard_map/jit(cholesky)/cholesky | solution.py:102
  432.5 1.0 convolution_dynamic-update-slice_fusion.1
  433.5 1.2 convolution_subtract_fusion.2
  434.8 11.7 %cholesky.253 = f32[128,128]{1,0:T(8,128)S(1)} custom-call(f32[128,128]{1,0:T(8,128)S(1)} %convolution_subtract_fusion.2), custom_call_target="Cholesky" | custom-call | tf_op jit(solution)/shard_map/jit(cholesky)/cholesky | solution.py:102
  446.5 0.6 compare_reduce_fusion
  447.1 0.6 compare_reduce_fusion.2
  450.2 1.4 select_select_fusion
  451.6 14.3 %while.1 = (s32[]{:T(128)}, f32[512,512]{1,0:T(8,128)}, s32[4,2]{0,1:T(2,128)S(1)}, f32[4,128,128]{2,1,0:T(8,128)}, s32[]{:T(128)}) while((s32[]{:T(128)}, f32[512,512]{1,0:T(8,128)}, s32[4,2]{0,1:T(2,128)S(1)}, f32[4,128,128]{2,1,0:T(8,128)}, s32[]{:T(128)}) %tuple.27), condition=%wide.while_cond, body=%wide.while_body.sunk | while | flops 2 | bytes 132705 | solution.py:103
  452.3 2.9 bitcast_dynamic-update-slice_fusion.2
  455.9 2.9 bitcast_dynamic-update-slice_fusion.2
  459.5 2.9 bitcast_dynamic-update-slice_fusion.2
  463.1 2.9 bitcast_dynamic-update-slice_fusion.2
  465.9 40.8 %custom-call.37 = f32[4,128,128]{1,2,0:T(8,128)} custom-call(f32[4,128,128]{2,1,0:T(8,128)} %get-tuple-element.12), custom_call_target="InvertDiagBlocksLowerTriangular" | custom-call | tf_op jit(solution)/shard_map/jit(_cho_solve)/triangular_solve | solution.py:103
  506.7 9.6 %fusion.2 = f32[512,32]{0,1:T(8,128)S(1)} fusion(f32[512,4096]{1,0:T(8,128)} %reshape.183, f32[32,1,4096]{2,1,0:T(1,128)S(1)} %constant_dynamic-slice_fusion.1), kind=kOutput, calls=%fused_computation.22 | convolution fusion | flops 805306368 | bytes 8978432 | tf_op jit(solution)/shard_map/dot_general | solution.py:53
  519.7 0.7 copy.14
  (49 shorter events, 6.8 us)
Async XLA Ops:
  7.4 1.7 copy-start
  7.4 64.1 %all-reduce.3.cloned.1.call-start = ((), (), s32[]{:S(2)}) async-start(), calls=%async_computation | async-start | bytes 262144 | tf_op jit(solution)/shard_map/psum | solution.py:82
  11.5 166.1 %all-gather.7.cloned.1.call-start = ((), (), s32[]{:S(2)}) async-start(), calls=%async_computation.2 | async-start | bytes 2113536 | tf_op jit(solution)/shard_map/all_gather | solution.py:98
  30.3 295.1 %all-gather.5.cloned.1.call-start = ((), (), s32[]{:S(2)}) async-start(), calls=%async_computation.1 | async-start | bytes 8454144 | tf_op jit(solution)/shard_map/all_gather | solution.py:97
  355.1 1.1 copy-start.2
  380.4 0.7 copy-start.4
  465.9 50.6 %copy-start.1 = (f32[512,512]{1,0:T(8,128)S(1)}, f32[512,512]{1,0:T(8,128)}, u32[]{:S(2)}) copy-start(f32[512,512]{1,0:T(8,128)} %get-tuple-element.85) | copy-start | bytes 3145732
  506.7 9.6 %copy-start.3 = (f32[4,128,128]{1,2,0:T(8,128)S(1)}, f32[4,128,128]{1,2,0:T(8,128)}, u32[]{:S(2)}) copy-start(f32[4,128,128]{1,2,0:T(8,128)} %custom-call.37) | copy-start | bytes 786436
Sparse Core Ops, SparseCore 0:
  11.6 59.8 all-reduce.2
Sparse Core Ops, SparseCore 1:
  30.4 147.1 all-gather.6
  181.1 144.3 all-gather.4
where the time goes:
time: 534 us; the launch traced here: 528 us
  waiting for transfers between devices  290 us (54%)
  other arithmetic  129 us (24%)
  matrix products  44.1 us (8%)
  local copies, waits for them, and re-layouts  31.5 us (6%)
  between operations  18.5 us (3%)
  blocking collectives  14.5 us (3%)
    all_gather x1, waiting for transfers between devices, shards(): lax.all_gather(train_sketch, 'dp', axis=0, tiled=True)  147 us
    all_gather x1, waiting for transfers between devices, shards(): lax.all_gather(query_sketch, 'dp', axis=0, tiled=True)  104 us
    another operation x14, other arithmetic, shards(): factor = jnp.linalg.cholesky(damped)  82.9 us
    another operation x4, other arithmetic, shards(): solved = jax.scipy.linalg.cho_solve((factor, True), cross)  42.3 us
    psum x1, waiting for transfers between devices, shards(): train_both, query_both = lax.psum((train_both, query_both), 'mp')  39.7 us
    dot_general x1, matrix products, full_products(): jnp.dot(all_train, all_train.T, precision=lax.Precision.HIGHEST, preferre...  16.9 us
    psum x1, blocking collectives, shards(): train_both, query_both = lax.psum((train_both, query_both), 'mp')  14.5 us
    another operation x12, local copies, waits for them, and re-layouts  14.3 us
  transfers between devices with their start and end apart: 3, of which 3 were waited for; matrix products, arithmetic and copies ran while one was open for 2% of the time, Pallas kernels for 0%

commit v1 on v0

v1 whole, which is shorter than its diff:
```python
import jax
import jax.numpy as jnp
from jax import lax
from jax.experimental import pallas as pl
from jax.experimental.pallas import tpu as pltpu
from jax.sharding import PartitionSpec as P

damping = 2.0
F32 = jnp.float32
HIGHEST = lax.Precision.HIGHEST
VMEM_LIMIT = 40 * 1024 * 1024

NY, NZ, NC = 4, 16, 2
VM = pl.BlockSpec(memory_space=pltpu.VMEM)
SM = pl.BlockSpec(memory_space=pltpu.SMEM)


def params():
    return pltpu.CompilerParams(vmem_limit_bytes=VMEM_LIMIT)


def dot(a, b, ca, cb, precision=HIGHEST):
    return lax.dot_general(
        a, b, (((ca,), (cb,)), ((), ())), precision=precision, preferred_element_type=F32
    )


def project_kernel(tg, ta, qg, qa, of, inf, out):
    n = tg.shape[0] * tg.shape[1]
    out[0:n, 0:64] = dot(tg[...].reshape(n, tg.shape[2]), of[...], 1, 1, None)
    out[0:n, 64:128] = dot(ta[...].reshape(n, ta.shape[2]), inf[...], 1, 1, None)
    m = n + qg.shape[1]
    out[n:m, 0:64] = dot(qg[0], of[...], 1, 1, None)
    out[n:m, 64:128] = dot(qa[0], inf[...], 1, 1, None)


def project(tg, ta, qg, qa, of, inf):
    return pl.pallas_call(
        project_kernel,
        out_shape=jax.ShapeDtypeStruct((320, 128), F32),
        in_specs=[VM] * 6,
        out_specs=VM,
        compiler_params=params(),
        name="project",
    )(tg, ta, qg, qa, of, inf)


def sketch_kernel(pos, tlen, qlen, p0, p1, p2, p3, train, both, sums, square):
    sums[...] = (p0[...] + p1[...]) + (p2[...] + p3[...])
    row = pl.multiple_of(pos[0] * 16, 16)
    token = lax.broadcasted_iota(jnp.int32, (64, 128), 0)
    lane = lax.broadcasted_iota(jnp.int32, (8, 128), 1)
    for e in range(5):
        length = tlen[e] if e < 4 else qlen[0]
        real = (token < length).astype(F32)
        if e < 4:
            real = real / jnp.full((64, 128), length, jnp.int32).astype(F32)
        x = sums[64 * e : 64 * e + 64, :]
        square[...] = dot(x * real, x, 0, 0)
        low = square[pl.ds(row, 8), :]
        high = square[pl.ds(row + 8, 8), :]
        tile = jnp.where(lane < 64, pltpu.roll(low, 64, 1), high)
        if e < 4:
            train[8 * e : 8 * e + 8, :] = tile
        both[8 * e : 8 * e + 8, :] = tile


def sketch(pos, tlen, qlen, parts):
    return pl.pallas_call(
        sketch_kernel,
        out_shape=(
            jax.ShapeDtypeStruct((32, 128), F32),
            jax.ShapeDtypeStruct((40, 128), F32),
        ),
        in_specs=[SM] * 3 + [VM] * 4,
        out_specs=(VM, VM),
        scratch_shapes=[pltpu.VMEM((320, 128), F32), pltpu.VMEM((128, 128), F32)],
        compiler_params=params(),
        name="sketch",
    )(pos, tlen, qlen, *parts)


def tile_kernel(pos, *refs):
    line = refs[:NZ]
    plane = refs[NZ : NZ + 8]
    out, rows, cols = refs[NZ + 8 :]
    y, z, c = pos[1], pos[2], pos[3]
    for t in range(NZ):
        at = lax.rem(z + t, NZ)
        for i in range(4):
            start = pl.multiple_of((i * NZ + at) * 8, 8)
            rows[pl.ds(start, 8), :] = line[t][8 * i : 8 * i + 8, :]
    for h in range(2):
        cols[(24 * h + 20) * 8 : (24 * h + 24) * 8, :] = jnp.zeros((32, 128), F32)
    for t in range(8):
        oy = lax.rem(y + t // 2, NY)
        oc = lax.rem(c + t % 2, NC)
        b = oy * 2 + oc
        start = pl.multiple_of(((b // 4) * 24 + lax.rem(b, 4) * 4) * 8, 8)
        cols[pl.ds(start, 32), :] = plane[t][0:32, :]
        start = pl.multiple_of((oc * 24 + 16 + oy) * 8, 8)
        cols[pl.ds(start, 8), :] = plane[t][32:40, :]
    total = jnp.zeros((48, 64), F32)
    for s in range(8):
        total += dot(cols[pl.ds(s, 48, stride=8), :], rows[pl.ds(s, 64, stride=8), :], 1, 1)
    out[:, 0:64] = total[0:24]
    out[:, 64:128] = total[24:48]


def tile(pos, line, plane):
    return pl.pallas_call(
        tile_kernel,
        out_shape=jax.ShapeDtypeStruct((24, 128), F32),
        in_specs=[SM] + [VM] * (NZ + 8),
        out_specs=VM,
        scratch_shapes=[pltpu.VMEM((512, 128), F32), pltpu.VMEM((384, 128), F32)],
        compiler_params=params(),
        name="tile",
    )(pos, *line, *plane)


def add_kernel(pos, p0, p1, p2, p3, out, sums):
    sums[...] = (p0[...] + p1[...]) + (p2[...] + p3[...])
    out[0:16, :] = sums[0:16, :]
    own = lax.broadcasted_iota(jnp.int32, (8, 128), 0) == pos[0]
    query = jnp.sum(jnp.where(own, sums[16:24, :], 0.0), axis=0, keepdims=True)
    out[16:24, :] = jnp.broadcast_to(query, (8, 128))


def add(pos, parts):
    return pl.pallas_call(
        add_kernel,
        out_shape=jax.ShapeDtypeStruct((24, 128), F32),
        in_specs=[SM] + [VM] * 4,
        out_specs=VM,
        scratch_shapes=[pltpu.VMEM((24, 128), F32)],
        compiler_params=params(),
        name="add",
    )(pos, *parts)


def panel_kernel(pos, *refs):
    parts = refs[:NZ]
    out, held = refs[NZ:]
    for t in range(NZ):
        held[lax.rem(pos[2] + t, NZ)] = parts[t][...]
    for z in range(NZ):
        out[pl.ds(z, 16, stride=NZ), :] = held[z, 0:16, :]
        out[256 + z : 257 + z, :] = held[z, 16:17, :]


def panel(pos, parts):
    return pl.pallas_call(
        panel_kernel,
        out_shape=jax.ShapeDtypeStruct((272, 128), F32),
        in_specs=[SM] + [VM] * NZ,
        out_specs=VM,
        scratch_shapes=[pltpu.VMEM((NZ, 24, 128), F32)],
        compiler_params=params(),
        name="panel",
    )(pos, *parts)


def inverse_factor(tiles):
    lane = lax.broadcasted_iota(jnp.int32, (8, 128), 1)
    count = len(tiles)
    tiles = list(tiles)
    for q in range(count):
        first = 8 * q
        block = tiles[q]
        a = {}
        for c in range(8):
            for p in range(c, 8):
                one = block[p : p + 1, first + c : first + c + 1]
                a[p, c] = jnp.broadcast_to(one, (8, 128))
        w = {}
        low = {}
        for p in range(8):
            scale = lax.rsqrt(a[p, p])
            for k in range(p + 1, 8):
                low[k, p] = a[k, p] * scale
            for k in range(p + 1, 8):
                for c in range(p + 1, k + 1):
                    a[k, c] = a[k, c] - low[k, p] * low[c, p]
            w[p, p] = scale
            for c in range(p):
                part = low[p, c] * w[c, c]
                for k in range(c + 1, p):
                    part = part + low[p, k] * w[k, c]
                w[p, c] = -(part * scale)
        inside = (lane >= first) & (lane < first + 8)
        raw = []
        for c in range(8):
            line = jnp.broadcast_to(block[c : c + 1, :], (8, 128))
            unit = (lane == first + c).astype(F32)
            raw.append(jnp.where(inside, unit, line))
        lines = []
        for p in range(8):
            line = w[p, 0] * raw[0]
            for c in range(1, p + 1):
                line = line + w[p, c] * raw[c]
            lines.append(line)
        sub = lax.broadcasted_iota(jnp.int32, (8, 128), 0)
        merged = lines[0]
        for p in range(1, 8):
            merged = jnp.where(sub == p, lines[p], merged)
        tiles[q] = merged
        for r in range(q + 1, count):
            cols = [
                jnp.broadcast_to(tiles[r][:, first + c : first + c + 1], (8, 128))
                for c in range(8)
            ]
            update = None
            for p in range(8):
                part = w[p, 0] * cols[0]
                for c in range(1, p + 1):
                    part = part + w[p, c] * cols[c]
                update = part * lines[p] if update is None else update + part * lines[p]
            tiles[r] = jnp.where(inside, 0.0, tiles[r]) - update
    for q in range(count):
        row = lax.broadcasted_iota(jnp.int32, (8, 128), 0) + 8 * q
        tiles[q] = jnp.where(lane <= row, tiles[q], 0.0)
    return tiles


def solve_kernel(pos, *refs):
    panels = refs[:8]
    out, order, full, inv, x = refs[8:]
    m, y, z, c = pos[0], pos[1], pos[2], pos[3]
    lane = lax.broadcasted_iota(jnp.int32, (256, 128), 1)
    left = lane < 64
    for t in range(8):
        b = lax.rem(y + t // 2, NY) * 2 + lax.rem(c + t % 2, NC)
        order[b] = panels[t][...]
    for j in range(NY):
        even = order[2 * j, 0:256, :]
        odd = order[2 * j + 1, 0:256, :]
        full[0:256, 128 * j : 128 * j + 128] = jnp.where(left, even, pltpu.roll(odd, 64, 1))
        full[256:512, 128 * j : 128 * j + 128] = jnp.where(left, pltpu.roll(even, 64, 1), odd)
    for b in range(8):
        both = order[b, 256:272, :]
        stacked = jnp.concatenate([both, both, both, both, both, both, both, both], axis=0)
        turned = stacked.T
        lane1 = lax.broadcasted_iota(jnp.int32, (64, 128), 1)
        pick = jnp.where(lane1 < 16, turned[0:64, :], turned[64:128, :])
        full[64 * b : 64 * b + 64, 512:640] = jnp.where(lane1 < 32, pick, 0.0)
    eye = (
        lax.broadcasted_iota(jnp.int32, (128, 128), 0)
        == lax.broadcasted_iota(jnp.int32, (128, 128), 1)
    ).astype(F32) * damping
    for k in range(4):
        s = slice(128 * k, 128 * k + 128)
        full[s, s] = full[s, s] + eye

    def step(k, carry):
        at = pl.multiple_of(k * 128, 128)
        tiles = [full[pl.ds(at + 8 * t, 8), pl.ds(at, 128)] for t in range(16)]
        tiles = inverse_factor(tiles)
        for t in range(16):
            inv[k, 8 * t : 8 * t + 8, :] = tiles[t]
        strip = dot(inv[k], full[pl.ds(at, 128), :], 1, 0)
        full[pl.ds(at, 128), :] = strip

        def trail(i, inner):
            to = pl.multiple_of(i * 128, 128)
            mine = full[pl.ds(at, 128), pl.ds(to, 128)]
            full[pl.ds(to, 128), :] -= dot(mine, full[pl.ds(at, 128), :], 0, 0)
            return inner

        return lax.fori_loop(k + 1, 4, trail, carry)

    lax.fori_loop(0, 4, step, 0)
    for k in (3, 2, 1, 0):
        s = slice(128 * k, 128 * k + 128)
        rest = full[s, 512:640]
        if k < 3:
            rest = rest - dot(full[s, 128 * k + 128 : 512], x[128 * k + 128 : 512, :], 1, 0)
        x[s, :] = dot(inv[k], rest, 0, 0)
    sub = lax.broadcasted_iota(jnp.int32, (8, 128), 0)
    for i in range(4):
        start = pl.multiple_of((y * 2 + c) * 64 + i * 16 + (z // 8) * 8, 8)
        eight = x[pl.ds(start, 8), :]
        one = jnp.sum(jnp.where(sub == lax.rem(z, 8), eight, 0.0), axis=0, keepdims=True)
        out[i : i + 1, :] = one


def solve(pos, panels):
    return pl.pallas_call(
        solve_kernel,
        out_shape=jax.ShapeDtypeStruct((4, 128), F32),
        in_specs=[SM] + [VM] * 8,
        out_specs=VM,
        scratch_shapes=[
            pltpu.VMEM((8, 272, 128), F32),
            pltpu.VMEM((512, 640), F32),
            pltpu.VMEM((4, 128, 128), F32),
            pltpu.VMEM((512, 128), F32),
        ],
        compiler_params=params(),
        name="solve",
    )(pos, *panels)


def index(y, z, c):
    return ((y % NY) * NZ + z % NZ) * NC + c % NC


def from_dp(value, dy, dz, dc):
    pairs = [
        (index(y + dy, z + dz, c + dc), index(y, z, c))
        for y in range(NY)
        for z in range(NZ)
        for c in range(NC)
    ]
    return lax.ppermute(value, "dp", pairs)


def from_mp(value, dx):
    return lax.ppermute(value, "mp", [((x + dx) % 4, x) for x in range(4)])


def shards(tg, ta, qg, qa, of, inf, tlen, qlen):
    d = lax.axis_index("dp")
    m = lax.axis_index("mp")
    pos = jnp.stack([m, d // (NZ * NC), (d // NC) % NZ, d % NC]).astype(jnp.int32)
    partial = project(tg, ta, qg, qa, of, inf)
    train, both = sketch(pos, tlen, qlen, [partial] + [from_mp(partial, s) for s in (1, 2, 3)])
    copies = jnp.broadcast_to(train[None], (NZ, 32, 128))
    groups = [[index(y, z, c) for z in range(NZ)] for y in range(NY) for c in range(NC)]
    zline = lax.all_to_all(copies, "dp", 0, 0, axis_index_groups=groups, tiled=True)
    z = pos[2]
    line = [zline[s] for s in range(NZ)]
    plane = [both] + [from_dp(both, t // 2, 0, t % 2) for t in range(1, 8)]
    part = tile(jnp.stack([pos[0], pos[1], 0 * z, pos[3]]), line, plane)
    summed = add(pos, [part] + [from_mp(part, s) for s in (1, 2, 3)])
    own = panel(pos, [summed] + [from_dp(summed, 0, s, 0) for s in range(1, NZ)])
    ys = [own] + [from_dp(own, s, 0, 0) for s in (1, 2, 3)]
    panels = []
    for s in range(4):
        panels += [ys[s], from_dp(ys[s], 0, 0, 1)]
    result = solve(pos, panels)[:, :32]
    return result.reshape(4, 2, 16).transpose(0, 2, 1).reshape(4, 32)


def solution(mesh):
    return jax.shard_map(
        shards,
        mesh=mesh,
        in_specs=(
            P("dp", None, "mp"),
            P("dp", None, "mp"),
            P("dp", None, "mp"),
            P("dp", None, "mp"),
            P(None, "mp"),
            P(None, "mp"),
            P("dp"),
            P("dp"),
        ),
        out_specs=P("dp", "mp"),
        check_vma=False,
    )
```

time: 534 us -> 213 us (0.40)
  waiting for transfers between devices: 290 us -> 7.44 us
  starting transfers between devices: 0.09 us -> 162 us
  other arithmetic: 129 us -> 0.16 us
  matrix products: 44.1 us -> 0 us
  Pallas kernels: 0 us -> 32.4 us
  local copies, waits for them, and re-layouts: 31.5 us -> 7.98 us
  between operations: 18.5 us -> 1.25 us
  blocking collectives: 14.5 us -> 0 us
    all_gather x2 -> x0, waiting for transfers between devices: 251 us -> none  [the longest x1 147 us: shards(): lax.all_gather(train_sketch, 'dp', axis=0, tiled=True)]
    ppermute x0 -> x35, starting transfers between devices: none -> 147 us  [the longest x29 126 us: from_dp(): return lax.ppermute(value, 'dp', pairs)]
    another operation x18 -> x2, other arithmetic: 125 us -> 0.16 us  [the longest x1 0.08 us: shards(): part = tile(jnp.stack([pos[0], pos[1], 0 * z, pos[3]]), line, plane)]
    psum x1 -> x0, waiting for transfers between devices: 39.7 us -> none  [shards(): train_both, query_both = lax.psum((train_both, query_both), 'mp')]
    dot_general x8 -> x0, matrix products: 33.9 us -> none  [the longest x1 16.9 us: full_products(): jnp.dot(all_train, all_train.T, precision=lax.Precision.HIGHEST, preferre...]
    pallas_call x0 -> x6, Pallas kernels: none -> 32.4 us  [the longest x1 27.9 us: solve(): pl.pallas_call(solve_kernel, out_shape=jax.ShapeDtypeStruct((4, 128), F32...]
    another operation x17 -> x0, local copies, waits for them, and re-layouts: 15 us -> none
    all_to_all x0 -> x1, starting transfers between devices: none -> 14.9 us  [shards(): lax.all_to_all(copies, 'dp', 0, 0, axis_index_groups=groups, tiled=True)]
  transfers between devices with their start and end apart: 3 -> 36, of which waited for: 3 -> 6; matrix products, arithmetic and copies ran while one was open for 2% -> 0% of each run, Pallas kernels for 0% -> 0%
where the time goes in v1:
time: 213 us; the launch traced here: 211 us
  starting transfers between devices  162 us (76%)
  Pallas kernels  32.4 us (15%)
  local copies, waits for them, and re-layouts  7.98 us (4%)
  waiting for transfers between devices  7.44 us (3%)
    ppermute x29, starting transfers between devices, from_dp(): return lax.ppermute(value, 'dp', pairs)  126 us
    pallas_call x1, Pallas kernels, solve(): pl.pallas_call(solve_kernel, out_shape=jax.ShapeDtypeStruct((4, 128), F32...  27.9 us
    ppermute x6, starting transfers between devices, from_mp(): return lax.ppermute(value, 'mp', [((x + dx) % 4, x) for x in range(4)])  21.6 us
    all_to_all x1, starting transfers between devices, shards(): lax.all_to_all(copies, 'dp', 0, 0, axis_index_groups=groups, tiled=True)  14.9 us
    unnamed x14, local copies, waits for them, and re-layouts  6.39 us
  transfers between devices with their start and end apart: 36, of which 6 were waited for; matrix products, arithmetic and copies ran while one was open for 0% of the time, Pallas kernels for 0%

profile of v1, /device:TPU:1, one launch (start us, length us, event | category | flops | bytes accessed | tf_op | source)
XLA Modules:
  0.0 211.5 jit_solution(4604232372849992827)
XLA Ops:
  0.0 1.5 copy-done
  1.5 1.0 copy-done.1
  2.5 1.0 copy-done.2
  3.6 1.0 copy-done.3
  6.4 1.0 project.1.p0
  7.4 3.9 %collective-permute-start.2 = (f32[320,128]{1,0:T(8,128)S(1)}, f32[320,128]{1,0:T(8,128)S(1)}, u32[]{:S(2)}, u32[]{:S(2)}) collective-permute-start(f32[320,128]{1,0:T(8,128)S(1)} %project.1.p0), channel_id=1, source_target_pairs={{3,0},{0,1},{1,2},{2,3},{7,4},{4,5},{5,6},{6,7},{11,8},{8,9},{9,10... | collective-permute-start | bytes 491528 | tf_op jit(solution)/shard_map/ppermute | solution.py:319
  11.3 4.4 %collective-permute-start.1 = (f32[320,128]{1,0:T(8,128)S(1)}, f32[320,128]{1,0:T(8,128)S(1)}, u32[]{:S(2)}, u32[]{:S(2)}) collective-permute-start(f32[320,128]{1,0:T(8,128)S(1)} %project.1.p0), channel_id=1, source_target_pairs={{2,0},{3,1},{0,2},{1,3},{6,4},{7,5},{4,6},{5,7},{10,8},{11,9},{8,1... | collective-permute-start | bytes 491528 | tf_op jit(solution)/shard_map/ppermute | solution.py:319
  15.7 3.1 %collective-permute-start = (f32[320,128]{1,0:T(8,128)S(1)}, f32[320,128]{1,0:T(8,128)S(1)}, u32[]{:S(2)}, u32[]{:S(2)}) collective-permute-start(f32[320,128]{1,0:T(8,128)S(1)} %project.1.p0), channel_id=1, source_target_pairs={{1,0},{2,1},{3,2},{0,3},{5,4},{6,5},{7,6},{4,7},{9,8},{10,9},{11,1... | collective-permute-start | bytes 491528 | tf_op jit(solution)/shard_map/ppermute | solution.py:319
  20.0 2.1 collective-permute-done.p1
  22.0 1.1 sketch.1
  23.9 14.9 %all-to-all-start = ((f32[16,32,128]{2,1,0:T(8,128)}), f32[16,32,128]{2,1,0:T(8,128)S(1)}, u32[]{:S(2)}, u32[]{:S(2)}) async-start(f32[16,32,128]{2,1,0:T(8,128)} %broadcast_in_dim.2), calls=%async_computation | async-start | bytes 524288 | tf_op jit(solution)/shard_map/all_to_all | solution.py:330
  38.8 5.6 %collective-permute-start.9 = (f32[40,128]{1,0:T(8,128)S(1)}, f32[40,128]{1,0:T(8,128)S(1)}, u32[]{:S(2)}, u32[]{:S(2)}) collective-permute-start(f32[40,128]{1,0:T(8,128)S(1)} %get-tuple-element.8.refs_16_), channel_id=1, source_target_pairs={{388,0},{384,4},{396,8},{392,12},{404,16},{400,20},{412,24},{408,2... | collective-permute-start | bytes 61448 | tf_op jit(solution)/shard_map/ppermute | solution.py:315
  44.3 3.2 %collective-permute-start.8 = (f32[40,128]{1,0:T(8,128)S(1)}, f32[40,128]{1,0:T(8,128)S(1)}, u32[]{:S(2)}, u32[]{:S(2)}) collective-permute-start(f32[40,128]{1,0:T(8,128)S(1)} %get-tuple-element.8.refs_16_), channel_id=1, source_target_pairs={{384,0},{388,4},{392,8},{396,12},{400,16},{404,20},{408,24},{412,2... | collective-permute-start | bytes 61448 | tf_op jit(solution)/shard_map/ppermute | solution.py:315
  47.6 3.5 %collective-permute-start.7 = (f32[40,128]{1,0:T(8,128)S(1)}, f32[40,128]{1,0:T(8,128)S(1)}, u32[]{:S(2)}, u32[]{:S(2)}) collective-permute-start(f32[40,128]{1,0:T(8,128)S(1)} %get-tuple-element.8.refs_16_), channel_id=1, source_target_pairs={{260,0},{256,4},{268,8},{264,12},{276,16},{272,20},{284,24},{280,2... | collective-permute-start | bytes 61448 | tf_op jit(solution)/shard_map/ppermute | solution.py:315
  51.1 2.3 %collective-permute-start.6 = (f32[40,128]{1,0:T(8,128)S(1)}, f32[40,128]{1,0:T(8,128)S(1)}, u32[]{:S(2)}, u32[]{:S(2)}) collective-permute-start(f32[40,128]{1,0:T(8,128)S(1)} %get-tuple-element.8.refs_16_), channel_id=1, source_target_pairs={{256,0},{260,4},{264,8},{268,12},{272,16},{276,20},{280,24},{284,2... | collective-permute-start | bytes 61448 | tf_op jit(solution)/shard_map/ppermute | solution.py:315
  53.4 4.9 %collective-permute-start.5 = (f32[40,128]{1,0:T(8,128)S(1)}, f32[40,128]{1,0:T(8,128)S(1)}, u32[]{:S(2)}, u32[]{:S(2)}) collective-permute-start(f32[40,128]{1,0:T(8,128)S(1)} %get-tuple-element.8.refs_16_), channel_id=1, source_target_pairs={{132,0},{128,4},{140,8},{136,12},{148,16},{144,20},{156,24},{152,2... | collective-permute-start | bytes 61448 | tf_op jit(solution)/shard_map/ppermute | solution.py:315
  58.3 2.1 %collective-permute-start.4 = (f32[40,128]{1,0:T(8,128)S(1)}, f32[40,128]{1,0:T(8,128)S(1)}, u32[]{:S(2)}, u32[]{:S(2)}) collective-permute-start(f32[40,128]{1,0:T(8,128)S(1)} %get-tuple-element.8.refs_16_), channel_id=1, source_target_pairs={{128,0},{132,4},{136,8},{140,12},{144,16},{148,20},{152,24},{156,2... | collective-permute-start | bytes 61448 | tf_op jit(solution)/shard_map/ppermute | solution.py:315
  60.4 2.4 %collective-permute-start.3 = (f32[40,128]{1,0:T(8,128)S(1)}, f32[40,128]{1,0:T(8,128)S(1)}, u32[]{:S(2)}, u32[]{:S(2)}) collective-permute-start(f32[40,128]{1,0:T(8,128)S(1)} %get-tuple-element.8.refs_16_), channel_id=1, source_target_pairs={{4,0},{0,4},{12,8},{8,12},{20,16},{16,20},{28,24},{24,28},{36,32},... | collective-permute-start | bytes 61448 | tf_op jit(solution)/shard_map/ppermute | solution.py:315
  63.6 1.2 tile.1.p0
  64.8 3.8 %collective-permute-start.12 = (f32[24,128]{1,0:T(8,128)S(1)}, f32[24,128]{1,0:T(8,128)S(1)}, u32[]{:S(2)}, u32[]{:S(2)}) collective-permute-start(f32[24,128]{1,0:T(8,128)S(1)} %tile.1.p0), channel_id=1, source_target_pairs={{3,0},{0,1},{1,2},{2,3},{7,4},{4,5},{5,6},{6,7},{11,8},{8,9},{9,10... | collective-permute-start | bytes 36872 | tf_op jit(solution)/shard_map/ppermute | solution.py:319
  68.6 3.6 %collective-permute-start.11 = (f32[24,128]{1,0:T(8,128)S(1)}, f32[24,128]{1,0:T(8,128)S(1)}, u32[]{:S(2)}, u32[]{:S(2)}) collective-permute-start(f32[24,128]{1,0:T(8,128)S(1)} %tile.1.p0), channel_id=1, source_target_pairs={{2,0},{3,1},{0,2},{1,3},{6,4},{7,5},{4,6},{5,7},{10,8},{11,9},{8,1... | collective-permute-start | bytes 36872 | tf_op jit(solution)/shard_map/ppermute | solution.py:319
  72.2 2.9 %collective-permute-start.10 = (f32[24,128]{1,0:T(8,128)S(1)}, f32[24,128]{1,0:T(8,128)S(1)}, u32[]{:S(2)}, u32[]{:S(2)}) collective-permute-start(f32[24,128]{1,0:T(8,128)S(1)} %tile.1.p0), channel_id=1, source_target_pairs={{1,0},{2,1},{3,2},{0,3},{5,4},{6,5},{7,6},{4,7},{9,8},{10,9},{11,1... | collective-permute-start | bytes 36872 | tf_op jit(solution)/shard_map/ppermute | solution.py:319
  75.2 1.5 collective-permute-done.10.p1
  77.2 3.5 %collective-permute-start.27 = (f32[24,128]{1,0:T(8,128)S(1)}, f32[24,128]{1,0:T(8,128)S(1)}, u32[]{:S(2)}, u32[]{:S(2)}) collective-permute-start(f32[24,128]{1,0:T(8,128)S(1)} %add.27.refs_0_), channel_id=1, source_target_pairs={{120,0},{124,4},{0,8},{4,12},{8,16},{12,20},{16,24},{20,28},{24,32... | collective-permute-start | bytes 36872 | tf_op jit(solution)/shard_map/ppermute | solution.py:315
  80.8 4.0 %collective-permute-start.26 = (f32[24,128]{1,0:T(8,128)S(1)}, f32[24,128]{1,0:T(8,128)S(1)}, u32[]{:S(2)}, u32[]{:S(2)}) collective-permute-start(f32[24,128]{1,0:T(8,128)S(1)} %add.27.refs_0_), channel_id=1, source_target_pairs={{112,0},{116,4},{120,8},{124,12},{0,16},{4,20},{8,24},{12,28},{16,... | collective-permute-start | bytes 36872 | tf_op jit(solution)/shard_map/ppermute | solution.py:315
  84.8 6.1 %collective-permute-start.25 = (f32[24,128]{1,0:T(8,128)S(1)}, f32[24,128]{1,0:T(8,128)S(1)}, u32[]{:S(2)}, u32[]{:S(2)}) collective-permute-start(f32[24,128]{1,0:T(8,128)S(1)} %add.27.refs_0_), channel_id=1, source_target_pairs={{104,0},{108,4},{112,8},{116,12},{120,16},{124,20},{0,24},{4,28},{... | collective-permute-start | bytes 36872 | tf_op jit(solution)/shard_map/ppermute | solution.py:315
  90.9 5.2 %collective-permute-start.24 = (f32[24,128]{1,0:T(8,128)S(1)}, f32[24,128]{1,0:T(8,128)S(1)}, u32[]{:S(2)}, u32[]{:S(2)}) collective-permute-start(f32[24,128]{1,0:T(8,128)S(1)} %add.27.refs_0_), channel_id=1, source_target_pairs={{96,0},{100,4},{104,8},{108,12},{112,16},{116,20},{120,24},{124,28... | collective-permute-start | bytes 36872 | tf_op jit(solution)/shard_map/ppermute | solution.py:315
  96.1 2.2 %collective-permute-start.23 = (f32[24,128]{1,0:T(8,128)S(1)}, f32[24,128]{1,0:T(8,128)S(1)}, u32[]{:S(2)}, u32[]{:S(2)}) collective-permute-start(f32[24,128]{1,0:T(8,128)S(1)} %add.27.refs_0_), channel_id=1, source_target_pairs={{88,0},{92,4},{96,8},{100,12},{104,16},{108,20},{112,24},{116,28},... | collective-permute-start | bytes 36872 | tf_op jit(solution)/shard_map/ppermute | solution.py:315
  98.3 7.9 %collective-permute-start.22 = (f32[24,128]{1,0:T(8,128)S(1)}, f32[24,128]{1,0:T(8,128)S(1)}, u32[]{:S(2)}, u32[]{:S(2)}) collective-permute-start(f32[24,128]{1,0:T(8,128)S(1)} %add.27.refs_0_), channel_id=1, source_target_pairs={{80,0},{84,4},{88,8},{92,12},{96,16},{100,20},{104,24},{108,28},{1... | collective-permute-start | bytes 36872 | tf_op jit(solution)/shard_map/ppermute | solution.py:315
  106.2 6.1 %collective-permute-start.21 = (f32[24,128]{1,0:T(8,128)S(1)}, f32[24,128]{1,0:T(8,128)S(1)}, u32[]{:S(2)}, u32[]{:S(2)}) collective-permute-start(f32[24,128]{1,0:T(8,128)S(1)} %add.27.refs_0_), channel_id=1, source_target_pairs={{72,0},{76,4},{80,8},{84,12},{88,16},{92,20},{96,24},{100,28},{104... | collective-permute-start | bytes 36872 | tf_op jit(solution)/shard_map/ppermute | solution.py:315
  112.3 7.0 %collective-permute-start.20 = (f32[24,128]{1,0:T(8,128)S(1)}, f32[24,128]{1,0:T(8,128)S(1)}, u32[]{:S(2)}, u32[]{:S(2)}) collective-permute-start(f32[24,128]{1,0:T(8,128)S(1)} %add.27.refs_0_), channel_id=1, source_target_pairs={{64,0},{68,4},{72,8},{76,12},{80,16},{84,20},{88,24},{92,28},{96,3... | collective-permute-start | bytes 36872 | tf_op jit(solution)/shard_map/ppermute | solution.py:315
  119.4 6.1 %collective-permute-start.19 = (f32[24,128]{1,0:T(8,128)S(1)}, f32[24,128]{1,0:T(8,128)S(1)}, u32[]{:S(2)}, u32[]{:S(2)}) collective-permute-start(f32[24,128]{1,0:T(8,128)S(1)} %add.27.refs_0_), channel_id=1, source_target_pairs={{56,0},{60,4},{64,8},{68,12},{72,16},{76,20},{80,24},{84,28},{88,3... | collective-permute-start | bytes 36872 | tf_op jit(solution)/shard_map/ppermute | solution.py:315
  125.5 7.9 %collective-permute-start.18 = (f32[24,128]{1,0:T(8,128)S(1)}, f32[24,128]{1,0:T(8,128)S(1)}, u32[]{:S(2)}, u32[]{:S(2)}) collective-permute-start(f32[24,128]{1,0:T(8,128)S(1)} %add.27.refs_0_), channel_id=1, source_target_pairs={{48,0},{52,4},{56,8},{60,12},{64,16},{68,20},{72,24},{76,28},{80,3... | collective-permute-start | bytes 36872 | tf_op jit(solution)/shard_map/ppermute | solution.py:315
  133.4 2.2 %collective-permute-start.17 = (f32[24,128]{1,0:T(8,128)S(1)}, f32[24,128]{1,0:T(8,128)S(1)}, u32[]{:S(2)}, u32[]{:S(2)}) collective-permute-start(f32[24,128]{1,0:T(8,128)S(1)} %add.27.refs_0_), channel_id=1, source_target_pairs={{40,0},{44,4},{48,8},{52,12},{56,16},{60,20},{64,24},{68,28},{72,3... | collective-permute-start | bytes 36872 | tf_op jit(solution)/shard_map/ppermute | solution.py:315
  135.6 5.2 %collective-permute-start.16 = (f32[24,128]{1,0:T(8,128)S(1)}, f32[24,128]{1,0:T(8,128)S(1)}, u32[]{:S(2)}, u32[]{:S(2)}) collective-permute-start(f32[24,128]{1,0:T(8,128)S(1)} %add.27.refs_0_), channel_id=1, source_target_pairs={{32,0},{36,4},{40,8},{44,12},{48,16},{52,20},{56,24},{60,28},{64,3... | collective-permute-start | bytes 36872 | tf_op jit(solution)/shard_map/ppermute | solution.py:315
  140.8 6.1 %collective-permute-start.15 = (f32[24,128]{1,0:T(8,128)S(1)}, f32[24,128]{1,0:T(8,128)S(1)}, u32[]{:S(2)}, u32[]{:S(2)}) collective-permute-start(f32[24,128]{1,0:T(8,128)S(1)} %add.27.refs_0_), channel_id=1, source_target_pairs={{24,0},{28,4},{32,8},{36,12},{40,16},{44,20},{48,24},{52,28},{56,3... | collective-permute-start | bytes 36872 | tf_op jit(solution)/shard_map/ppermute | solution.py:315
  146.9 4.0 %collective-permute-start.14 = (f32[24,128]{1,0:T(8,128)S(1)}, f32[24,128]{1,0:T(8,128)S(1)}, u32[]{:S(2)}, u32[]{:S(2)}) collective-permute-start(f32[24,128]{1,0:T(8,128)S(1)} %add.27.refs_0_), channel_id=1, source_target_pairs={{16,0},{20,4},{24,8},{28,12},{32,16},{36,20},{40,24},{44,28},{48,3... | collective-permute-start | bytes 36872 | tf_op jit(solution)/shard_map/ppermute | solution.py:315
  150.9 3.1 %collective-permute-start.13 = (f32[24,128]{1,0:T(8,128)S(1)}, f32[24,128]{1,0:T(8,128)S(1)}, u32[]{:S(2)}, u32[]{:S(2)}) collective-permute-start(f32[24,128]{1,0:T(8,128)S(1)} %add.27.refs_0_), channel_id=1, source_target_pairs={{8,0},{12,4},{16,8},{20,12},{24,16},{28,20},{32,24},{36,28},{40,32... | collective-permute-start | bytes 36872 | tf_op jit(solution)/shard_map/ppermute | solution.py:315
  154.1 1.3 collective-permute-done.13.refs_1_
  156.0 3.0 %collective-permute-start.33 = (f32[272,128]{1,0:T(8,128)S(1)}, f32[272,128]{1,0:T(8,128)S(1)}, u32[]{:S(2)}, u32[]{:S(2)}) collective-permute-start(f32[272,128]{1,0:T(8,128)S(1)} %panel.1.refs_0_), channel_id=1, source_target_pairs={{384,0},{388,4},{392,8},{396,12},{400,16},{404,20},{408,24},{412,2... | collective-permute-start | bytes 417800 | tf_op jit(solution)/shard_map/ppermute | solution.py:315
  159.1 3.3 %collective-permute-start.31 = (f32[272,128]{1,0:T(8,128)S(1)}, f32[272,128]{1,0:T(8,128)S(1)}, u32[]{:S(2)}, u32[]{:S(2)}) collective-permute-start(f32[272,128]{1,0:T(8,128)S(1)} %panel.1.refs_0_), channel_id=1, source_target_pairs={{256,0},{260,4},{264,8},{268,12},{272,16},{276,20},{280,24},{284,2... | collective-permute-start | bytes 417800 | tf_op jit(solution)/shard_map/ppermute | solution.py:315
  162.4 3.0 %collective-permute-start.29 = (f32[272,128]{1,0:T(8,128)S(1)}, f32[272,128]{1,0:T(8,128)S(1)}, u32[]{:S(2)}, u32[]{:S(2)}) collective-permute-start(f32[272,128]{1,0:T(8,128)S(1)} %panel.1.refs_0_), channel_id=1, source_target_pairs={{128,0},{132,4},{136,8},{140,12},{144,16},{148,20},{152,24},{156,2... | collective-permute-start | bytes 417800 | tf_op jit(solution)/shard_map/ppermute | solution.py:315
  165.4 9.7 %collective-permute-start.28 = (f32[272,128]{1,0:T(8,128)S(1)}, f32[272,128]{1,0:T(8,128)S(1)}, u32[]{:S(2)}, u32[]{:S(2)}) collective-permute-start(f32[272,128]{1,0:T(8,128)S(1)} %panel.1.refs_0_), channel_id=1, source_target_pairs={{4,0},{0,4},{12,8},{8,12},{20,16},{16,20},{28,24},{24,28},{36,32},... | collective-permute-start | bytes 417800 | tf_op jit(solution)/shard_map/ppermute | solution.py:315
  175.1 1.9 collective-permute-start.34
  177.0 2.4 %collective-permute-start.32 = (f32[272,128]{1,0:T(8,128)S(1)}, f32[272,128]{1,0:T(8,128)S(1)}, u32[]{:S(2)}, u32[]{:S(2)}) collective-permute-start(f32[272,128]{1,0:T(8,128)S(1)} %collective-permute-done.31.refs_4_), channel_id=1, source_target_pairs={{4,0},{0,4},{12,8},{8,12},{20,16},{16,20},{28,24},{24,28},{36,32},... | collective-permute-start | bytes 417800 | tf_op jit(solution)/shard_map/ppermute | solution.py:315
  179.4 1.9 collective-permute-start.30
  181.4 1.3 collective-permute-done.30.refs_3_
  182.7 27.9 %solve.1 = f32[4,128]{1,0:T(4,128)S(1)} custom-call(s32[4]{0:T(128)S(1)} %add_add_fusion.pos, f32[272,128]{1,0:T(8,128)S(1)} %panel.1.refs_0_, f32[272,128]{1,0:T(8,128)S(1)} %collective-permute-done.28.refs_1_, f32[272,128]{1,0:T(8,128)S(1)} %collective-permute-done.29.refs_2_, f32[272,128]{1,0:T(8,128)S(1)} %collective-permute-done.30.refs_3_, ...), custom_call_target="tpu_custom_call" | custom-call | tf_op jit(solution)/shard_map/solve/pallas_call | solution.py:288
  (51 shorter events, 6.0 us)
Async XLA Ops:
  0.0 1.5 copy-start
  1.5 1.0 copy-start.1
  2.5 1.0 copy-start.2
  3.6 1.0 copy-start.3
  4.6 0.9 copy-start.4
  5.5 0.9 copy-start.5
  6.4 15.6 %copy-start.6 = (s32[4]{0:T(128)S(1)}, s32[4]{0:T(128)}, u32[]{:S(2)}) copy-start(s32[4]{0:T(128)} %tlen.1) | copy-start | bytes 52
  7.4 12.2 %collective-permute-start.2 = (f32[320,128]{1,0:T(8,128)S(1)}, f32[320,128]{1,0:T(8,128)S(1)}, u32[]{:S(2)}, u32[]{:S(2)}) collective-permute-start(f32[320,128]{1,0:T(8,128)S(1)} %project.1.p0), channel_id=1, source_target_pairs={{3,0},{0,1},{1,2},{2,3},{7,4},{4,5},{5,6},{6,7},{11,8},{8,9},{9,10... | collective-permute-start | bytes 491528 | tf_op jit(solution)/shard_map/ppermute | solution.py:319
  11.3 8.6 %collective-permute-start.1 = (f32[320,128]{1,0:T(8,128)S(1)}, f32[320,128]{1,0:T(8,128)S(1)}, u32[]{:S(2)}, u32[]{:S(2)}) collective-permute-start(f32[320,128]{1,0:T(8,128)S(1)} %project.1.p0), channel_id=1, source_target_pairs={{2,0},{3,1},{0,2},{1,3},{6,4},{7,5},{4,6},{5,7},{10,8},{11,9},{8,1... | collective-permute-start | bytes 491528 | tf_op jit(solution)/shard_map/ppermute | solution.py:319
  15.7 6.4 %collective-permute-start = (f32[320,128]{1,0:T(8,128)S(1)}, f32[320,128]{1,0:T(8,128)S(1)}, u32[]{:S(2)}, u32[]{:S(2)}) collective-permute-start(f32[320,128]{1,0:T(8,128)S(1)} %project.1.p0), channel_id=1, source_target_pairs={{1,0},{2,1},{3,2},{0,3},{5,4},{6,5},{7,6},{4,7},{9,8},{10,9},{11,1... | collective-permute-start | bytes 491528 | tf_op jit(solution)/shard_map/ppermute | solution.py:319
  23.9 38.9 %all-to-all-start = ((f32[16,32,128]{2,1,0:T(8,128)}), f32[16,32,128]{2,1,0:T(8,128)S(1)}, u32[]{:S(2)}, u32[]{:S(2)}) async-start(f32[16,32,128]{2,1,0:T(8,128)} %broadcast_in_dim.2), calls=%async_computation | async-start | bytes 524288 | tf_op jit(solution)/shard_map/all_to_all | solution.py:330
  38.8 19.5 %collective-permute-start.9 = (f32[40,128]{1,0:T(8,128)S(1)}, f32[40,128]{1,0:T(8,128)S(1)}, u32[]{:S(2)}, u32[]{:S(2)}) collective-permute-start(f32[40,128]{1,0:T(8,128)S(1)} %get-tuple-element.8.refs_16_), channel_id=1, source_target_pairs={{388,0},{384,4},{396,8},{392,12},{404,16},{400,20},{412,24},{408,2... | collective-permute-start | bytes 61448 | tf_op jit(solution)/shard_map/ppermute | solution.py:315
  44.3 16.1 %collective-permute-start.8 = (f32[40,128]{1,0:T(8,128)S(1)}, f32[40,128]{1,0:T(8,128)S(1)}, u32[]{:S(2)}, u32[]{:S(2)}) collective-permute-start(f32[40,128]{1,0:T(8,128)S(1)} %get-tuple-element.8.refs_16_), channel_id=1, source_target_pairs={{384,0},{388,4},{392,8},{396,12},{400,16},{404,20},{408,24},{412,2... | collective-permute-start | bytes 61448 | tf_op jit(solution)/shard_map/ppermute | solution.py:315
  47.6 15.2 %collective-permute-start.7 = (f32[40,128]{1,0:T(8,128)S(1)}, f32[40,128]{1,0:T(8,128)S(1)}, u32[]{:S(2)}, u32[]{:S(2)}) collective-permute-start(f32[40,128]{1,0:T(8,128)S(1)} %get-tuple-element.8.refs_16_), channel_id=1, source_target_pairs={{260,0},{256,4},{268,8},{264,12},{276,16},{272,20},{284,24},{280,2... | collective-permute-start | bytes 61448 | tf_op jit(solution)/shard_map/ppermute | solution.py:315
  51.1 11.7 %collective-permute-start.6 = (f32[40,128]{1,0:T(8,128)S(1)}, f32[40,128]{1,0:T(8,128)S(1)}, u32[]{:S(2)}, u32[]{:S(2)}) collective-permute-start(f32[40,128]{1,0:T(8,128)S(1)} %get-tuple-element.8.refs_16_), channel_id=1, source_target_pairs={{256,0},{260,4},{264,8},{268,12},{272,16},{276,20},{280,24},{284,2... | collective-permute-start | bytes 61448 | tf_op jit(solution)/shard_map/ppermute | solution.py:315
  53.4 9.5 %collective-permute-start.5 = (f32[40,128]{1,0:T(8,128)S(1)}, f32[40,128]{1,0:T(8,128)S(1)}, u32[]{:S(2)}, u32[]{:S(2)}) collective-permute-start(f32[40,128]{1,0:T(8,128)S(1)} %get-tuple-element.8.refs_16_), channel_id=1, source_target_pairs={{132,0},{128,4},{140,8},{136,12},{148,16},{144,20},{156,24},{152,2... | collective-permute-start | bytes 61448 | tf_op jit(solution)/shard_map/ppermute | solution.py:315
  58.3 4.6 %collective-permute-start.4 = (f32[40,128]{1,0:T(8,128)S(1)}, f32[40,128]{1,0:T(8,128)S(1)}, u32[]{:S(2)}, u32[]{:S(2)}) collective-permute-start(f32[40,128]{1,0:T(8,128)S(1)} %get-tuple-element.8.refs_16_), channel_id=1, source_target_pairs={{128,0},{132,4},{136,8},{140,12},{144,16},{148,20},{152,24},{156,2... | collective-permute-start | bytes 61448 | tf_op jit(solution)/shard_map/ppermute | solution.py:315
  60.4 3.2 %collective-permute-start.3 = (f32[40,128]{1,0:T(8,128)S(1)}, f32[40,128]{1,0:T(8,128)S(1)}, u32[]{:S(2)}, u32[]{:S(2)}) collective-permute-start(f32[40,128]{1,0:T(8,128)S(1)} %get-tuple-element.8.refs_16_), channel_id=1, source_target_pairs={{4,0},{0,4},{12,8},{8,12},{20,16},{16,20},{28,24},{24,28},{36,32},... | collective-permute-start | bytes 61448 | tf_op jit(solution)/shard_map/ppermute | solution.py:315
  64.8 10.3 %collective-permute-start.12 = (f32[24,128]{1,0:T(8,128)S(1)}, f32[24,128]{1,0:T(8,128)S(1)}, u32[]{:S(2)}, u32[]{:S(2)}) collective-permute-start(f32[24,128]{1,0:T(8,128)S(1)} %tile.1.p0), channel_id=1, source_target_pairs={{3,0},{0,1},{1,2},{2,3},{7,4},{4,5},{5,6},{6,7},{11,8},{8,9},{9,10... | collective-permute-start | bytes 36872 | tf_op jit(solution)/shard_map/ppermute | solution.py:319
  68.6 6.5 %collective-permute-start.11 = (f32[24,128]{1,0:T(8,128)S(1)}, f32[24,128]{1,0:T(8,128)S(1)}, u32[]{:S(2)}, u32[]{:S(2)}) collective-permute-start(f32[24,128]{1,0:T(8,128)S(1)} %tile.1.p0), channel_id=1, source_target_pairs={{2,0},{3,1},{0,2},{1,3},{6,4},{7,5},{4,6},{5,7},{10,8},{11,9},{8,1... | collective-permute-start | bytes 36872 | tf_op jit(solution)/shard_map/ppermute | solution.py:319
  72.2 4.4 %collective-permute-start.10 = (f32[24,128]{1,0:T(8,128)S(1)}, f32[24,128]{1,0:T(8,128)S(1)}, u32[]{:S(2)}, u32[]{:S(2)}) collective-permute-start(f32[24,128]{1,0:T(8,128)S(1)} %tile.1.p0), channel_id=1, source_target_pairs={{1,0},{2,1},{3,2},{0,3},{5,4},{6,5},{7,6},{4,7},{9,8},{10,9},{11,1... | collective-permute-start | bytes 36872 | tf_op jit(solution)/shard_map/ppermute | solution.py:319
  77.2 21.1 %collective-permute-start.27 = (f32[24,128]{1,0:T(8,128)S(1)}, f32[24,128]{1,0:T(8,128)S(1)}, u32[]{:S(2)}, u32[]{:S(2)}) collective-permute-start(f32[24,128]{1,0:T(8,128)S(1)} %add.27.refs_0_), channel_id=1, source_target_pairs={{120,0},{124,4},{0,8},{4,12},{8,16},{12,20},{16,24},{20,28},{24,32... | collective-permute-start | bytes 36872 | tf_op jit(solution)/shard_map/ppermute | solution.py:315
  80.8 25.4 %collective-permute-start.26 = (f32[24,128]{1,0:T(8,128)S(1)}, f32[24,128]{1,0:T(8,128)S(1)}, u32[]{:S(2)}, u32[]{:S(2)}) collective-permute-start(f32[24,128]{1,0:T(8,128)S(1)} %add.27.refs_0_), channel_id=1, source_target_pairs={{112,0},{116,4},{120,8},{124,12},{0,16},{4,20},{8,24},{12,28},{16,... | collective-permute-start | bytes 36872 | tf_op jit(solution)/shard_map/ppermute | solution.py:315
  84.8 27.6 %collective-permute-start.25 = (f32[24,128]{1,0:T(8,128)S(1)}, f32[24,128]{1,0:T(8,128)S(1)}, u32[]{:S(2)}, u32[]{:S(2)}) collective-permute-start(f32[24,128]{1,0:T(8,128)S(1)} %add.27.refs_0_), channel_id=1, source_target_pairs={{104,0},{108,4},{112,8},{116,12},{120,16},{124,20},{0,24},{4,28},{... | collective-permute-start | bytes 36872 | tf_op jit(solution)/shard_map/ppermute | solution.py:315
  90.9 28.5 %collective-permute-start.24 = (f32[24,128]{1,0:T(8,128)S(1)}, f32[24,128]{1,0:T(8,128)S(1)}, u32[]{:S(2)}, u32[]{:S(2)}) collective-permute-start(f32[24,128]{1,0:T(8,128)S(1)} %add.27.refs_0_), channel_id=1, source_target_pairs={{96,0},{100,4},{104,8},{108,12},{112,16},{116,20},{120,24},{124,28... | collective-permute-start | bytes 36872 | tf_op jit(solution)/shard_map/ppermute | solution.py:315
  96.1 29.4 %collective-permute-start.23 = (f32[24,128]{1,0:T(8,128)S(1)}, f32[24,128]{1,0:T(8,128)S(1)}, u32[]{:S(2)}, u32[]{:S(2)}) collective-permute-start(f32[24,128]{1,0:T(8,128)S(1)} %add.27.refs_0_), channel_id=1, source_target_pairs={{88,0},{92,4},{96,8},{100,12},{104,16},{108,20},{112,24},{116,28},... | collective-permute-start | bytes 36872 | tf_op jit(solution)/shard_map/ppermute | solution.py:315
  98.3 35.1 %collective-permute-start.22 = (f32[24,128]{1,0:T(8,128)S(1)}, f32[24,128]{1,0:T(8,128)S(1)}, u32[]{:S(2)}, u32[]{:S(2)}) collective-permute-start(f32[24,128]{1,0:T(8,128)S(1)} %add.27.refs_0_), channel_id=1, source_target_pairs={{80,0},{84,4},{88,8},{92,12},{96,16},{100,20},{104,24},{108,28},{1... | collective-permute-start | bytes 36872 | tf_op jit(solution)/shard_map/ppermute | solution.py:315
  106.2 29.4 %collective-permute-start.21 = (f32[24,128]{1,0:T(8,128)S(1)}, f32[24,128]{1,0:T(8,128)S(1)}, u32[]{:S(2)}, u32[]{:S(2)}) collective-permute-start(f32[24,128]{1,0:T(8,128)S(1)} %add.27.refs_0_), channel_id=1, source_target_pairs={{72,0},{76,4},{80,8},{84,12},{88,16},{92,20},{96,24},{100,28},{104... | collective-permute-start | bytes 36872 | tf_op jit(solution)/shard_map/ppermute | solution.py:315
  112.3 28.5 %collective-permute-start.20 = (f32[24,128]{1,0:T(8,128)S(1)}, f32[24,128]{1,0:T(8,128)S(1)}, u32[]{:S(2)}, u32[]{:S(2)}) collective-permute-start(f32[24,128]{1,0:T(8,128)S(1)} %add.27.refs_0_), channel_id=1, source_target_pairs={{64,0},{68,4},{72,8},{76,12},{80,16},{84,20},{88,24},{92,28},{96,3... | collective-permute-start | bytes 36872 | tf_op jit(solution)/shard_map/ppermute | solution.py:315
  119.4 27.6 %collective-permute-start.19 = (f32[24,128]{1,0:T(8,128)S(1)}, f32[24,128]{1,0:T(8,128)S(1)}, u32[]{:S(2)}, u32[]{:S(2)}) collective-permute-start(f32[24,128]{1,0:T(8,128)S(1)} %add.27.refs_0_), channel_id=1, source_target_pairs={{56,0},{60,4},{64,8},{68,12},{72,16},{76,20},{80,24},{84,28},{88,3... | collective-permute-start | bytes 36872 | tf_op jit(solution)/shard_map/ppermute | solution.py:315
  125.5 25.5 %collective-permute-start.18 = (f32[24,128]{1,0:T(8,128)S(1)}, f32[24,128]{1,0:T(8,128)S(1)}, u32[]{:S(2)}, u32[]{:S(2)}) collective-permute-start(f32[24,128]{1,0:T(8,128)S(1)} %add.27.refs_0_), channel_id=1, source_target_pairs={{48,0},{52,4},{56,8},{60,12},{64,16},{68,20},{72,24},{76,28},{80,3... | collective-permute-start | bytes 36872 | tf_op jit(solution)/shard_map/ppermute | solution.py:315
  133.4 20.7 %collective-permute-start.17 = (f32[24,128]{1,0:T(8,128)S(1)}, f32[24,128]{1,0:T(8,128)S(1)}, u32[]{:S(2)}, u32[]{:S(2)}) collective-permute-start(f32[24,128]{1,0:T(8,128)S(1)} %add.27.refs_0_), channel_id=1, source_target_pairs={{40,0},{44,4},{48,8},{52,12},{56,16},{60,20},{64,24},{68,28},{72,3... | collective-permute-start | bytes 36872 | tf_op jit(solution)/shard_map/ppermute | solution.py:315
  135.6 18.5 %collective-permute-start.16 = (f32[24,128]{1,0:T(8,128)S(1)}, f32[24,128]{1,0:T(8,128)S(1)}, u32[]{:S(2)}, u32[]{:S(2)}) collective-permute-start(f32[24,128]{1,0:T(8,128)S(1)} %add.27.refs_0_), channel_id=1, source_target_pairs={{32,0},{36,4},{40,8},{44,12},{48,16},{52,20},{56,24},{60,28},{64,3... | collective-permute-start | bytes 36872 | tf_op jit(solution)/shard_map/ppermute | solution.py:315
  140.8 13.2 %collective-permute-start.15 = (f32[24,128]{1,0:T(8,128)S(1)}, f32[24,128]{1,0:T(8,128)S(1)}, u32[]{:S(2)}, u32[]{:S(2)}) collective-permute-start(f32[24,128]{1,0:T(8,128)S(1)} %add.27.refs_0_), channel_id=1, source_target_pairs={{24,0},{28,4},{32,8},{36,12},{40,16},{44,20},{48,24},{52,28},{56,3... | collective-permute-start | bytes 36872 | tf_op jit(solution)/shard_map/ppermute | solution.py:315
  146.9 7.1 %collective-permute-start.14 = (f32[24,128]{1,0:T(8,128)S(1)}, f32[24,128]{1,0:T(8,128)S(1)}, u32[]{:S(2)}, u32[]{:S(2)}) collective-permute-start(f32[24,128]{1,0:T(8,128)S(1)} %add.27.refs_0_), channel_id=1, source_target_pairs={{16,0},{20,4},{24,8},{28,12},{32,16},{36,20},{40,24},{44,28},{48,3... | collective-permute-start | bytes 36872 | tf_op jit(solution)/shard_map/ppermute | solution.py:315
  150.9 4.4 %collective-permute-start.13 = (f32[24,128]{1,0:T(8,128)S(1)}, f32[24,128]{1,0:T(8,128)S(1)}, u32[]{:S(2)}, u32[]{:S(2)}) collective-permute-start(f32[24,128]{1,0:T(8,128)S(1)} %add.27.refs_0_), channel_id=1, source_target_pairs={{8,0},{12,4},{16,8},{20,12},{24,16},{28,20},{32,24},{36,28},{40,32... | collective-permute-start | bytes 36872 | tf_op jit(solution)/shard_map/ppermute | solution.py:315
  156.0 19.1 %collective-permute-start.33 = (f32[272,128]{1,0:T(8,128)S(1)}, f32[272,128]{1,0:T(8,128)S(1)}, u32[]{:S(2)}, u32[]{:S(2)}) collective-permute-start(f32[272,128]{1,0:T(8,128)S(1)} %panel.1.refs_0_), channel_id=1, source_target_pairs={{384,0},{388,4},{392,8},{396,12},{400,16},{404,20},{408,24},{412,2... | collective-permute-start | bytes 417800 | tf_op jit(solution)/shard_map/ppermute | solution.py:315
  159.1 18.0 %collective-permute-start.31 = (f32[272,128]{1,0:T(8,128)S(1)}, f32[272,128]{1,0:T(8,128)S(1)}, u32[]{:S(2)}, u32[]{:S(2)}) collective-permute-start(f32[272,128]{1,0:T(8,128)S(1)} %panel.1.refs_0_), channel_id=1, source_target_pairs={{256,0},{260,4},{264,8},{268,12},{272,16},{276,20},{280,24},{284,2... | collective-permute-start | bytes 417800 | tf_op jit(solution)/shard_map/ppermute | solution.py:315
  162.4 17.1 %collective-permute-start.29 = (f32[272,128]{1,0:T(8,128)S(1)}, f32[272,128]{1,0:T(8,128)S(1)}, u32[]{:S(2)}, u32[]{:S(2)}) collective-permute-start(f32[272,128]{1,0:T(8,128)S(1)} %panel.1.refs_0_), channel_id=1, source_target_pairs={{128,0},{132,4},{136,8},{140,12},{144,16},{148,20},{152,24},{156,2... | collective-permute-start | bytes 417800 | tf_op jit(solution)/shard_map/ppermute | solution.py:315
  165.4 16.0 %collective-permute-start.28 = (f32[272,128]{1,0:T(8,128)S(1)}, f32[272,128]{1,0:T(8,128)S(1)}, u32[]{:S(2)}, u32[]{:S(2)}) collective-permute-start(f32[272,128]{1,0:T(8,128)S(1)} %panel.1.refs_0_), channel_id=1, source_target_pairs={{4,0},{0,4},{12,8},{8,12},{20,16},{16,20},{28,24},{24,28},{36,32},... | collective-permute-start | bytes 417800 | tf_op jit(solution)/shard_map/ppermute | solution.py:315
  175.1 6.3 %collective-permute-start.34 = (f32[272,128]{1,0:T(8,128)S(1)}, f32[272,128]{1,0:T(8,128)S(1)}, u32[]{:S(2)}, u32[]{:S(2)}) collective-permute-start(f32[272,128]{1,0:T(8,128)S(1)} %collective-permute-done.33.refs_6_), channel_id=1, source_target_pairs={{4,0},{0,4},{12,8},{8,12},{20,16},{16,20},{28,24},{24,28},{36,32},... | collective-permute-start | bytes 417800 | tf_op jit(solution)/shard_map/ppermute | solution.py:315
  177.0 4.4 %collective-permute-start.32 = (f32[272,128]{1,0:T(8,128)S(1)}, f32[272,128]{1,0:T(8,128)S(1)}, u32[]{:S(2)}, u32[]{:S(2)}) collective-permute-start(f32[272,128]{1,0:T(8,128)S(1)} %collective-permute-done.31.refs_4_), channel_id=1, source_target_pairs={{4,0},{0,4},{12,8},{8,12},{20,16},{16,20},{28,24},{24,28},{36,32},... | collective-permute-start | bytes 417800 | tf_op jit(solution)/shard_map/ppermute | solution.py:315
  179.4 3.3 %collective-permute-start.30 = (f32[272,128]{1,0:T(8,128)S(1)}, f32[272,128]{1,0:T(8,128)S(1)}, u32[]{:S(2)}, u32[]{:S(2)}) collective-permute-start(f32[272,128]{1,0:T(8,128)S(1)} %collective-permute-done.29.refs_2_), channel_id=1, source_target_pairs={{4,0},{0,4},{12,8},{8,12},{20,16},{16,20},{28,24},{24,28},{36,32},... | collective-permute-start | bytes 417800 | tf_op jit(solution)/shard_map/ppermute | solution.py:315

commit v2 on v0

v2 whole, which is shorter than its diff:
```python
import jax
import jax.numpy as jnp
from jax import lax
from jax.experimental import pallas as pl
from jax.experimental.pallas import tpu as pltpu
from jax.sharding import PartitionSpec as P

damping = 2.0
F32 = jnp.float32
HIGHEST = lax.Precision.HIGHEST
MB = 1024 * 1024

NY, NZ, NC = 4, 16, 2
VM = pl.BlockSpec(memory_space=pltpu.VMEM)
SM = pl.BlockSpec(memory_space=pltpu.SMEM)
ANY = pl.BlockSpec(memory_space=pl.ANY)


def params(limit=40 * MB):
    return pltpu.CompilerParams(vmem_limit_bytes=limit)


def shape(*sizes):
    return jax.ShapeDtypeStruct(sizes, F32)


def dot(a, b, ca, cb, precision=HIGHEST):
    return lax.dot_general(
        a, b, (((ca,), (cb,)), ((), ())), precision=precision, preferred_element_type=F32
    )


def lanes(*sizes):
    return lax.broadcasted_iota(jnp.int32, sizes, 1)


CHUNKS = 4


def project_kernel(tg, ta, qg, qa, of, inf, out, g, a, fo, fi, acc, sem):
    copies = []

    def start(src, dst):
        copy = pltpu.make_async_copy(src, dst, sem.at[len(copies)])
        copy.start()
        copies.append(copy)

    start(inf.at[0:32], fi.at[32:64])
    start(inf.at[32:64], fi.at[96:128])
    start(ta, a.at[0:4])
    start(qa, a.at[4:5])
    start(of.at[0:32], fo.at[0:32])
    start(of.at[32:64], fo.at[64:96])
    width = g.shape[2] // CHUNKS
    for j in range(CHUNKS):
        s = slice(j * width, (j + 1) * width)
        start(tg.at[:, :, s], g.at[0:4, :, s])
        start(qg.at[:, :, s], g.at[4:5, :, s])
    for at in (0, 64):
        fi[at : at + 32, :] = jnp.zeros((32, fi.shape[1]), fi.dtype)
        fo[at + 32 : at + 64, :] = jnp.zeros((32, fo.shape[1]), fo.dtype)
    for copy in copies[:4]:
        copy.wait()
    acc[...] = dot(a[...].reshape(320, a.shape[2]), fi[...], 1, 1, None)
    copies[4].wait()
    copies[5].wait()
    for j in range(CHUNKS):
        copies[6 + 2 * j].wait()
        copies[7 + 2 * j].wait()
        s = slice(j * width, (j + 1) * width)
        acc[...] += dot(g[:, :, s].reshape(320, width), fo[:, s], 1, 1, None)
    for low, high, to, n in ((0, 128, 0, 128), (256, 288, 128, 32)):
        left = lanes(n, 128) < 64
        first = acc[low : low + n, :]
        second = acc[high : high + n, :]
        for p in range(4):
            one = pltpu.roll(first, (128 - 32 * p) % 128, 1) if p else first
            two = pltpu.roll(second, (64 - 32 * p) % 128, 1) if p != 2 else second
            out[p, to : to + n, :] = jnp.where(left, one, two)


def project(tg, ta, qg, qa, of, inf):
    kg, ka = tg.shape[2], ta.shape[2]
    return pl.pallas_call(
        project_kernel,
        out_shape=shape(4, 160, 128),
        in_specs=[ANY] * 6,
        out_specs=VM,
        scratch_shapes=[
            pltpu.VMEM((5, 64, kg), jnp.bfloat16),
            pltpu.VMEM((5, 64, ka), jnp.bfloat16),
            pltpu.VMEM((128, kg), jnp.bfloat16),
            pltpu.VMEM((128, ka), jnp.bfloat16),
            pltpu.VMEM((320, 128), F32),
            pltpu.SemaphoreType.DMA((6 + 2 * CHUNKS,)),
        ],
        compiler_params=params(56 * MB),
        name="project",
    )(tg, ta, qg, qa, of, inf)


def sketch_kernel(tlen, qlen, parts, zcopies, own, square):
    lane = lanes(8, 128)

    def fold(row, col):
        total = None
        for g in range(4):
            piece = square[row + 8 * g : row + 8 * g + 8, :]
            shift = (32 * g - col) % 128
            piece = pltpu.roll(piece, shift, 1) if shift else piece
            piece = jnp.where((lane >= 32 * g) & (lane < 32 * g + 32), piece, 0.0)
            total = piece if total is None else total + piece
        return total

    def emit(e, tile):
        for t in range(NZ):
            if e < 4:
                zcopies[t, 8 * e : 8 * e + 8, :] = tile
        own[8 * e : 8 * e + 8, :] = tile

    def outer(low, n, weight):
        s = slice(low, low + n)
        x = (parts[0, s, :] + parts[1, s, :]) + (parts[2, s, :] + parts[3, s, :])
        square[...] = dot(x * weight, x, 0, 0)

    token = lax.broadcasted_iota(jnp.int32, (64, 128), 0)
    left = lanes(64, 128) < 64
    for e in range(2):
        length = jnp.where(left, tlen[e], tlen[e + 2])
        weight = (token < length).astype(F32) / length.astype(F32)
        outer(64 * e, 64, weight)
        emit(e, fold(0, 32))
        emit(e + 2, fold(64, 96))
    token = token[0:32] + jnp.where(left[0:32], 0, 32)
    outer(128, 32, (token < qlen[0]).astype(F32))
    emit(4, fold(0, 32) + fold(64, 96))


def sketch(tlen, qlen, parts):
    return pl.pallas_call(
        sketch_kernel,
        out_shape=(shape(NZ, 32, 128), shape(40, 128)),
        in_specs=[SM] * 2 + [VM],
        out_specs=(VM, VM),
        scratch_shapes=[pltpu.VMEM((128, 128), F32)],
        compiler_params=params(),
        name="sketch",
    )(tlen, qlen, parts)


def tile_kernel(pos, line, p0, p1, p2, p3, out, cols, held):
    y = pos[0] // (NZ * NC)
    c = lax.rem(pos[0], NC)
    for t, pair in enumerate((p0, p1, p2, p3)):
        for h in range(2):
            b = lax.rem(y + t, NY) * NC + lax.rem(c + h, NC)
            start = pl.multiple_of(b * 40, 8)
            cols[pl.ds(start, 40), :] = pair[40 * h : 40 * h + 40, :]
    total = None
    for s in range(8):
        rows = [line[pl.ds(8 * i + s, NZ, stride=32), :] for i in range(4)]
        part = dot(cols[pl.ds(s, 40, stride=8), :], jnp.concatenate(rows, axis=0), 1, 1)
        total = part if total is None else total + part
    held[:, 0:64] = total
    held[:, 64:128] = total
    for p in range(4):
        out[p] = jnp.zeros((8, 128), F32)
        for h in range(2):
            s = slice(64 * h, 64 * h + 64)
            row = 5 * (4 * h + p)
            out[p, 0:4, s] = held[row : row + 4, s]
            row = 5 * (2 * p + h) + 4
            out[p, 4:5, s] = held[row : row + 1, s]


def tile(pos, line, pairs):
    return pl.pallas_call(
        tile_kernel,
        out_shape=shape(4, 8, 128),
        in_specs=[SM] + [VM] * 5,
        out_specs=VM,
        scratch_shapes=[pltpu.VMEM((320, 128), F32), pltpu.VMEM((40, 128), F32)],
        compiler_params=params(),
        name="tile",
    )(pos, line, *pairs)


def add_kernel(parts, out):
    total = (parts[0] + parts[1]) + (parts[2] + parts[3])
    for t in range(NZ):
        out[t] = total


def add(parts):
    return pl.pallas_call(
        add_kernel,
        out_shape=shape(NZ, 8, 128),
        in_specs=[VM],
        out_specs=VM,
        compiler_params=params(),
        name="add",
    )(parts)


def panel_kernel(parts, out):
    for z in range(NZ):
        gram = parts[z, 0:4, :]
        query = parts[z, 4:5, :]
        for t in range(NY * 4):
            out[t, pl.ds(z, 4, stride=NZ), :] = gram
            out[t, 64 + z : 65 + z, :] = query


def panel(parts):
    return pl.pallas_call(
        panel_kernel,
        out_shape=shape(NY * 4, 80, 128),
        in_specs=[VM],
        out_specs=VM,
        compiler_params=params(),
        name="panel",
    )(parts)


def inverse_factor(tiles):
    lane = lanes(8, 128)
    sub = lax.broadcasted_iota(jnp.int32, (8, 128), 0)
    count = len(tiles)
    tiles = list(tiles)
    for q in range(count):
        first = 8 * q
        block = tiles[q]
        inside = (lane >= first) & (lane < first + 8)

        def column(r, c):
            return jnp.broadcast_to(tiles[r][:, first + c : first + c + 1], (8, 128))

        a = {}
        for c in range(8):
            whole = column(q, c)
            for p in range(c, 8):
                a[p, c] = jnp.broadcast_to(whole[p : p + 1, :], (8, 128))
        low = {}
        scale = []
        lines = []
        for p in range(8):
            scale.append(lax.rsqrt(a[p, p]))
            for k in range(p + 1, 8):
                low[k, p] = a[k, p] * scale[p]
            for k in range(p + 1, 8):
                for c in range(p + 1, k + 1):
                    a[k, c] = a[k, c] - low[k, p] * low[c, p]
            unit = (lane == first + p).astype(F32)
            line = jnp.where(inside, unit, jnp.broadcast_to(block[p : p + 1, :], (8, 128)))
            for k in range(p):
                line = line - low[p, k] * lines[k]
            lines.append(line * scale[p])
        merged = lines[0]
        for p in range(1, 8):
            merged = jnp.where(sub == p, lines[p], merged)
        tiles[q] = merged
        if q + 1 < count:
            rest = jnp.where(inside, 0.0, tiles[q + 1])
            cols = []
            for p in range(8):
                col = column(q + 1, p)
                for k in range(p):
                    col = col - low[p, k] * cols[k]
                cols.append(col * scale[p])
                rest = rest - cols[p] * lines[p]
        if q + 2 < count:
            back = [None] * 8
            for p in range(7, -1, -1):
                line = lines[p]
                for k in range(7, p, -1):
                    line = line - low[k, p] * back[k]
                back[p] = line * scale[p]
            other = jnp.where(inside, 0.0, tiles[q + 2])
            for c in range(8):
                other = other - column(q + 2, c) * back[c]
            tiles[q + 2] = other
        if q + 3 < count:
            stacked = back[0]
            for p in range(1, 8):
                stacked = jnp.where(sub == p, back[p], stacked)
            far = dot(block, stacked, 0, 0)
            for r in range(q + 3, count):
                tiles[r] = jnp.where(inside, 0.0, tiles[r]) - far[8 * r : 8 * r + 8, :]
        if q + 1 < count:
            tiles[q + 1] = rest
    for q in range(count):
        tiles[q] = jnp.where(lane <= sub + 8 * q, tiles[q], 0.0)
    return tiles


def solve_kernel(pos, mine, theirs, out, full, inv, turn):
    d = pos[0]
    y = d // (NZ * NC)
    z = lax.rem(d // NC, NZ)
    c = lax.rem(d, NC)
    base = (y * NC + c) * 64 + z
    first = c == 0
    lane = lanes(128, 128)
    row = lax.broadcasted_iota(jnp.int32, (128, 128), 0)
    left = lane < 64
    eye = (lane == row).astype(F32) * damping

    def split(at, s):
        one, two = mine[at, s, :], theirs[at, s, :]
        return jnp.where(first, one, two), jnp.where(first, two, one)

    for j in range(NY):
        for k in range(j + 1):
            halves = []
            for g in (2 * (k % 2), 2 * (k % 2) + 1):
                even, odd = split(4 * j + g, slice(0, 64))
                if k < 2:
                    halves.append(jnp.where(left[:64], even, pltpu.roll(odd, 64, 1)))
                else:
                    halves.append(jnp.where(left[:64], pltpu.roll(even, 64, 1), odd))
            block = jnp.concatenate(halves, axis=0)
            if j == k:
                block = block + eye
            full[128 * k : 128 * k + 128, 128 * j : 128 * j + 128] = block
        even, odd = split(4 * j + pos[1], slice(64, 80))
        turn[pl.ds(0, 16, stride=2), :] = jnp.where(left[:16], even, pltpu.roll(odd, 64, 1))
        turn[pl.ds(1, 16, stride=2), :] = jnp.where(left[:16], pltpu.roll(even, 64, 1), odd)
        turned = turn[...].T
        unit = (row + 128 * j == base + (lane - 32) * 16).astype(F32)
        right = jnp.where(lane < 32, turned, jnp.where(lane < 36, unit, 0.0))
        full[128 * j : 128 * j + 128, 512:640] = right
    product = None
    diagonal = full[0:128, 0:128]
    for k in range(4):
        s = slice(128 * k, 128 * k + 128)
        tiles = inverse_factor([diagonal[8 * t : 8 * t + 8, :] for t in range(16)])
        for t in range(16):
            inv[k, 8 * t : 8 * t + 8, :] = tiles[t]
        after = 128 * k + 128
        if k < 3:
            n = slice(after, after + 128)
            strip = dot(inv[k], full[s, n], 1, 0)
            full[s, n] = strip
            diagonal = full[n, n] - dot(strip, strip, 0, 0)
            rest = slice(after + 128, 640)
            full[s, rest] = dot(inv[k], full[s, rest], 1, 0)
            full[n, rest] -= dot(full[s, n], full[s, rest], 0, 0)
            for i in range(k + 2, 4):
                to = slice(128 * i, 128 * i + 128)
                full[to, 128 * i : 640] -= dot(full[s, to], full[s, 128 * i : 640], 0, 0)
        else:
            full[s, after:640] = dot(inv[k], full[s, after:640], 1, 0)
        part = dot(full[s, 512:640], full[s, 512:640], 0, 0)
        product = part if product is None else product + part
    out[...] = product[32:36, 0:32]


def solve(pos, mine, theirs):
    return pl.pallas_call(
        solve_kernel,
        out_shape=shape(4, 32),
        in_specs=[SM] + [VM] * 2,
        out_specs=VM,
        scratch_shapes=[
            pltpu.VMEM((512, 640), F32),
            pltpu.VMEM((4, 128, 128), F32),
            pltpu.VMEM((128, 128), F32),
        ],
        compiler_params=params(),
        name="solve",
    )(pos, mine, theirs)


def index(y, z, c):
    return (y * NZ + z) * NC + c


def exchange(value, axes, groups):
    return lax.all_to_all(value, axes, 0, 0, axis_index_groups=groups, tiled=True)


def shards(tg, ta, qg, qa, of, inf, tlen, qlen):
    ys, zs, cs = range(NY), range(NZ), range(NC)
    everyone = [(y, z, c) for y in ys for z in zs for c in cs]
    line_groups = [[index(y, z, c) for z in zs] for y in ys for c in cs]
    face_groups = [
        [index(y, z, c) * 4 + x for y in ys for x in range(4)] for z in zs for c in cs
    ]
    cores = [(index(y, z, 1 - c), index(y, z, c)) for y, z, c in everyone]
    pos = jnp.stack([lax.axis_index("dp"), lax.axis_index("mp")]).astype(jnp.int32)
    parts = project(tg, ta, qg, qa, of, inf)
    parts = lax.all_to_all(parts, "mp", 0, 0, tiled=True)
    zcopies, own = sketch(tlen, qlen, parts)
    line = exchange(zcopies, "dp", line_groups).reshape(NZ * 32, 128)
    pair = jnp.concatenate([own, lax.ppermute(own, "dp", cores)], axis=0)
    pairs = [pair]
    for t in (1, 2, 3):
        from_y = [(index((y + t) % NY, z, c), index(y, z, c)) for y, z, c in everyone]
        pairs.append(lax.ppermute(pair, "dp", from_y))
    tiles = lax.all_to_all(tile(pos, line, pairs), "mp", 0, 0, tiled=True)
    panels = panel(exchange(add(tiles), "dp", line_groups))
    mine = exchange(panels, ("dp", "mp"), face_groups)
    theirs = lax.ppermute(mine, "dp", cores)
    return solve(pos, mine, theirs)


def solution(mesh):
    return jax.shard_map(
        shards,
        mesh=mesh,
        in_specs=(
            P("dp", None, "mp"),
            P("dp", None, "mp"),
            P("dp", None, "mp"),
            P("dp", None, "mp"),
            P(None, "mp"),
            P(None, "mp"),
            P("dp"),
            P("dp"),
        ),
        out_specs=P("dp", "mp"),
        check_vma=False,
    )
```

time: 534 us -> 126 us (0.24); the launches traced: 528 us -> 126 us
  waiting for transfers between devices: 290 us -> 9.54 us
  other arithmetic: 129 us -> 0.08 us
  matrix products: 44.1 us -> 0 us
  starting transfers between devices: 0.09 us -> 43.4 us
  local copies, waits for them, and re-layouts: 31.5 us -> 0.01 us
  Pallas kernels: 0 us -> 29.1 us
  blocking collectives: 14.5 us -> 43.1 us
  between operations: 18.5 us -> 0.75 us
    all_gather x2 -> x0, waiting for transfers between devices: 251 us -> none  [the longest x1 147 us: shards(): lax.all_gather(train_sketch, 'dp', axis=0, tiled=True)]
    another operation x18 -> x1, other arithmetic: 125 us -> 0.08 us  [shards(): jnp.stack([lax.axis_index('dp'), lax.axis_index('mp')]).astype(jnp.int32)]
    all_to_all x0 -> x3, blocking collectives: none -> 43.1 us  [the longest x2 36.6 us: exchange(): lax.all_to_all(value, axes, 0, 0, axis_index_groups=groups, tiled=True)]
    psum x1 -> x0, waiting for transfers between devices: 39.7 us -> none  [shards(): train_both, query_both = lax.psum((train_both, query_both), 'mp')]
    dot_general x8 -> x0, matrix products: 33.9 us -> none  [the longest x1 16.9 us: full_products(): jnp.dot(all_train, all_train.T, precision=lax.Precision.HIGHEST, preferre...]
    pallas_call x0 -> x6, Pallas kernels: none -> 29.1 us  [the longest x1 21.7 us: solve(): pl.pallas_call(solve_kernel, out_shape=shape(4, 32), in_specs=[SM] + [VM]...]
    ppermute x0 -> x5, starting transfers between devices: none -> 23.4 us  [the longest x3 10.7 us: shards(): pairs.append(lax.ppermute(pair, 'dp', from_y))]
    all_to_all x0 -> x2, starting transfers between devices: none -> 20 us  [the longest x1 15.2 us: exchange(): lax.all_to_all(value, axes, 0, 0, axis_index_groups=groups, tiled=True)]
  transfers between devices with their start and end apart: 3 -> 7, of which waited for: 3 -> 4; matrix products, arithmetic and copies ran while one was open for 2% -> 0% of each run, Pallas kernels for 0% -> 0%
where the time goes in v2:
time: 126 us
  starting transfers between devices  43.4 us (34%)
  blocking collectives  43.1 us (34%)
  Pallas kernels  29.1 us (23%)
  waiting for transfers between devices  9.54 us (8%)
    all_to_all x2, blocking collectives, exchange(): lax.all_to_all(value, axes, 0, 0, axis_index_groups=groups, tiled=True)  36.6 us
    pallas_call x1, Pallas kernels, solve(): pl.pallas_call(solve_kernel, out_shape=shape(4, 32), in_specs=[SM] + [VM]...  21.7 us
    all_to_all x1, starting transfers between devices, exchange(): lax.all_to_all(value, axes, 0, 0, axis_index_groups=groups, tiled=True)  15.2 us
    ppermute x3, starting transfers between devices, shards(): pairs.append(lax.ppermute(pair, 'dp', from_y))  10.7 us
    ppermute x1, starting transfers between devices, shards(): theirs = lax.ppermute(mine, 'dp', cores)  8.3 us
    all_to_all x1, blocking collectives, shards(): tiles = lax.all_to_all(tile(pos, line, pairs), 'mp', 0, 0, tiled=True)  6.56 us
    all_to_all x1, waiting for transfers between devices, shards(): parts = lax.all_to_all(parts, 'mp', 0, 0, tiled=True)  5.23 us
    all_to_all x1, starting transfers between devices, shards(): parts = lax.all_to_all(parts, 'mp', 0, 0, tiled=True)  4.85 us
  transfers between devices with their start and end apart: 7, of which 4 were waited for; matrix products, arithmetic and copies ran while one was open for 0% of the time, Pallas kernels for 0%

profile of v2, /device:TPU:1, one launch (start us, length us, event | category | flops | bytes accessed | tf_op | source)
XLA Modules:
  0.0 126.0 jit_solution(2327545626898334813)
XLA Ops:
  0.0 0.0 copy-start
  0.0 4.2 %project.1 = f32[4,160,128]{2,1,0:T(8,128)} custom-call(bf16[4,64,3584]{2,1,0:T(8,128)(2,1)} %tg.1, bf16[4,64,1024]{2,1,0:T(8,128)(2,1)} %ta.1, bf16[1,64,3584]{2,1,0:T(8,128)(2,1)} %qg.1, bf16[1,64,1024]{2,1,0:T(8,128)(2,1)} %qa.1, bf16[64,3584]{1,0:T(8,128)(2,1)} %of.1, bf16[64,1024]{1,0:T(8,128)(2,1)} %inf.1), custom_call_target="tpu_custom_call" | custom-call | tf_op jit(solution)/shard_map/project/pallas_call | solution.py:84
  4.2 4.9 %all-to-all-start = ((f32[4,160,128]{2,1,0:T(8,128)}), f32[4,160,128]{2,1,0:T(8,128)S(1)}, u32[]{:S(2)}, u32[]{:S(2)}) async-start(f32[4,160,128]{2,1,0:T(8,128)} %project.1), calls=%async_computation | async-start | bytes 655360 | tf_op jit(solution)/shard_map/all_to_all | solution.py:392
  9.7 5.2 %all-to-all-done.parts = f32[4,160,128]{2,1,0:T(8,128)S(1)} async-done(((f32[4,160,128]{2,1,0:T(8,128)}), f32[4,160,128]{2,1,0:T(8,128)S(1)}, u32[]{:S(2)}, u32[]{:S(2)}) %all-to-all-start) | async-done | bytes 327712 | tf_op jit(solution)/shard_map/all_to_all | solution.py:392
  14.9 0.0 copy-done
  15.0 1.7 %sketch.1 = (f32[16,32,128]{2,1,0:T(8,128)}, f32[40,128]{1,0:T(8,128)S(1)}) custom-call(s32[4]{0:T(128)S(1)} %copy-done, s32[1]{0:T(128)S(6)} %copy.10.qlen, f32[4,160,128]{2,1,0:T(8,128)S(1)} %all-to-all-done.parts), custom_call_target="tpu_custom_call" | custom-call | tf_op jit(solution)/shard_map/sketch/pallas_call | solution.py:140
  16.7 15.2 %all-to-all-start.1 = ((f32[16,32,128]{2,1,0:T(8,128)}), f32[16,32,128]{2,1,0:T(8,128)S(1)}, u32[]{:S(2)}, u32[]{:S(2)}) async-start(f32[16,32,128]{2,1,0:T(8,128)} %get-tuple-element.7), calls=%async_computation.1 | async-start | bytes 524288 | tf_op jit(solution)/shard_map/all_to_all | solution.py:379
  31.9 4.3 %collective-permute-start = (f32[40,128]{1,0:T(8,128)S(1)}, f32[40,128]{1,0:T(8,128)S(1)}, u32[]{:S(2)}, u32[]{:S(2)}) collective-permute-start(f32[40,128]{1,0:T(8,128)S(1)} %get-tuple-element.8), channel_id=1, source_target_pairs={{4,0},{0,4},{12,8},{8,12},{20,16},{16,20},{28,24},{24,28},{36,32},... | collective-permute-start | bytes 61448 | tf_op jit(solution)/shard_map/ppermute | solution.py:395
  36.2 0.8 collective-permute-done
  37.0 3.2 %collective-permute-start.3 = (f32[80,128]{1,0:T(8,128)S(1)}, f32[80,128]{1,0:T(8,128)S(1)}, u32[]{:S(2)}, u32[]{:S(2)}) collective-permute-start(f32[80,128]{1,0:T(8,128)S(1)} %constant_dynamic-update-slice_fusion.p0), channel_id=1, source_target_pairs={{384,0},{388,4},{392,8},{396,12},{400,16},{404,20},{408,24},{412,2... | collective-permute-start | bytes 122888 | tf_op jit(solution)/shard_map/ppermute | solution.py:399
  40.2 4.5 %collective-permute-start.2 = (f32[80,128]{1,0:T(8,128)S(1)}, f32[80,128]{1,0:T(8,128)S(1)}, u32[]{:S(2)}, u32[]{:S(2)}) collective-permute-start(f32[80,128]{1,0:T(8,128)S(1)} %constant_dynamic-update-slice_fusion.p0), channel_id=1, source_target_pairs={{256,0},{260,4},{264,8},{268,12},{272,16},{276,20},{280,24},{284,2... | collective-permute-start | bytes 122888 | tf_op jit(solution)/shard_map/ppermute | solution.py:399
  44.8 3.0 %collective-permute-start.1 = (f32[80,128]{1,0:T(8,128)S(1)}, f32[80,128]{1,0:T(8,128)S(1)}, u32[]{:S(2)}, u32[]{:S(2)}) collective-permute-start(f32[80,128]{1,0:T(8,128)S(1)} %constant_dynamic-update-slice_fusion.p0), channel_id=1, source_target_pairs={{128,0},{132,4},{136,8},{140,12},{144,16},{148,20},{152,24},{156,2... | collective-permute-start | bytes 122888 | tf_op jit(solution)/shard_map/ppermute | solution.py:399
  47.8 0.1 pad_add_fusion.pos
  47.8 0.0 collective-permute-done.3.p3
  47.9 0.0 collective-permute-done.2.p2
  47.9 2.0 %collective-permute-done.1.p1 = f32[80,128]{1,0:T(8,128)S(1)} collective-permute-done((f32[80,128]{1,0:T(8,128)S(1)}, f32[80,128]{1,0:T(8,128)S(1)}, u32[]{:S(2)}, u32[]{:S(2)}) %collective-permute-start.1) | collective-permute-done | bytes 40992 | tf_op jit(solution)/shard_map/ppermute | solution.py:399
  49.8 0.0 all-to-all-done.1
  49.8 1.2 tile.1
  51.0 6.6 %all_to_all.25.parts = f32[4,8,128]{2,1,0:T(8,128)S(1)} all-to-all(f32[4,8,128]{2,1,0:T(8,128)S(1)} %tile.1), channel_id=1, replica_groups=mesh['dp'=128,'mp'=4] {'mp'}, dimensions={0} | all-to-all | bytes 32768 | tf_op jit(solution)/shard_map/all_to_all | solution.py:400
  57.6 22.8 %all_to_all.26.parts = f32[16,8,128]{2,1,0:T(8,128)S(1)} all-to-all(f32[16,8,128]{2,1,0:T(8,128)S(1)} %add.3), channel_id=1, replica_groups={{0,8,16,24,32,40,48,56,64,72,80,88,96,104,112,120},{4,12,20,28,36,44,52..., dimensions={0} | all-to-all | bytes 131072 | tf_op jit(solution)/shard_map/all_to_all | solution.py:379
  80.4 0.3 panel.1
  80.7 13.8 %all_to_all.27.mine = f32[16,80,128]{2,1,0:T(8,128)S(1)} all-to-all(f32[16,80,128]{2,1,0:T(8,128)S(1)} %panel.1), channel_id=1, replica_groups={{0,1,2,3,128,129,130,131,256,257,258,259,384,385,386,387},{4,5,6,7,132,..., dimensions={0} | all-to-all | bytes 1310720 | tf_op jit(solution)/shard_map/all_to_all | solution.py:379
  94.5 8.3 %collective-permute-start.4 = (f32[16,80,128]{2,1,0:T(8,128)S(1)}, f32[16,80,128]{2,1,0:T(8,128)S(1)}, u32[]{:S(2)}, u32[]{:S(2)}) collective-permute-start(f32[16,80,128]{2,1,0:T(8,128)S(1)} %all_to_all.27.mine), channel_id=1, source_target_pairs={{4,0},{0,4},{12,8},{8,12},{20,16},{16,20},{28,24},{24,28},{36,32},... | collective-permute-start | bytes 1966088 | tf_op jit(solution)/shard_map/ppermute | solution.py:403
  102.8 1.5 %collective-permute-done.4.theirs = f32[16,80,128]{2,1,0:T(8,128)S(1)} collective-permute-done((f32[16,80,128]{2,1,0:T(8,128)S(1)}, f32[16,80,128]{2,1,0:T(8,128)S(1)}, u32[]{:S(2)}, u32[]{:S(2)}) %collective-permute-start.4) | collective-permute-done | bytes 655392 | tf_op jit(solution)/shard_map/ppermute | solution.py:403
  104.3 21.7 %solve.1 = f32[4,32]{1,0:T(4,128)} custom-call(s32[2]{0:T(128)S(1)} %pad_add_fusion.pos, f32[16,80,128]{2,1,0:T(8,128)S(1)} %all_to_all.27.mine, f32[16,80,128]{2,1,0:T(8,128)S(1)} %collective-permute-done.4.theirs), custom_call_target="tpu_custom_call" | custom-call | tf_op jit(solution)/shard_map/solve/pallas_call | solution.py:359
  (3 shorter events, 0.0 us)
Async XLA Ops:
  0.0 15.0 %copy-start = (s32[4]{0:T(128)S(1)}, s32[4]{0:T(128)}, u32[]{:S(2)}) copy-start(s32[4]{0:T(128)} %tlen.1) | copy-start | bytes 52
  4.2 10.7 %all-to-all-start = ((f32[4,160,128]{2,1,0:T(8,128)}), f32[4,160,128]{2,1,0:T(8,128)S(1)}, u32[]{:S(2)}, u32[]{:S(2)}) async-start(f32[4,160,128]{2,1,0:T(8,128)} %project.1), calls=%async_computation | async-start | bytes 655360 | tf_op jit(solution)/shard_map/all_to_all | solution.py:392
  16.7 33.2 %all-to-all-start.1 = ((f32[16,32,128]{2,1,0:T(8,128)}), f32[16,32,128]{2,1,0:T(8,128)S(1)}, u32[]{:S(2)}, u32[]{:S(2)}) async-start(f32[16,32,128]{2,1,0:T(8,128)} %get-tuple-element.7), calls=%async_computation.1 | async-start | bytes 524288 | tf_op jit(solution)/shard_map/all_to_all | solution.py:379
  31.9 5.2 %collective-permute-start = (f32[40,128]{1,0:T(8,128)S(1)}, f32[40,128]{1,0:T(8,128)S(1)}, u32[]{:S(2)}, u32[]{:S(2)}) collective-permute-start(f32[40,128]{1,0:T(8,128)S(1)} %get-tuple-element.8), channel_id=1, source_target_pairs={{4,0},{0,4},{12,8},{8,12},{20,16},{16,20},{28,24},{24,28},{36,32},... | collective-permute-start | bytes 61448 | tf_op jit(solution)/shard_map/ppermute | solution.py:395
  37.0 10.8 %collective-permute-start.3 = (f32[80,128]{1,0:T(8,128)S(1)}, f32[80,128]{1,0:T(8,128)S(1)}, u32[]{:S(2)}, u32[]{:S(2)}) collective-permute-start(f32[80,128]{1,0:T(8,128)S(1)} %constant_dynamic-update-slice_fusion.p0), channel_id=1, source_target_pairs={{384,0},{388,4},{392,8},{396,12},{400,16},{404,20},{408,24},{412,2... | collective-permute-start | bytes 122888 | tf_op jit(solution)/shard_map/ppermute | solution.py:399
  40.2 7.6 %collective-permute-start.2 = (f32[80,128]{1,0:T(8,128)S(1)}, f32[80,128]{1,0:T(8,128)S(1)}, u32[]{:S(2)}, u32[]{:S(2)}) collective-permute-start(f32[80,128]{1,0:T(8,128)S(1)} %constant_dynamic-update-slice_fusion.p0), channel_id=1, source_target_pairs={{256,0},{260,4},{264,8},{268,12},{272,16},{276,20},{280,24},{284,2... | collective-permute-start | bytes 122888 | tf_op jit(solution)/shard_map/ppermute | solution.py:399
  44.8 5.0 %collective-permute-start.1 = (f32[80,128]{1,0:T(8,128)S(1)}, f32[80,128]{1,0:T(8,128)S(1)}, u32[]{:S(2)}, u32[]{:S(2)}) collective-permute-start(f32[80,128]{1,0:T(8,128)S(1)} %constant_dynamic-update-slice_fusion.p0), channel_id=1, source_target_pairs={{128,0},{132,4},{136,8},{140,12},{144,16},{148,20},{152,24},{156,2... | collective-permute-start | bytes 122888 | tf_op jit(solution)/shard_map/ppermute | solution.py:399
  94.5 9.8 %collective-permute-start.4 = (f32[16,80,128]{2,1,0:T(8,128)S(1)}, f32[16,80,128]{2,1,0:T(8,128)S(1)}, u32[]{:S(2)}, u32[]{:S(2)}) collective-permute-start(f32[16,80,128]{2,1,0:T(8,128)S(1)} %all_to_all.27.mine), channel_id=1, source_target_pairs={{4,0},{0,4},{12,8},{8,12},{20,16},{16,20},{28,24},{24,28},{36,32},... | collective-permute-start | bytes 1966088 | tf_op jit(solution)/shard_map/ppermute | solution.py:403

commit v3 on v2

--- a/solution.py
+++ b/solution.py
@@ -148,14 +148,17 @@
     )(tlen, qlen, parts)
 
 
-def tile_kernel(pos, line, p0, p1, p2, p3, out, cols, held):
+def tile_kernel(pos, line, near, away, out, cols, held):
     y = pos[0] // (NZ * NC)
     c = lax.rem(pos[0], NC)
-    for t, pair in enumerate((p0, p1, p2, p3)):
+    for t, pairs in enumerate((near, near, away, away)):
+        at = y if t < 2 else NY - 1 - y
+        at = at if t % 2 == 0 else at + 1 - 2 * lax.rem(at, 2)
         for h in range(2):
-            b = lax.rem(y + t, NY) * NC + lax.rem(c + h, NC)
+            b = at * NC + lax.rem(c + h, NC)
             start = pl.multiple_of(b * 40, 8)
-            cols[pl.ds(start, 40), :] = pair[40 * h : 40 * h + 40, :]
+            row = 80 * (t % 2) + 40 * h
+            cols[pl.ds(start, 40), :] = pairs[row : row + 40, :]
     total = None
     for s in range(8):
         rows = [line[pl.ds(8 * i + s, NZ, stride=32), :] for i in range(4)]
@@ -164,25 +167,26 @@
     held[:, 0:64] = total
     held[:, 64:128] = total
     for p in range(4):
-        out[p] = jnp.zeros((8, 128), F32)
+        out[p, 16:24, :] = jnp.zeros((8, 128), F32)
         for h in range(2):
             s = slice(64 * h, 64 * h + 64)
-            row = 5 * (4 * h + p)
-            out[p, 0:4, s] = held[row : row + 4, s]
+            for g in range(4):
+                row = 5 * (4 * h + g)
+                out[p, 4 * g : 4 * g + 4, s] = held[row : row + 4, s]
             row = 5 * (2 * p + h) + 4
-            out[p, 4:5, s] = held[row : row + 1, s]
-
-
-def tile(pos, line, pairs):
+            out[p, 16:17, s] = held[row : row + 1, s]
+
+
+def tile(pos, line, near, away):
     return pl.pallas_call(
         tile_kernel,
-        out_shape=shape(4, 8, 128),
-        in_specs=[SM] + [VM] * 5,
+        out_shape=shape(4, 24, 128),
+        in_specs=[SM] + [VM] * 3,
         out_specs=VM,
         scratch_shapes=[pltpu.VMEM((320, 128), F32), pltpu.VMEM((40, 128), F32)],
         compiler_params=params(),
         name="tile",
-    )(pos, line, *pairs)
+    )(pos, line, near, away)
 
 
 def add_kernel(parts, out):
@@ -194,7 +198,7 @@
 def add(parts):
     return pl.pallas_call(
         add_kernel,
-        out_shape=shape(NZ, 8, 128),
+        out_shape=shape(NZ, 24, 128),
         in_specs=[VM],
         out_specs=VM,
         compiler_params=params(),
@@ -204,17 +208,17 @@
 
 def panel_kernel(parts, out):
     for z in range(NZ):
-        gram = parts[z, 0:4, :]
-        query = parts[z, 4:5, :]
-        for t in range(NY * 4):
-            out[t, pl.ds(z, 4, stride=NZ), :] = gram
-            out[t, 64 + z : 65 + z, :] = query
+        both = parts[z, 0:16, :]
+        query = parts[z, 16:17, :]
+        for t in range(NY):
+            out[t, pl.ds(z, 16, stride=NZ), :] = both
+            out[t, 256 + z : 257 + z, :] = query
 
 
 def panel(parts):
     return pl.pallas_call(
         panel_kernel,
-        out_shape=shape(NY * 4, 80, 128),
+        out_shape=shape(NY, 272, 128),
         in_specs=[VM],
         out_specs=VM,
         compiler_params=params(),
@@ -240,41 +244,51 @@
             whole = column(q, c)
             for p in range(c, 8):
                 a[p, c] = jnp.broadcast_to(whole[p : p + 1, :], (8, 128))
-        low = {}
-        scale = []
-        lines = []
-        for p in range(8):
-            scale.append(lax.rsqrt(a[p, p]))
-            for k in range(p + 1, 8):
-                low[k, p] = a[k, p] * scale[p]
-            for k in range(p + 1, 8):
-                for c in range(p + 1, k + 1):
-                    a[k, c] = a[k, c] - low[k, p] * low[c, p]
-            unit = (lane == first + p).astype(F32)
-            line = jnp.where(inside, unit, jnp.broadcast_to(block[p : p + 1, :], (8, 128)))
-            for k in range(p):
-                line = line - low[p, k] * lines[k]
-            lines.append(line * scale[p])
-        merged = lines[0]
+        mult = {}
+        lines, scaled, rows = [], [], []
+        for p in range(0, 8, 2):
+            d, o, e = a[p, p], a[p + 1, p], a[p + 1, p + 1]
+            root = lax.rsqrt(d * e - o * o)
+            inverse = root * root
+            for k in range(p + 2, 8):
+                mult[k, p] = (a[k, p] * e - a[k, p + 1] * o) * inverse
+                mult[k, p + 1] = (a[k, p + 1] * d - a[k, p] * o) * inverse
+            for k in range(p + 2, 8):
+                for c in range(p + 2, k + 1):
+                    a[k, c] = a[k, c] - (mult[k, p] * a[c, p] + mult[k, p + 1] * a[c, p + 1])
+            for r in (p, p + 1):
+                unit = (lane == first + r).astype(F32)
+                line = jnp.broadcast_to(block[r : r + 1, :], (8, 128))
+                line = jnp.where(inside, unit, line)
+                for k in range(p):
+                    line = line - mult[r, k] * lines[k]
+                lines.append(line)
+            low, high = lines[p], lines[p + 1]
+            turned = high * d - low * o
+            scaled.append((low * e - high * o) * inverse)
+            scaled.append(turned * inverse)
+            top = lax.rsqrt(d)
+            rows.append(low * top)
+            rows.append(turned * (top * root))
+        merged = rows[0]
         for p in range(1, 8):
-            merged = jnp.where(sub == p, lines[p], merged)
+            merged = jnp.where(sub == p, rows[p], merged)
         tiles[q] = merged
         if q + 1 < count:
             rest = jnp.where(inside, 0.0, tiles[q + 1])
             cols = []
-            for p in range(8):
-                col = column(q + 1, p)
-                for k in range(p):
-                    col = col - low[p, k] * cols[k]
-                cols.append(col * scale[p])
-                rest = rest - cols[p] * lines[p]
+            for p in range(0, 8, 2):
+                for r in (p, p + 1):
+                    col = column(q + 1, r)
+                    for k in range(p):
+                        col = col - mult[r, k] * cols[k]
+                    cols.append(col)
+                rest = rest - (cols[p] * scaled[p] + cols[p + 1] * scaled[p + 1])
         if q + 2 < count:
-            back = [None] * 8
-            for p in range(7, -1, -1):
-                line = lines[p]
-                for k in range(7, p, -1):
-                    line = line - low[k, p] * back[k]
-                back[p] = line * scale[p]
+            back = list(scaled)
+            for p in range(5, -1, -1):
+                for k in range(7, p + 1 - p % 2, -1):
+                    back[p] = back[p] - mult[k, p] * back[k]
             other = jnp.where(inside, 0.0, tiles[q + 2])
             for c in range(8):
                 other = other - column(q + 2, c) * back[c]
@@ -305,24 +319,20 @@
     left = lane < 64
     eye = (lane == row).astype(F32) * damping
 
-    def split(at, s):
-        one, two = mine[at, s, :], theirs[at, s, :]
-        return jnp.where(first, one, two), jnp.where(first, two, one)
-
     for j in range(NY):
         for k in range(j + 1):
-            halves = []
-            for g in (2 * (k % 2), 2 * (k % 2) + 1):
-                even, odd = split(4 * j + g, slice(0, 64))
-                if k < 2:
-                    halves.append(jnp.where(left[:64], even, pltpu.roll(odd, 64, 1)))
-                else:
-                    halves.append(jnp.where(left[:64], pltpu.roll(even, 64, 1), odd))
-            block = jnp.concatenate(halves, axis=0)
+            s = slice(128 * (k % 2), 128 * (k % 2) + 128)
+            even = jnp.where(first, mine[j, s, :], theirs[j, s, :])
+            odd = jnp.where(first, theirs[j, s, :], mine[j, s, :])
+            if k < 2:
+                block = jnp.where(left, even, pltpu.roll(odd, 64, 1))
+            else:
+                block = jnp.where(left, pltpu.roll(even, 64, 1), odd)
             if j == k:
                 block = block + eye
             full[128 * k : 128 * k + 128, 128 * j : 128 * j + 128] = block
-        even, odd = split(4 * j + pos[1], slice(64, 80))
+        even = jnp.where(first, mine[j, 256:272, :], theirs[j, 256:272, :])
+        odd = jnp.where(first, theirs[j, 256:272, :], mine[j, 256:272, :])
         turn[pl.ds(0, 16, stride=2), :] = jnp.where(left[:16], even, pltpu.roll(odd, 64, 1))
         turn[pl.ds(1, 16, stride=2), :] = jnp.where(left[:16], pltpu.roll(even, 64, 1), odd)
         turned = turn[...].T
@@ -375,33 +385,40 @@
     return (y * NZ + z) * NC + c
 
 
-def exchange(value, axes, groups):
-    return lax.all_to_all(value, axes, 0, 0, axis_index_groups=groups, tiled=True)
+def exchange(value, groups):
+    return lax.all_to_all(value, "dp", 0, 0, axis_index_groups=groups, tiled=True)
+
+
+def swap(value, partner):
+    pairs = [
+        (index(*partner(y, z, c)), index(y, z, c))
+        for y in range(NY)
+        for z in range(NZ)
+        for c in range(NC)
+    ]
+    return lax.ppermute(value, "dp", pairs)
+
+
+def other_core(y, z, c):
+    return y, z, 1 - c
 
 
 def shards(tg, ta, qg, qa, of, inf, tlen, qlen):
     ys, zs, cs = range(NY), range(NZ), range(NC)
-    everyone = [(y, z, c) for y in ys for z in zs for c in cs]
     line_groups = [[index(y, z, c) for z in zs] for y in ys for c in cs]
-    face_groups = [
-        [index(y, z, c) * 4 + x for y in ys for x in range(4)] for z in zs for c in cs
-    ]
-    cores = [(index(y, z, 1 - c), index(y, z, c)) for y, z, c in everyone]
-    pos = jnp.stack([lax.axis_index("dp"), lax.axis_index("mp")]).astype(jnp.int32)
+    y_groups = [[index(y, z, c) for y in ys] for z in zs for c in cs]
+    pos = lax.axis_index("dp").astype(jnp.int32).reshape(1)
     parts = project(tg, ta, qg, qa, of, inf)
     parts = lax.all_to_all(parts, "mp", 0, 0, tiled=True)
     zcopies, own = sketch(tlen, qlen, parts)
-    line = exchange(zcopies, "dp", line_groups).reshape(NZ * 32, 128)
-    pair = jnp.concatenate([own, lax.ppermute(own, "dp", cores)], axis=0)
-    pairs = [pair]
-    for t in (1, 2, 3):
-        from_y = [(index((y + t) % NY, z, c), index(y, z, c)) for y, z, c in everyone]
-        pairs.append(lax.ppermute(pair, "dp", from_y))
-    tiles = lax.all_to_all(tile(pos, line, pairs), "mp", 0, 0, tiled=True)
-    panels = panel(exchange(add(tiles), "dp", line_groups))
-    mine = exchange(panels, ("dp", "mp"), face_groups)
-    theirs = lax.ppermute(mine, "dp", cores)
-    return solve(pos, mine, theirs)
+    pair = jnp.concatenate([own, swap(own, other_core)], axis=0)
+    line = exchange(zcopies, line_groups).reshape(NZ * 32, 128)
+    near = jnp.concatenate([pair, swap(pair, lambda y, z, c: (y ^ 1, z, c))], axis=0)
+    away = swap(near, lambda y, z, c: (NY - 1 - y, z, c))
+    tiles = lax.all_to_all(tile(pos, line, near, away), "mp", 0, 0, tiled=True)
+    panels = panel(exchange(add(tiles), line_groups))
+    mine = exchange(panels, y_groups)
+    return solve(pos, mine, swap(mine, other_core))
 
 
 def solution(mesh):

time: 126 us -> 124 us (0.984)
  blocking collectives: 43.1 us -> 41.2 us
  waiting for transfers between devices: 9.54 us -> 11.3 us
  starting transfers between devices: 43.4 us -> 42 us
    all_to_all x3, blocking collectives: 43.1 us -> 41.2 us  [the longest x2 34.4 us: exchange(): lax.all_to_all(value, 'dp', 0, 0, axis_index_groups=groups, tiled=True)]
    ppermute x5 -> x4, waiting for transfers between devices: 4.31 us -> 6.11 us  [swap(): return lax.ppermute(value, 'dp', pairs)]
    ppermute x5 -> x4, starting transfers between devices: 23.4 us -> 21.9 us  [swap(): return lax.ppermute(value, 'dp', pairs)]
  transfers between devices with their start and end apart: 7 -> 6, of which waited for: 4 -> 5; matrix products, arithmetic and copies ran while one was open for 0% -> 0% of each run, Pallas kernels for 0% -> 0%
where the time goes in v3:
time: 124 us; the launch traced here: 123 us
  starting transfers between devices  42 us (34%)
  blocking collectives  41.2 us (33%)
  Pallas kernels  27.9 us (22%)
  waiting for transfers between devices  11.3 us (9%)
    all_to_all x2, blocking collectives, exchange(): lax.all_to_all(value, 'dp', 0, 0, axis_index_groups=groups, tiled=True)  34.4 us
    ppermute x4, starting transfers between devices, swap(): return lax.ppermute(value, 'dp', pairs)  21.9 us
    pallas_call x1, Pallas kernels, solve(): pl.pallas_call(solve_kernel, out_shape=shape(4, 32), in_specs=[SM] + [VM]...  21.1 us
    all_to_all x1, starting transfers between devices, exchange(): lax.all_to_all(value, 'dp', 0, 0, axis_index_groups=groups, tiled=True)  15.2 us
    all_to_all x1, blocking collectives, shards(): tiles = lax.all_to_all(tile(pos, line, near, away), 'mp', 0, 0, tiled=True)  6.75 us
    ppermute x4, waiting for transfers between devices, swap(): return lax.ppermute(value, 'dp', pairs)  6.11 us
    all_to_all x1, waiting for transfers between devices, shards(): parts = lax.all_to_all(parts, 'mp', 0, 0, tiled=True)  5.23 us
    all_to_all x1, starting transfers between devices, shards(): parts = lax.all_to_all(parts, 'mp', 0, 0, tiled=True)  4.85 us
  transfers between devices with their start and end apart: 6, of which 5 were waited for; matrix products, arithmetic and copies ran while one was open for 0% of the time, Pallas kernels for 0%

profile of v3, /device:TPU:1, one launch (start us, length us, event | category | flops | bytes accessed | tf_op | source)
XLA Modules:
  0.0 123.2 jit_solution(9381678536767233194)
XLA Ops:
  0.0 0.0 copy-start
  0.0 4.2 %project.1 = f32[4,160,128]{2,1,0:T(8,128)} custom-call(bf16[4,64,3584]{2,1,0:T(8,128)(2,1)} %tg.1, bf16[4,64,1024]{2,1,0:T(8,128)(2,1)} %ta.1, bf16[1,64,3584]{2,1,0:T(8,128)(2,1)} %qg.1, bf16[1,64,1024]{2,1,0:T(8,128)(2,1)} %qa.1, bf16[64,3584]{1,0:T(8,128)(2,1)} %of.1, bf16[64,1024]{1,0:T(8,128)(2,1)} %inf.1), custom_call_target="tpu_custom_call" | custom-call | tf_op jit(solution)/shard_map/project/pallas_call | solution.py:84
  4.2 4.9 %all-to-all-start = ((f32[4,160,128]{2,1,0:T(8,128)}), f32[4,160,128]{2,1,0:T(8,128)S(1)}, u32[]{:S(2)}, u32[]{:S(2)}) async-start(f32[4,160,128]{2,1,0:T(8,128)} %project.1), calls=%async_computation | async-start | bytes 655360 | tf_op jit(solution)/shard_map/all_to_all | solution.py:412
  9.7 5.2 %all-to-all-done.parts = f32[4,160,128]{2,1,0:T(8,128)S(1)} async-done(((f32[4,160,128]{2,1,0:T(8,128)}), f32[4,160,128]{2,1,0:T(8,128)S(1)}, u32[]{:S(2)}, u32[]{:S(2)}) %all-to-all-start) | async-done | bytes 327712 | tf_op jit(solution)/shard_map/all_to_all | solution.py:412
  14.9 0.0 copy-done
  14.9 1.7 %sketch.1 = (f32[16,32,128]{2,1,0:T(8,128)}, f32[40,128]{1,0:T(8,128)S(1)}) custom-call(s32[4]{0:T(128)S(1)} %copy-done, s32[1]{0:T(128)S(6)} %copy.11.qlen, f32[4,160,128]{2,1,0:T(8,128)S(1)} %all-to-all-done.parts), custom_call_target="tpu_custom_call" | custom-call | tf_op jit(solution)/shard_map/sketch/pallas_call | solution.py:140
  16.6 15.2 %all-to-all-start.1 = ((f32[16,32,128]{2,1,0:T(8,128)}), f32[16,32,128]{2,1,0:T(8,128)S(1)}, u32[]{:S(2)}, u32[]{:S(2)}) async-start(f32[16,32,128]{2,1,0:T(8,128)} %get-tuple-element.7), calls=%async_computation.1 | async-start | bytes 524288 | tf_op jit(solution)/shard_map/all_to_all | solution.py:389
  31.8 4.3 %collective-permute-start = (f32[40,128]{1,0:T(8,128)S(1)}, f32[40,128]{1,0:T(8,128)S(1)}, u32[]{:S(2)}, u32[]{:S(2)}) collective-permute-start(f32[40,128]{1,0:T(8,128)S(1)} %get-tuple-element.8), channel_id=1, source_target_pairs={{4,0},{0,4},{12,8},{8,12},{20,16},{16,20},{28,24},{24,28},{36,32},... | collective-permute-start | bytes 61448 | tf_op jit(solution)/shard_map/ppermute | solution.py:399
  36.2 0.8 collective-permute-done
  37.0 3.2 %collective-permute-start.1 = (f32[80,128]{1,0:T(8,128)S(1)}, f32[80,128]{1,0:T(8,128)S(1)}, u32[]{:S(2)}, u32[]{:S(2)}) collective-permute-start(f32[80,128]{1,0:T(8,128)S(1)} %pad_maximum_fusion), channel_id=1, source_target_pairs={{128,0},{132,4},{136,8},{140,12},{144,16},{148,20},{152,24},{156,2... | collective-permute-start | bytes 122888 | tf_op jit(solution)/shard_map/ppermute | solution.py:399
  40.2 1.8 %collective-permute-done.1 = f32[80,128]{1,0:T(8,128)S(1)} collective-permute-done((f32[80,128]{1,0:T(8,128)S(1)}, f32[80,128]{1,0:T(8,128)S(1)}, u32[]{:S(2)}, u32[]{:S(2)}) %collective-permute-start.1) | collective-permute-done | bytes 40992 | tf_op jit(solution)/shard_map/ppermute | solution.py:399
  42.1 4.6 %collective-permute-start.2 = (f32[160,128]{1,0:T(8,128)S(1)}, f32[160,128]{1,0:T(8,128)S(1)}, u32[]{:S(2)}, u32[]{:S(2)}) collective-permute-start(f32[160,128]{1,0:T(8,128)S(1)} %constant_dynamic-update-slice_fusion.near), channel_id=1, source_target_pairs={{384,0},{388,4},{392,8},{396,12},{400,16},{404,20},{408,24},{412,2... | collective-permute-start | bytes 245768 | tf_op jit(solution)/shard_map/ppermute | solution.py:399
  46.7 2.1 %collective-permute-done.2.away = f32[160,128]{1,0:T(8,128)S(1)} collective-permute-done((f32[160,128]{1,0:T(8,128)S(1)}, f32[160,128]{1,0:T(8,128)S(1)}, u32[]{:S(2)}, u32[]{:S(2)}) %collective-permute-start.2) | collective-permute-done | bytes 81952 | tf_op jit(solution)/shard_map/ppermute | solution.py:399
  48.8 0.0 all-to-all-done.1
  48.8 0.7 tile.1
  49.5 6.7 %all_to_all.25.parts = f32[4,24,128]{2,1,0:T(8,128)S(1)} all-to-all(f32[4,24,128]{2,1,0:T(8,128)S(1)} %tile.1), channel_id=1, replica_groups=mesh['dp'=128,'mp'=4] {'mp'}, dimensions={0} | all-to-all | bytes 98304 | tf_op jit(solution)/shard_map/all_to_all | solution.py:418
  56.2 23.6 %all_to_all.26.parts = f32[16,24,128]{2,1,0:T(8,128)S(1)} all-to-all(f32[16,24,128]{2,1,0:T(8,128)S(1)} %add.1), channel_id=1, replica_groups={{0,8,16,24,32,40,48,56,64,72,80,88,96,104,112,120},{4,12,20,28,36,44,52..., dimensions={0} | all-to-all | bytes 393216 | tf_op jit(solution)/shard_map/all_to_all | solution.py:389
  79.8 0.3 panel.1
  80.1 10.9 %all_to_all.27.mine = f32[4,272,128]{2,1,0:T(8,128)S(1)} all-to-all(f32[4,272,128]{2,1,0:T(8,128)S(1)} %panel.1), channel_id=1, replica_groups={{0,128,256,384},{4,132,260,388},{8,136,264,392},{12,140,268,396},{16,14..., dimensions={0} | all-to-all | bytes 1114112 | tf_op jit(solution)/shard_map/all_to_all | solution.py:389
  90.9 9.8 %collective-permute-start.3 = (f32[4,272,128]{2,1,0:T(8,128)S(1)}, f32[4,272,128]{2,1,0:T(8,128)S(1)}, u32[]{:S(2)}, u32[]{:S(2)}) collective-permute-start(f32[4,272,128]{2,1,0:T(8,128)S(1)} %all_to_all.27.mine), channel_id=1, source_target_pairs={{4,0},{0,4},{12,8},{8,12},{20,16},{16,20},{28,24},{24,28},{36,32},... | collective-permute-start | bytes 1671176 | tf_op jit(solution)/shard_map/ppermute | solution.py:399
  100.7 1.4 %collective-permute-done.3.theirs = f32[4,272,128]{2,1,0:T(8,128)S(1)} collective-permute-done((f32[4,272,128]{2,1,0:T(8,128)S(1)}, f32[4,272,128]{2,1,0:T(8,128)S(1)}, u32[]{:S(2)}, u32[]{:S(2)}) %collective-permute-start.3) | collective-permute-done | bytes 557088 | tf_op jit(solution)/shard_map/ppermute | solution.py:399
  102.1 21.1 %solve.1 = f32[4,32]{1,0:T(4,128)} custom-call(s32[1]{0:T(128)} %bitcast.pos, f32[4,272,128]{2,1,0:T(8,128)S(1)} %all_to_all.27.mine, f32[4,272,128]{2,1,0:T(8,128)S(1)} %collective-permute-done.3.theirs), custom_call_target="tpu_custom_call" | custom-call | tf_op jit(solution)/shard_map/solve/pallas_call | solution.py:369
  (5 shorter events, 0.0 us)
Async XLA Ops:
  0.0 14.9 %copy-start = (s32[4]{0:T(128)S(1)}, s32[4]{0:T(128)}, u32[]{:S(2)}) copy-start(s32[4]{0:T(128)} %tlen.1) | copy-start | bytes 52
  4.2 10.7 %all-to-all-start = ((f32[4,160,128]{2,1,0:T(8,128)}), f32[4,160,128]{2,1,0:T(8,128)S(1)}, u32[]{:S(2)}, u32[]{:S(2)}) async-start(f32[4,160,128]{2,1,0:T(8,128)} %project.1), calls=%async_computation | async-start | bytes 655360 | tf_op jit(solution)/shard_map/all_to_all | solution.py:412
  16.6 32.2 %all-to-all-start.1 = ((f32[16,32,128]{2,1,0:T(8,128)}), f32[16,32,128]{2,1,0:T(8,128)S(1)}, u32[]{:S(2)}, u32[]{:S(2)}) async-start(f32[16,32,128]{2,1,0:T(8,128)} %get-tuple-element.7), calls=%async_computation.1 | async-start | bytes 524288 | tf_op jit(solution)/shard_map/all_to_all | solution.py:389
  31.8 5.2 %collective-permute-start = (f32[40,128]{1,0:T(8,128)S(1)}, f32[40,128]{1,0:T(8,128)S(1)}, u32[]{:S(2)}, u32[]{:S(2)}) collective-permute-start(f32[40,128]{1,0:T(8,128)S(1)} %get-tuple-element.8), channel_id=1, source_target_pairs={{4,0},{0,4},{12,8},{8,12},{20,16},{16,20},{28,24},{24,28},{36,32},... | collective-permute-start | bytes 61448 | tf_op jit(solution)/shard_map/ppermute | solution.py:399
  37.0 5.0 %collective-permute-start.1 = (f32[80,128]{1,0:T(8,128)S(1)}, f32[80,128]{1,0:T(8,128)S(1)}, u32[]{:S(2)}, u32[]{:S(2)}) collective-permute-start(f32[80,128]{1,0:T(8,128)S(1)} %pad_maximum_fusion), channel_id=1, source_target_pairs={{128,0},{132,4},{136,8},{140,12},{144,16},{148,20},{152,24},{156,2... | collective-permute-start | bytes 122888 | tf_op jit(solution)/shard_map/ppermute | solution.py:399
  42.1 6.8 %collective-permute-start.2 = (f32[160,128]{1,0:T(8,128)S(1)}, f32[160,128]{1,0:T(8,128)S(1)}, u32[]{:S(2)}, u32[]{:S(2)}) collective-permute-start(f32[160,128]{1,0:T(8,128)S(1)} %constant_dynamic-update-slice_fusion.near), channel_id=1, source_target_pairs={{384,0},{388,4},{392,8},{396,12},{400,16},{404,20},{408,24},{412,2... | collective-permute-start | bytes 245768 | tf_op jit(solution)/shard_map/ppermute | solution.py:399
  90.9 11.2 %collective-permute-start.3 = (f32[4,272,128]{2,1,0:T(8,128)S(1)}, f32[4,272,128]{2,1,0:T(8,128)S(1)}, u32[]{:S(2)}, u32[]{:S(2)}) collective-permute-start(f32[4,272,128]{2,1,0:T(8,128)S(1)} %all_to_all.27.mine), channel_id=1, source_target_pairs={{4,0},{0,4},{12,8},{8,12},{20,16},{16,20},{28,24},{24,28},{36,32},... | collective-permute-start | bytes 1671176 | tf_op jit(solution)/shard_map/ppermute | solution.py:399

commit v4 on v3

--- a/solution.py
+++ b/solution.py
@@ -226,22 +226,43 @@
     )(parts)
 
 
+def rank16(a, b):
+    def parts(x):
+        one = x.astype(jnp.bfloat16)
+        x = x - one.astype(F32)
+        two = x.astype(jnp.bfloat16)
+        return one, two, (x - two.astype(F32)).astype(jnp.bfloat16)
+
+    a1, a2, a3 = parts(a)
+    b1, b2, b3 = parts(b)
+    left = jnp.concatenate([a1, a1, a2, a2, a1, a3], axis=0)
+    right = jnp.concatenate([b1, b2, b1, b2, b3, b1], axis=0)
+    return dot(left, right, 0, 0, None)
+
+
 def inverse_factor(tiles):
     lane = lanes(8, 128)
     sub = lax.broadcasted_iota(jnp.int32, (8, 128), 0)
     count = len(tiles)
     tiles = list(tiles)
-    for q in range(count):
-        first = 8 * q
+
+    def inside(q):
+        return (lane >= 8 * q) & (lane < 8 * q + 8)
+
+    def column(r, q, c):
+        return jnp.broadcast_to(tiles[r][:, 8 * q + c : 8 * q + c + 1], (8, 128))
+
+    def stack(rows):
+        merged = rows[0]
+        for p in range(1, 8):
+            merged = jnp.where(sub == p, rows[p], merged)
+        return merged
+
+    def panel_of(q):
         block = tiles[q]
-        inside = (lane >= first) & (lane < first + 8)
-
-        def column(r, c):
-            return jnp.broadcast_to(tiles[r][:, first + c : first + c + 1], (8, 128))
-
         a = {}
         for c in range(8):
-            whole = column(q, c)
+            whole = column(q, q, c)
             for p in range(c, 8):
                 a[p, c] = jnp.broadcast_to(whole[p : p + 1, :], (8, 128))
         mult = {}
@@ -257,9 +278,9 @@
                 for c in range(p + 2, k + 1):
                     a[k, c] = a[k, c] - (mult[k, p] * a[c, p] + mult[k, p + 1] * a[c, p + 1])
             for r in (p, p + 1):
-                unit = (lane == first + r).astype(F32)
+                unit = (lane == 8 * q + r).astype(F32)
                 line = jnp.broadcast_to(block[r : r + 1, :], (8, 128))
-                line = jnp.where(inside, unit, line)
+                line = jnp.where(inside(q), unit, line)
                 for k in range(p):
                     line = line - mult[r, k] * lines[k]
                 lines.append(line)
@@ -270,38 +291,48 @@
             top = lax.rsqrt(d)
             rows.append(low * top)
             rows.append(turned * (top * root))
-        merged = rows[0]
-        for p in range(1, 8):
-            merged = jnp.where(sub == p, rows[p], merged)
-        tiles[q] = merged
-        if q + 1 < count:
-            rest = jnp.where(inside, 0.0, tiles[q + 1])
-            cols = []
-            for p in range(0, 8, 2):
-                for r in (p, p + 1):
-                    col = column(q + 1, r)
-                    for k in range(p):
-                        col = col - mult[r, k] * cols[k]
-                    cols.append(col)
-                rest = rest - (cols[p] * scaled[p] + cols[p + 1] * scaled[p + 1])
+        tiles[q] = stack(rows)
+        return block, mult, scaled
+
+    def update_next(q, mult, scaled):
+        rest = jnp.where(inside(q), 0.0, tiles[q + 1])
+        cols = []
+        for p in range(0, 8, 2):
+            for r in (p, p + 1):
+                col = column(q + 1, q, r)
+                for k in range(p):
+                    col = col - mult[r, k] * cols[k]
+                cols.append(col)
+            rest = rest - (cols[p] * scaled[p] + cols[p + 1] * scaled[p + 1])
+        tiles[q + 1] = rest
+
+    def substitute(mult, scaled):
+        back = list(scaled)
+        for p in range(5, -1, -1):
+            for k in range(7, p + 1 - p % 2, -1):
+                back[p] = back[p] - mult[k, p] * back[k]
+        return back
+
+    for q in range(0, count, 2):
+        block0, mult0, scaled0 = panel_of(q)
+        update_next(q, mult0, scaled0)
         if q + 2 < count:
-            back = list(scaled)
-            for p in range(5, -1, -1):
-                for k in range(7, p + 1 - p % 2, -1):
-                    back[p] = back[p] - mult[k, p] * back[k]
-            other = jnp.where(inside, 0.0, tiles[q + 2])
+            back0 = substitute(mult0, scaled0)
+            other = jnp.where(inside(q), 0.0, tiles[q + 2])
             for c in range(8):
-                other = other - column(q + 2, c) * back[c]
+                other = other - column(q + 2, q, c) * back0[c]
             tiles[q + 2] = other
-        if q + 3 < count:
-            stacked = back[0]
-            for p in range(1, 8):
-                stacked = jnp.where(sub == p, back[p], stacked)
-            far = dot(block, stacked, 0, 0)
+        block1, mult1, scaled1 = panel_of(q + 1)
+        if q + 2 < count:
+            update_next(q + 1, mult1, scaled1)
+            back1 = substitute(mult1, scaled1)
+            both = inside(q) | inside(q + 1)
+            right = jnp.concatenate(
+                [jnp.where(inside(q + 1), 0.0, stack(back0)), stack(back1)], axis=0
+            )
+            far = rank16(jnp.concatenate([block0, block1], axis=0), right)
             for r in range(q + 3, count):
-                tiles[r] = jnp.where(inside, 0.0, tiles[r]) - far[8 * r : 8 * r + 8, :]
-        if q + 1 < count:
-            tiles[q + 1] = rest
+                tiles[r] = jnp.where(both, 0.0, tiles[r]) - far[8 * r : 8 * r + 8, :]
     for q in range(count):
         tiles[q] = jnp.where(lane <= sub + 8 * q, tiles[q], 0.0)
     return tiles
@@ -331,6 +362,8 @@
             if j == k:
                 block = block + eye
             full[128 * k : 128 * k + 128, 128 * j : 128 * j + 128] = block
+        for k in range(j + 1, NY):
+            full[128 * k : 128 * k + 128, 128 * j : 128 * j + 128] = jnp.zeros((128, 128), F32)
         even = jnp.where(first, mine[j, 256:272, :], theirs[j, 256:272, :])
         odd = jnp.where(first, theirs[j, 256:272, :], mine[j, 256:272, :])
         turn[pl.ds(0, 16, stride=2), :] = jnp.where(left[:16], even, pltpu.roll(odd, 64, 1))
@@ -339,29 +372,23 @@
         unit = (row + 128 * j == base + (lane - 32) * 16).astype(F32)
         right = jnp.where(lane < 32, turned, jnp.where(lane < 36, unit, 0.0))
         full[128 * j : 128 * j + 128, 512:640] = right
-    product = None
-    diagonal = full[0:128, 0:128]
-    for k in range(4):
-        s = slice(128 * k, 128 * k + 128)
-        tiles = inverse_factor([diagonal[8 * t : 8 * t + 8, :] for t in range(16)])
+    def step(k, carry):
+        at = pl.multiple_of(k * 128, 128)
+        s = pl.ds(at, 128)
+        tiles = inverse_factor([full[pl.ds(at + 8 * t, 8), s] for t in range(16)])
         for t in range(16):
-            inv[k, 8 * t : 8 * t + 8, :] = tiles[t]
-        after = 128 * k + 128
-        if k < 3:
-            n = slice(after, after + 128)
-            strip = dot(inv[k], full[s, n], 1, 0)
-            full[s, n] = strip
-            diagonal = full[n, n] - dot(strip, strip, 0, 0)
-            rest = slice(after + 128, 640)
-            full[s, rest] = dot(inv[k], full[s, rest], 1, 0)
-            full[n, rest] -= dot(full[s, n], full[s, rest], 0, 0)
-            for i in range(k + 2, 4):
-                to = slice(128 * i, 128 * i + 128)
-                full[to, 128 * i : 640] -= dot(full[s, to], full[s, 128 * i : 640], 0, 0)
-        else:
-            full[s, after:640] = dot(inv[k], full[s, after:640], 1, 0)
-        part = dot(full[s, 512:640], full[s, 512:640], 0, 0)
-        product = part if product is None else product + part
+            inv[8 * t : 8 * t + 8, :] = tiles[t]
+        full[s, :] = dot(inv[...], full[s, :], 1, 0)
+
+        def trail(i, inner):
+            to = pl.ds(pl.multiple_of(i * 128, 128), 128)
+            full[to, :] -= dot(full[s, to], full[s, :], 0, 0)
+            return inner
+
+        return lax.fori_loop(k + 1, 4, trail, carry)
+
+    lax.fori_loop(0, 4, step, 0)
+    product = dot(full[:, 512:640], full[:, 512:640], 0, 0)
     out[...] = product[32:36, 0:32]
 
 
@@ -373,7 +400,7 @@
         out_specs=VM,
         scratch_shapes=[
             pltpu.VMEM((512, 640), F32),
-            pltpu.VMEM((4, 128, 128), F32),
+            pltpu.VMEM((128, 128), F32),
             pltpu.VMEM((128, 128), F32),
         ],
         compiler_params=params(),

time: 124 us -> 122 us (0.984)
  Pallas kernels: 27.9 us -> 26 us
    pallas_call x1, Pallas kernels: 21.1 us -> 19.2 us  [solve(): pl.pallas_call(solve_kernel, out_shape=shape(4, 32), in_specs=[SM] + [VM]...]
where the time goes in v4:
time: 122 us; the launch traced here: 121 us
  starting transfers between devices  41.8 us (34%)
  blocking collectives  41.2 us (34%)
  Pallas kernels  26 us (21%)
  waiting for transfers between devices  11.5 us (9%)
    all_to_all x2, blocking collectives, exchange(): lax.all_to_all(value, 'dp', 0, 0, axis_index_groups=groups, tiled=True)  34.4 us
    ppermute x4, starting transfers between devices, swap(): return lax.ppermute(value, 'dp', pairs)  21.8 us
    pallas_call x1, Pallas kernels, solve(): pl.pallas_call(solve_kernel, out_shape=shape(4, 32), in_specs=[SM] + [VM]...  19.2 us
    all_to_all x1, starting transfers between devices, exchange(): lax.all_to_all(value, 'dp', 0, 0, axis_index_groups=groups, tiled=True)  15.2 us
    all_to_all x1, blocking collectives, shards(): tiles = lax.all_to_all(tile(pos, line, near, away), 'mp', 0, 0, tiled=True)  6.75 us
    ppermute x4, waiting for transfers between devices, swap(): return lax.ppermute(value, 'dp', pairs)  6.29 us
    all_to_all x1, waiting for transfers between devices, shards(): parts = lax.all_to_all(parts, 'mp', 0, 0, tiled=True)  5.23 us
    all_to_all x1, starting transfers between devices, shards(): parts = lax.all_to_all(parts, 'mp', 0, 0, tiled=True)  4.85 us
  transfers between devices with their start and end apart: 6, of which 5 were waited for; matrix products, arithmetic and copies ran while one was open for 0% of the time, Pallas kernels for 0%

profile of v4, /device:TPU:1, one launch (start us, length us, event | category | flops | bytes accessed | tf_op | source)
XLA Modules:
  0.0 121.3 jit_solution(18151828603520254463)
XLA Ops:
  0.0 0.0 copy-start
  0.0 4.2 %project.1 = f32[4,160,128]{2,1,0:T(8,128)} custom-call(bf16[4,64,3584]{2,1,0:T(8,128)(2,1)} %tg.1, bf16[4,64,1024]{2,1,0:T(8,128)(2,1)} %ta.1, bf16[1,64,3584]{2,1,0:T(8,128)(2,1)} %qg.1, bf16[1,64,1024]{2,1,0:T(8,128)(2,1)} %qa.1, bf16[64,3584]{1,0:T(8,128)(2,1)} %of.1, bf16[64,1024]{1,0:T(8,128)(2,1)} %inf.1), custom_call_target="tpu_custom_call" | custom-call | tf_op jit(solution)/shard_map/project/pallas_call | solution.py:84
  4.2 4.9 %all-to-all-start = ((f32[4,160,128]{2,1,0:T(8,128)}), f32[4,160,128]{2,1,0:T(8,128)S(1)}, u32[]{:S(2)}, u32[]{:S(2)}) async-start(f32[4,160,128]{2,1,0:T(8,128)} %project.1), calls=%async_computation | async-start | bytes 655360 | tf_op jit(solution)/shard_map/all_to_all | solution.py:439
  9.7 5.2 %all-to-all-done.parts = f32[4,160,128]{2,1,0:T(8,128)S(1)} async-done(((f32[4,160,128]{2,1,0:T(8,128)}), f32[4,160,128]{2,1,0:T(8,128)S(1)}, u32[]{:S(2)}, u32[]{:S(2)}) %all-to-all-start) | async-done | bytes 327712 | tf_op jit(solution)/shard_map/all_to_all | solution.py:439
  14.9 0.0 copy-done
  14.9 1.7 %sketch.1 = (f32[16,32,128]{2,1,0:T(8,128)}, f32[40,128]{1,0:T(8,128)S(1)}) custom-call(s32[4]{0:T(128)S(1)} %copy-done, s32[1]{0:T(128)S(6)} %copy.11.qlen, f32[4,160,128]{2,1,0:T(8,128)S(1)} %all-to-all-done.parts), custom_call_target="tpu_custom_call" | custom-call | tf_op jit(solution)/shard_map/sketch/pallas_call | solution.py:140
  16.6 15.2 %all-to-all-start.1 = ((f32[16,32,128]{2,1,0:T(8,128)}), f32[16,32,128]{2,1,0:T(8,128)S(1)}, u32[]{:S(2)}, u32[]{:S(2)}) async-start(f32[16,32,128]{2,1,0:T(8,128)} %get-tuple-element.7), calls=%async_computation.1 | async-start | bytes 524288 | tf_op jit(solution)/shard_map/all_to_all | solution.py:416
  31.8 4.3 %collective-permute-start = (f32[40,128]{1,0:T(8,128)S(1)}, f32[40,128]{1,0:T(8,128)S(1)}, u32[]{:S(2)}, u32[]{:S(2)}) collective-permute-start(f32[40,128]{1,0:T(8,128)S(1)} %get-tuple-element.8), channel_id=1, source_target_pairs={{4,0},{0,4},{12,8},{8,12},{20,16},{16,20},{28,24},{24,28},{36,32},... | collective-permute-start | bytes 61448 | tf_op jit(solution)/shard_map/ppermute | solution.py:426
  36.2 0.8 collective-permute-done
  37.0 3.2 %collective-permute-start.1 = (f32[80,128]{1,0:T(8,128)S(1)}, f32[80,128]{1,0:T(8,128)S(1)}, u32[]{:S(2)}, u32[]{:S(2)}) collective-permute-start(f32[80,128]{1,0:T(8,128)S(1)} %pad_maximum_fusion), channel_id=1, source_target_pairs={{128,0},{132,4},{136,8},{140,12},{144,16},{148,20},{152,24},{156,2... | collective-permute-start | bytes 122888 | tf_op jit(solution)/shard_map/ppermute | solution.py:426
  40.2 1.8 %collective-permute-done.1 = f32[80,128]{1,0:T(8,128)S(1)} collective-permute-done((f32[80,128]{1,0:T(8,128)S(1)}, f32[80,128]{1,0:T(8,128)S(1)}, u32[]{:S(2)}, u32[]{:S(2)}) %collective-permute-start.1) | collective-permute-done | bytes 40992 | tf_op jit(solution)/shard_map/ppermute | solution.py:426
  42.1 4.6 %collective-permute-start.2 = (f32[160,128]{1,0:T(8,128)S(1)}, f32[160,128]{1,0:T(8,128)S(1)}, u32[]{:S(2)}, u32[]{:S(2)}) collective-permute-start(f32[160,128]{1,0:T(8,128)S(1)} %constant_dynamic-update-slice_fusion.near), channel_id=1, source_target_pairs={{384,0},{388,4},{392,8},{396,12},{400,16},{404,20},{408,24},{412,2... | collective-permute-start | bytes 245768 | tf_op jit(solution)/shard_map/ppermute | solution.py:426
  46.7 2.1 %collective-permute-done.2.away = f32[160,128]{1,0:T(8,128)S(1)} collective-permute-done((f32[160,128]{1,0:T(8,128)S(1)}, f32[160,128]{1,0:T(8,128)S(1)}, u32[]{:S(2)}, u32[]{:S(2)}) %collective-permute-start.2) | collective-permute-done | bytes 81952 | tf_op jit(solution)/shard_map/ppermute | solution.py:426
  48.8 0.0 all-to-all-done.1
  48.8 0.7 tile.1
  49.5 6.7 %all_to_all.25.parts = f32[4,24,128]{2,1,0:T(8,128)S(1)} all-to-all(f32[4,24,128]{2,1,0:T(8,128)S(1)} %tile.1), channel_id=1, replica_groups=mesh['dp'=128,'mp'=4] {'mp'}, dimensions={0} | all-to-all | bytes 98304 | tf_op jit(solution)/shard_map/all_to_all | solution.py:445
  56.2 23.6 %all_to_all.26.parts = f32[16,24,128]{2,1,0:T(8,128)S(1)} all-to-all(f32[16,24,128]{2,1,0:T(8,128)S(1)} %add.1), channel_id=1, replica_groups={{0,8,16,24,32,40,48,56,64,72,80,88,96,104,112,120},{4,12,20,28,36,44,52..., dimensions={0} | all-to-all | bytes 393216 | tf_op jit(solution)/shard_map/all_to_all | solution.py:416
  79.8 0.3 panel.1
  80.1 10.9 %all_to_all.27.mine = f32[4,272,128]{2,1,0:T(8,128)S(1)} all-to-all(f32[4,272,128]{2,1,0:T(8,128)S(1)} %panel.1), channel_id=1, replica_groups={{0,128,256,384},{4,132,260,388},{8,136,264,392},{12,140,268,396},{16,14..., dimensions={0} | all-to-all | bytes 1114112 | tf_op jit(solution)/shard_map/all_to_all | solution.py:416
  90.9 9.6 %collective-permute-start.3 = (f32[4,272,128]{2,1,0:T(8,128)S(1)}, f32[4,272,128]{2,1,0:T(8,128)S(1)}, u32[]{:S(2)}, u32[]{:S(2)}) collective-permute-start(f32[4,272,128]{2,1,0:T(8,128)S(1)} %all_to_all.27.mine), channel_id=1, source_target_pairs={{4,0},{0,4},{12,8},{8,12},{20,16},{16,20},{28,24},{24,28},{36,32},... | collective-permute-start | bytes 1671176 | tf_op jit(solution)/shard_map/ppermute | solution.py:426
  100.5 1.6 %collective-permute-done.3.theirs = f32[4,272,128]{2,1,0:T(8,128)S(1)} collective-permute-done((f32[4,272,128]{2,1,0:T(8,128)S(1)}, f32[4,272,128]{2,1,0:T(8,128)S(1)}, u32[]{:S(2)}, u32[]{:S(2)}) %collective-permute-start.3) | collective-permute-done | bytes 557088 | tf_op jit(solution)/shard_map/ppermute | solution.py:426
  102.1 19.2 %solve.1 = f32[4,32]{1,0:T(4,128)} custom-call(s32[1]{0:T(128)} %bitcast.pos, f32[4,272,128]{2,1,0:T(8,128)S(1)} %all_to_all.27.mine, f32[4,272,128]{2,1,0:T(8,128)S(1)} %collective-permute-done.3.theirs), custom_call_target="tpu_custom_call" | custom-call | tf_op jit(solution)/shard_map/solve/pallas_call | solution.py:396
  (5 shorter events, 0.0 us)
Async XLA Ops:
  0.0 14.9 %copy-start = (s32[4]{0:T(128)S(1)}, s32[4]{0:T(128)}, u32[]{:S(2)}) copy-start(s32[4]{0:T(128)} %tlen.1) | copy-start | bytes 52
  4.2 10.7 %all-to-all-start = ((f32[4,160,128]{2,1,0:T(8,128)}), f32[4,160,128]{2,1,0:T(8,128)S(1)}, u32[]{:S(2)}, u32[]{:S(2)}) async-start(f32[4,160,128]{2,1,0:T(8,128)} %project.1), calls=%async_computation | async-start | bytes 655360 | tf_op jit(solution)/shard_map/all_to_all | solution.py:439
  16.6 32.2 %all-to-all-start.1 = ((f32[16,32,128]{2,1,0:T(8,128)}), f32[16,32,128]{2,1,0:T(8,128)S(1)}, u32[]{:S(2)}, u32[]{:S(2)}) async-start(f32[16,32,128]{2,1,0:T(8,128)} %get-tuple-element.7), calls=%async_computation.1 | async-start | bytes 524288 | tf_op jit(solution)/shard_map/all_to_all | solution.py:416
  31.8 5.2 %collective-permute-start = (f32[40,128]{1,0:T(8,128)S(1)}, f32[40,128]{1,0:T(8,128)S(1)}, u32[]{:S(2)}, u32[]{:S(2)}) collective-permute-start(f32[40,128]{1,0:T(8,128)S(1)} %get-tuple-element.8), channel_id=1, source_target_pairs={{4,0},{0,4},{12,8},{8,12},{20,16},{16,20},{28,24},{24,28},{36,32},... | collective-permute-start | bytes 61448 | tf_op jit(solution)/shard_map/ppermute | solution.py:426
  37.0 5.0 %collective-permute-start.1 = (f32[80,128]{1,0:T(8,128)S(1)}, f32[80,128]{1,0:T(8,128)S(1)}, u32[]{:S(2)}, u32[]{:S(2)}) collective-permute-start(f32[80,128]{1,0:T(8,128)S(1)} %pad_maximum_fusion), channel_id=1, source_target_pairs={{128,0},{132,4},{136,8},{140,12},{144,16},{148,20},{152,24},{156,2... | collective-permute-start | bytes 122888 | tf_op jit(solution)/shard_map/ppermute | solution.py:426
  42.1 6.8 %collective-permute-start.2 = (f32[160,128]{1,0:T(8,128)S(1)}, f32[160,128]{1,0:T(8,128)S(1)}, u32[]{:S(2)}, u32[]{:S(2)}) collective-permute-start(f32[160,128]{1,0:T(8,128)S(1)} %constant_dynamic-update-slice_fusion.near), channel_id=1, source_target_pairs={{384,0},{388,4},{392,8},{396,12},{400,16},{404,20},{408,24},{412,2... | collective-permute-start | bytes 245768 | tf_op jit(solution)/shard_map/ppermute | solution.py:426
  90.9 11.2 %collective-permute-start.3 = (f32[4,272,128]{2,1,0:T(8,128)S(1)}, f32[4,272,128]{2,1,0:T(8,128)S(1)}, u32[]{:S(2)}, u32[]{:S(2)}) collective-permute-start(f32[4,272,128]{2,1,0:T(8,128)S(1)} %all_to_all.27.mine), channel_id=1, source_target_pairs={{4,0},{0,4},{12,8},{8,12},{20,16},{16,20},{28,24},{24,28},{36,32},... | collective-permute-start | bytes 1671176 | tf_op jit(solution)/shard_map/ppermute | solution.py:426

commit v5 on v4

--- a/solution.py
+++ b/solution.py
@@ -226,18 +226,19 @@
     )(parts)
 
 
-def rank16(a, b):
-    def parts(x):
-        one = x.astype(jnp.bfloat16)
-        x = x - one.astype(F32)
-        two = x.astype(jnp.bfloat16)
-        return one, two, (x - two.astype(F32)).astype(jnp.bfloat16)
-
-    a1, a2, a3 = parts(a)
-    b1, b2, b3 = parts(b)
-    left = jnp.concatenate([a1, a1, a2, a2, a1, a3], axis=0)
-    right = jnp.concatenate([b1, b2, b1, b2, b3, b1], axis=0)
-    return dot(left, right, 0, 0, None)
+def thirds(x):
+    one = x.astype(jnp.bfloat16)
+    x = x - one.astype(F32)
+    two = x.astype(jnp.bfloat16)
+    return one, two, (x - two.astype(F32)).astype(jnp.bfloat16)
+
+
+def stacked(a, b, ca, cb):
+    a1, a2, a3 = thirds(a)
+    b1, b2, b3 = thirds(b)
+    left = jnp.concatenate([a1, a1, a2, a2, a1, a3], axis=ca)
+    right = jnp.concatenate([b1, b2, b1, b2, b3, b1], axis=cb)
+    return dot(left, right, ca, cb, None)
 
 
 def inverse_factor(tiles):
@@ -330,7 +331,7 @@
             right = jnp.concatenate(
                 [jnp.where(inside(q + 1), 0.0, stack(back0)), stack(back1)], axis=0
             )
-            far = rank16(jnp.concatenate([block0, block1], axis=0), right)
+            far = stacked(jnp.concatenate([block0, block1], axis=0), right, 0, 0)
             for r in range(q + 3, count):
                 tiles[r] = jnp.where(both, 0.0, tiles[r]) - far[8 * r : 8 * r + 8, :]
     for q in range(count):
@@ -378,18 +379,24 @@
         tiles = inverse_factor([full[pl.ds(at + 8 * t, 8), s] for t in range(16)])
         for t in range(16):
             inv[8 * t : 8 * t + 8, :] = tiles[t]
-        full[s, :] = dot(inv[...], full[s, :], 1, 0)
-
-        def trail(i, inner):
-            to = pl.ds(pl.multiple_of(i * 128, 128), 128)
-            full[to, :] -= dot(full[s, to], full[s, :], 0, 0)
-            return inner
-
-        return lax.fori_loop(k + 1, 4, trail, carry)
+
+        for j in range(4):
+
+            @pl.when(k == j)
+            def _():
+                s = slice(128 * j, 128 * j + 128)
+                after = 128 * j + 128
+                strip = stacked(inv[...], full[s, after:640], 1, 0)
+                full[s, 512:640] = strip[:, 512 - after :]
+                if j < 3:
+                    turned = strip[:, : 512 - after].T
+                    full[after:512, after:640] -= stacked(turned, strip, 1, 0)
+
+        return carry
 
     lax.fori_loop(0, 4, step, 0)
-    product = dot(full[:, 512:640], full[:, 512:640], 0, 0)
-    out[...] = product[32:36, 0:32]
+    right = full[:, 512:640]
+    out[...] = stacked(right.T[32:40, :], right, 1, 0)[0:4, 0:32]
 
 
 def solve(pos, mine, theirs):

time: 122 us -> 120 us (0.984)
  Pallas kernels: 26 us -> 23.8 us
    pallas_call x1, Pallas kernels: 19.2 us -> 17 us  [solve(): pl.pallas_call(solve_kernel, out_shape=shape(4, 32), in_specs=[SM] + [VM]...]
where the time goes in v5:
time: 120 us; the launch traced here: 119 us
  starting transfers between devices  41.8 us (35%)
  blocking collectives  41.2 us (34%)
  Pallas kernels  23.8 us (20%)
  waiting for transfers between devices  11.5 us (10%)
    all_to_all x2, blocking collectives, exchange(): lax.all_to_all(value, 'dp', 0, 0, axis_index_groups=groups, tiled=True)  34.4 us
    ppermute x4, starting transfers between devices, swap(): return lax.ppermute(value, 'dp', pairs)  21.8 us
    pallas_call x1, Pallas kernels, solve(): pl.pallas_call(solve_kernel, out_shape=shape(4, 32), in_specs=[SM] + [VM]...  17 us
    all_to_all x1, starting transfers between devices, exchange(): lax.all_to_all(value, 'dp', 0, 0, axis_index_groups=groups, tiled=True)  15.2 us
    all_to_all x1, blocking collectives, shards(): tiles = lax.all_to_all(tile(pos, line, near, away), 'mp', 0, 0, tiled=True)  6.75 us
    ppermute x4, waiting for transfers between devices, swap(): return lax.ppermute(value, 'dp', pairs)  6.29 us
    all_to_all x1, waiting for transfers between devices, shards(): parts = lax.all_to_all(parts, 'mp', 0, 0, tiled=True)  5.23 us
    all_to_all x1, starting transfers between devices, shards(): parts = lax.all_to_all(parts, 'mp', 0, 0, tiled=True)  4.85 us
  transfers between devices with their start and end apart: 6, of which 5 were waited for; matrix products, arithmetic and copies ran while one was open for 0% of the time, Pallas kernels for 0%

profile of v5, /device:TPU:1, one launch (start us, length us, event | category | flops | bytes accessed | tf_op | source)
XLA Modules:
  0.0 119.0 jit_solution(850769925752318593)
XLA Ops:
  0.0 0.0 copy-start
  0.0 4.2 %project.1 = f32[4,160,128]{2,1,0:T(8,128)} custom-call(bf16[4,64,3584]{2,1,0:T(8,128)(2,1)} %tg.1, bf16[4,64,1024]{2,1,0:T(8,128)(2,1)} %ta.1, bf16[1,64,3584]{2,1,0:T(8,128)(2,1)} %qg.1, bf16[1,64,1024]{2,1,0:T(8,128)(2,1)} %qa.1, bf16[64,3584]{1,0:T(8,128)(2,1)} %of.1, bf16[64,1024]{1,0:T(8,128)(2,1)} %inf.1), custom_call_target="tpu_custom_call" | custom-call | tf_op jit(solution)/shard_map/project/pallas_call | solution.py:84
  4.2 4.9 %all-to-all-start = ((f32[4,160,128]{2,1,0:T(8,128)}), f32[4,160,128]{2,1,0:T(8,128)S(1)}, u32[]{:S(2)}, u32[]{:S(2)}) async-start(f32[4,160,128]{2,1,0:T(8,128)} %project.1), calls=%async_computation | async-start | bytes 655360 | tf_op jit(solution)/shard_map/all_to_all | solution.py:446
  9.7 5.2 %all-to-all-done.parts = f32[4,160,128]{2,1,0:T(8,128)S(1)} async-done(((f32[4,160,128]{2,1,0:T(8,128)}), f32[4,160,128]{2,1,0:T(8,128)S(1)}, u32[]{:S(2)}, u32[]{:S(2)}) %all-to-all-start) | async-done | bytes 327712 | tf_op jit(solution)/shard_map/all_to_all | solution.py:446
  14.9 0.0 copy-done
  14.9 1.7 %sketch.1 = (f32[16,32,128]{2,1,0:T(8,128)}, f32[40,128]{1,0:T(8,128)S(1)}) custom-call(s32[4]{0:T(128)S(1)} %copy-done, s32[1]{0:T(128)S(6)} %copy.11.qlen, f32[4,160,128]{2,1,0:T(8,128)S(1)} %all-to-all-done.parts), custom_call_target="tpu_custom_call" | custom-call | tf_op jit(solution)/shard_map/sketch/pallas_call | solution.py:140
  16.6 15.2 %all-to-all-start.1 = ((f32[16,32,128]{2,1,0:T(8,128)}), f32[16,32,128]{2,1,0:T(8,128)S(1)}, u32[]{:S(2)}, u32[]{:S(2)}) async-start(f32[16,32,128]{2,1,0:T(8,128)} %get-tuple-element.7), calls=%async_computation.1 | async-start | bytes 524288 | tf_op jit(solution)/shard_map/all_to_all | solution.py:423
  31.8 4.3 %collective-permute-start = (f32[40,128]{1,0:T(8,128)S(1)}, f32[40,128]{1,0:T(8,128)S(1)}, u32[]{:S(2)}, u32[]{:S(2)}) collective-permute-start(f32[40,128]{1,0:T(8,128)S(1)} %get-tuple-element.8), channel_id=1, source_target_pairs={{4,0},{0,4},{12,8},{8,12},{20,16},{16,20},{28,24},{24,28},{36,32},... | collective-permute-start | bytes 61448 | tf_op jit(solution)/shard_map/ppermute | solution.py:433
  36.2 0.8 collective-permute-done
  37.0 3.2 %collective-permute-start.1 = (f32[80,128]{1,0:T(8,128)S(1)}, f32[80,128]{1,0:T(8,128)S(1)}, u32[]{:S(2)}, u32[]{:S(2)}) collective-permute-start(f32[80,128]{1,0:T(8,128)S(1)} %pad_maximum_fusion), channel_id=1, source_target_pairs={{128,0},{132,4},{136,8},{140,12},{144,16},{148,20},{152,24},{156,2... | collective-permute-start | bytes 122888 | tf_op jit(solution)/shard_map/ppermute | solution.py:433
  40.2 1.8 %collective-permute-done.1 = f32[80,128]{1,0:T(8,128)S(1)} collective-permute-done((f32[80,128]{1,0:T(8,128)S(1)}, f32[80,128]{1,0:T(8,128)S(1)}, u32[]{:S(2)}, u32[]{:S(2)}) %collective-permute-start.1) | collective-permute-done | bytes 40992 | tf_op jit(solution)/shard_map/ppermute | solution.py:433
  42.1 4.6 %collective-permute-start.2 = (f32[160,128]{1,0:T(8,128)S(1)}, f32[160,128]{1,0:T(8,128)S(1)}, u32[]{:S(2)}, u32[]{:S(2)}) collective-permute-start(f32[160,128]{1,0:T(8,128)S(1)} %constant_dynamic-update-slice_fusion.near), channel_id=1, source_target_pairs={{384,0},{388,4},{392,8},{396,12},{400,16},{404,20},{408,24},{412,2... | collective-permute-start | bytes 245768 | tf_op jit(solution)/shard_map/ppermute | solution.py:433
  46.7 2.1 %collective-permute-done.2.away = f32[160,128]{1,0:T(8,128)S(1)} collective-permute-done((f32[160,128]{1,0:T(8,128)S(1)}, f32[160,128]{1,0:T(8,128)S(1)}, u32[]{:S(2)}, u32[]{:S(2)}) %collective-permute-start.2) | collective-permute-done | bytes 81952 | tf_op jit(solution)/shard_map/ppermute | solution.py:433
  48.8 0.0 all-to-all-done.1
  48.8 0.7 tile.1
  49.5 6.7 %all_to_all.25.parts = f32[4,24,128]{2,1,0:T(8,128)S(1)} all-to-all(f32[4,24,128]{2,1,0:T(8,128)S(1)} %tile.1), channel_id=1, replica_groups=mesh['dp'=128,'mp'=4] {'mp'}, dimensions={0} | all-to-all | bytes 98304 | tf_op jit(solution)/shard_map/all_to_all | solution.py:452
  56.2 23.6 %all_to_all.26.parts = f32[16,24,128]{2,1,0:T(8,128)S(1)} all-to-all(f32[16,24,128]{2,1,0:T(8,128)S(1)} %add.1), channel_id=1, replica_groups={{0,8,16,24,32,40,48,56,64,72,80,88,96,104,112,120},{4,12,20,28,36,44,52..., dimensions={0} | all-to-all | bytes 393216 | tf_op jit(solution)/shard_map/all_to_all | solution.py:423
  79.8 0.3 panel.1
  80.1 10.9 %all_to_all.27.mine = f32[4,272,128]{2,1,0:T(8,128)S(1)} all-to-all(f32[4,272,128]{2,1,0:T(8,128)S(1)} %panel.1), channel_id=1, replica_groups={{0,128,256,384},{4,132,260,388},{8,136,264,392},{12,140,268,396},{16,14..., dimensions={0} | all-to-all | bytes 1114112 | tf_op jit(solution)/shard_map/all_to_all | solution.py:423
  90.9 9.6 %collective-permute-start.3 = (f32[4,272,128]{2,1,0:T(8,128)S(1)}, f32[4,272,128]{2,1,0:T(8,128)S(1)}, u32[]{:S(2)}, u32[]{:S(2)}) collective-permute-start(f32[4,272,128]{2,1,0:T(8,128)S(1)} %all_to_all.27.mine), channel_id=1, source_target_pairs={{4,0},{0,4},{12,8},{8,12},{20,16},{16,20},{28,24},{24,28},{36,32},... | collective-permute-start | bytes 1671176 | tf_op jit(solution)/shard_map/ppermute | solution.py:433
  100.5 1.6 %collective-permute-done.3.theirs = f32[4,272,128]{2,1,0:T(8,128)S(1)} collective-permute-done((f32[4,272,128]{2,1,0:T(8,128)S(1)}, f32[4,272,128]{2,1,0:T(8,128)S(1)}, u32[]{:S(2)}, u32[]{:S(2)}) %collective-permute-start.3) | collective-permute-done | bytes 557088 | tf_op jit(solution)/shard_map/ppermute | solution.py:433
  102.1 17.0 %solve.1 = f32[4,32]{1,0:T(4,128)} custom-call(s32[1]{0:T(128)} %bitcast.pos, f32[4,272,128]{2,1,0:T(8,128)S(1)} %all_to_all.27.mine, f32[4,272,128]{2,1,0:T(8,128)S(1)} %collective-permute-done.3.theirs), custom_call_target="tpu_custom_call" | custom-call | tf_op jit(solution)/shard_map/solve/pallas_call | solution.py:403
  (5 shorter events, 0.0 us)
Async XLA Ops:
  0.0 14.9 %copy-start = (s32[4]{0:T(128)S(1)}, s32[4]{0:T(128)}, u32[]{:S(2)}) copy-start(s32[4]{0:T(128)} %tlen.1) | copy-start | bytes 52
  4.2 10.7 %all-to-all-start = ((f32[4,160,128]{2,1,0:T(8,128)}), f32[4,160,128]{2,1,0:T(8,128)S(1)}, u32[]{:S(2)}, u32[]{:S(2)}) async-start(f32[4,160,128]{2,1,0:T(8,128)} %project.1), calls=%async_computation | async-start | bytes 655360 | tf_op jit(solution)/shard_map/all_to_all | solution.py:446
  16.6 32.2 %all-to-all-start.1 = ((f32[16,32,128]{2,1,0:T(8,128)}), f32[16,32,128]{2,1,0:T(8,128)S(1)}, u32[]{:S(2)}, u32[]{:S(2)}) async-start(f32[16,32,128]{2,1,0:T(8,128)} %get-tuple-element.7), calls=%async_computation.1 | async-start | bytes 524288 | tf_op jit(solution)/shard_map/all_to_all | solution.py:423
  31.8 5.2 %collective-permute-start = (f32[40,128]{1,0:T(8,128)S(1)}, f32[40,128]{1,0:T(8,128)S(1)}, u32[]{:S(2)}, u32[]{:S(2)}) collective-permute-start(f32[40,128]{1,0:T(8,128)S(1)} %get-tuple-element.8), channel_id=1, source_target_pairs={{4,0},{0,4},{12,8},{8,12},{20,16},{16,20},{28,24},{24,28},{36,32},... | collective-permute-start | bytes 61448 | tf_op jit(solution)/shard_map/ppermute | solution.py:433
  37.0 5.0 %collective-permute-start.1 = (f32[80,128]{1,0:T(8,128)S(1)}, f32[80,128]{1,0:T(8,128)S(1)}, u32[]{:S(2)}, u32[]{:S(2)}) collective-permute-start(f32[80,128]{1,0:T(8,128)S(1)} %pad_maximum_fusion), channel_id=1, source_target_pairs={{128,0},{132,4},{136,8},{140,12},{144,16},{148,20},{152,24},{156,2... | collective-permute-start | bytes 122888 | tf_op jit(solution)/shard_map/ppermute | solution.py:433
  42.1 6.8 %collective-permute-start.2 = (f32[160,128]{1,0:T(8,128)S(1)}, f32[160,128]{1,0:T(8,128)S(1)}, u32[]{:S(2)}, u32[]{:S(2)}) collective-permute-start(f32[160,128]{1,0:T(8,128)S(1)} %constant_dynamic-update-slice_fusion.near), channel_id=1, source_target_pairs={{384,0},{388,4},{392,8},{396,12},{400,16},{404,20},{408,24},{412,2... | collective-permute-start | bytes 245768 | tf_op jit(solution)/shard_map/ppermute | solution.py:433
  90.9 11.2 %collective-permute-start.3 = (f32[4,272,128]{2,1,0:T(8,128)S(1)}, f32[4,272,128]{2,1,0:T(8,128)S(1)}, u32[]{:S(2)}, u32[]{:S(2)}) collective-permute-start(f32[4,272,128]{2,1,0:T(8,128)S(1)} %all_to_all.27.mine), channel_id=1, source_target_pairs={{4,0},{0,4},{12,8},{8,12},{20,16},{16,20},{28,24},{24,28},{36,32},... | collective-permute-start | bytes 1671176 | tf_op jit(solution)/shard_map/ppermute | solution.py:433

commit v6 on v5

--- a/solution.py
+++ b/solution.py
@@ -241,7 +241,7 @@
     return dot(left, right, ca, cb, None)
 
 
-def inverse_factor(tiles):
+def inverse_factor(tiles, hold):
     lane = lanes(8, 128)
     sub = lax.broadcasted_iota(jnp.int32, (8, 128), 0)
     count = len(tiles)
@@ -261,11 +261,12 @@
 
     def panel_of(q):
         block = tiles[q]
+        hold[q, 8] = block
         a = {}
         for c in range(8):
-            whole = column(q, q, c)
+            hold[q, c] = column(q, q, c)
             for p in range(c, 8):
-                a[p, c] = jnp.broadcast_to(whole[p : p + 1, :], (8, 128))
+                a[p, c] = jnp.broadcast_to(hold[q, c, p : p + 1, :], (8, 128))
         mult = {}
         lines, scaled, rows = [], [], []
         for p in range(0, 8, 2):
@@ -280,7 +281,7 @@
                     a[k, c] = a[k, c] - (mult[k, p] * a[c, p] + mult[k, p + 1] * a[c, p + 1])
             for r in (p, p + 1):
                 unit = (lane == 8 * q + r).astype(F32)
-                line = jnp.broadcast_to(block[r : r + 1, :], (8, 128))
+                line = jnp.broadcast_to(hold[q, 8, r : r + 1, :], (8, 128))
                 line = jnp.where(inside(q), unit, line)
                 for k in range(p):
                     line = line - mult[r, k] * lines[k]
@@ -339,7 +340,7 @@
     return tiles
 
 
-def solve_kernel(pos, mine, theirs, out, full, inv, turn):
+def solve_kernel(pos, mine, theirs, out, full, inv, turn, hold):
     d = pos[0]
     y = d // (NZ * NC)
     z = lax.rem(d // NC, NZ)
@@ -376,7 +377,7 @@
     def step(k, carry):
         at = pl.multiple_of(k * 128, 128)
         s = pl.ds(at, 128)
-        tiles = inverse_factor([full[pl.ds(at + 8 * t, 8), s] for t in range(16)])
+        tiles = inverse_factor([full[pl.ds(at + 8 * t, 8), s] for t in range(16)], hold)
         for t in range(16):
             inv[8 * t : 8 * t + 8, :] = tiles[t]
 
@@ -409,6 +410,7 @@
             pltpu.VMEM((512, 640), F32),
             pltpu.VMEM((128, 128), F32),
             pltpu.VMEM((128, 128), F32),
+            pltpu.VMEM((16, 9, 8, 128), F32),
         ],
         compiler_params=params(),
         name="solve",

time: 120 us -> 118 us (0.983)
  Pallas kernels: 23.8 us -> 21.8 us
    pallas_call x1, Pallas kernels: 17 us -> 15 us  [solve(): pl.pallas_call(solve_kernel, out_shape=shape(4, 32), in_specs=[SM] + [VM]...]
where the time goes in v6:
time: 118 us; the launch traced here: 117 us
  starting transfers between devices  41.8 us (35%)
  blocking collectives  41.2 us (35%)
  Pallas kernels  21.8 us (18%)
  waiting for transfers between devices  11.5 us (10%)
    all_to_all x2, blocking collectives, exchange(): lax.all_to_all(value, 'dp', 0, 0, axis_index_groups=groups, tiled=True)  34.4 us
    ppermute x4, starting transfers between devices, swap(): return lax.ppermute(value, 'dp', pairs)  21.8 us
    all_to_all x1, starting transfers between devices, exchange(): lax.all_to_all(value, 'dp', 0, 0, axis_index_groups=groups, tiled=True)  15.2 us
    pallas_call x1, Pallas kernels, solve(): pl.pallas_call(solve_kernel, out_shape=shape(4, 32), in_specs=[SM] + [VM]...  15 us
    all_to_all x1, blocking collectives, shards(): tiles = lax.all_to_all(tile(pos, line, near, away), 'mp', 0, 0, tiled=True)  6.75 us
    ppermute x4, waiting for transfers between devices, swap(): return lax.ppermute(value, 'dp', pairs)  6.29 us
    all_to_all x1, waiting for transfers between devices, shards(): parts = lax.all_to_all(parts, 'mp', 0, 0, tiled=True)  5.23 us
    all_to_all x1, starting transfers between devices, shards(): parts = lax.all_to_all(parts, 'mp', 0, 0, tiled=True)  4.85 us
  transfers between devices with their start and end apart: 6, of which 5 were waited for; matrix products, arithmetic and copies ran while one was open for 0% of the time, Pallas kernels for 0%

profile of v6, /device:TPU:1, one launch (start us, length us, event | category | flops | bytes accessed | tf_op | source)
XLA Modules:
  0.0 117.1 jit_solution(5897401065778169899)
XLA Ops:
  0.0 0.0 copy-start
  0.0 4.2 %project.1 = f32[4,160,128]{2,1,0:T(8,128)} custom-call(bf16[4,64,3584]{2,1,0:T(8,128)(2,1)} %tg.1, bf16[4,64,1024]{2,1,0:T(8,128)(2,1)} %ta.1, bf16[1,64,3584]{2,1,0:T(8,128)(2,1)} %qg.1, bf16[1,64,1024]{2,1,0:T(8,128)(2,1)} %qa.1, bf16[64,3584]{1,0:T(8,128)(2,1)} %of.1, bf16[64,1024]{1,0:T(8,128)(2,1)} %inf.1), custom_call_target="tpu_custom_call" | custom-call | tf_op jit(solution)/shard_map/project/pallas_call | solution.py:84
  4.2 4.9 %all-to-all-start = ((f32[4,160,128]{2,1,0:T(8,128)}), f32[4,160,128]{2,1,0:T(8,128)S(1)}, u32[]{:S(2)}, u32[]{:S(2)}) async-start(f32[4,160,128]{2,1,0:T(8,128)} %project.1), calls=%async_computation | async-start | bytes 655360 | tf_op jit(solution)/shard_map/all_to_all | solution.py:448
  9.7 5.2 %all-to-all-done.parts = f32[4,160,128]{2,1,0:T(8,128)S(1)} async-done(((f32[4,160,128]{2,1,0:T(8,128)}), f32[4,160,128]{2,1,0:T(8,128)S(1)}, u32[]{:S(2)}, u32[]{:S(2)}) %all-to-all-start) | async-done | bytes 327712 | tf_op jit(solution)/shard_map/all_to_all | solution.py:448
  14.9 0.0 copy-done
  14.9 1.7 %sketch.1 = (f32[16,32,128]{2,1,0:T(8,128)}, f32[40,128]{1,0:T(8,128)S(1)}) custom-call(s32[4]{0:T(128)S(1)} %copy-done, s32[1]{0:T(128)S(6)} %copy.11.qlen, f32[4,160,128]{2,1,0:T(8,128)S(1)} %all-to-all-done.parts), custom_call_target="tpu_custom_call" | custom-call | tf_op jit(solution)/shard_map/sketch/pallas_call | solution.py:140
  16.6 15.2 %all-to-all-start.1 = ((f32[16,32,128]{2,1,0:T(8,128)}), f32[16,32,128]{2,1,0:T(8,128)S(1)}, u32[]{:S(2)}, u32[]{:S(2)}) async-start(f32[16,32,128]{2,1,0:T(8,128)} %get-tuple-element.7), calls=%async_computation.1 | async-start | bytes 524288 | tf_op jit(solution)/shard_map/all_to_all | solution.py:425
  31.8 4.3 %collective-permute-start = (f32[40,128]{1,0:T(8,128)S(1)}, f32[40,128]{1,0:T(8,128)S(1)}, u32[]{:S(2)}, u32[]{:S(2)}) collective-permute-start(f32[40,128]{1,0:T(8,128)S(1)} %get-tuple-element.8), channel_id=1, source_target_pairs={{4,0},{0,4},{12,8},{8,12},{20,16},{16,20},{28,24},{24,28},{36,32},... | collective-permute-start | bytes 61448 | tf_op jit(solution)/shard_map/ppermute | solution.py:435
  36.2 0.8 collective-permute-done
  37.0 3.2 %collective-permute-start.1 = (f32[80,128]{1,0:T(8,128)S(1)}, f32[80,128]{1,0:T(8,128)S(1)}, u32[]{:S(2)}, u32[]{:S(2)}) collective-permute-start(f32[80,128]{1,0:T(8,128)S(1)} %pad_maximum_fusion), channel_id=1, source_target_pairs={{128,0},{132,4},{136,8},{140,12},{144,16},{148,20},{152,24},{156,2... | collective-permute-start | bytes 122888 | tf_op jit(solution)/shard_map/ppermute | solution.py:435
  40.2 1.8 %collective-permute-done.1 = f32[80,128]{1,0:T(8,128)S(1)} collective-permute-done((f32[80,128]{1,0:T(8,128)S(1)}, f32[80,128]{1,0:T(8,128)S(1)}, u32[]{:S(2)}, u32[]{:S(2)}) %collective-permute-start.1) | collective-permute-done | bytes 40992 | tf_op jit(solution)/shard_map/ppermute | solution.py:435
  42.1 4.6 %collective-permute-start.2 = (f32[160,128]{1,0:T(8,128)S(1)}, f32[160,128]{1,0:T(8,128)S(1)}, u32[]{:S(2)}, u32[]{:S(2)}) collective-permute-start(f32[160,128]{1,0:T(8,128)S(1)} %constant_dynamic-update-slice_fusion.near), channel_id=1, source_target_pairs={{384,0},{388,4},{392,8},{396,12},{400,16},{404,20},{408,24},{412,2... | collective-permute-start | bytes 245768 | tf_op jit(solution)/shard_map/ppermute | solution.py:435
  46.7 2.1 %collective-permute-done.2.away = f32[160,128]{1,0:T(8,128)S(1)} collective-permute-done((f32[160,128]{1,0:T(8,128)S(1)}, f32[160,128]{1,0:T(8,128)S(1)}, u32[]{:S(2)}, u32[]{:S(2)}) %collective-permute-start.2) | collective-permute-done | bytes 81952 | tf_op jit(solution)/shard_map/ppermute | solution.py:435
  48.8 0.0 all-to-all-done.1
  48.8 0.7 tile.1
  49.5 6.7 %all_to_all.25.parts = f32[4,24,128]{2,1,0:T(8,128)S(1)} all-to-all(f32[4,24,128]{2,1,0:T(8,128)S(1)} %tile.1), channel_id=1, replica_groups=mesh['dp'=128,'mp'=4] {'mp'}, dimensions={0} | all-to-all | bytes 98304 | tf_op jit(solution)/shard_map/all_to_all | solution.py:454
  56.2 23.6 %all_to_all.26.parts = f32[16,24,128]{2,1,0:T(8,128)S(1)} all-to-all(f32[16,24,128]{2,1,0:T(8,128)S(1)} %add.1), channel_id=1, replica_groups={{0,8,16,24,32,40,48,56,64,72,80,88,96,104,112,120},{4,12,20,28,36,44,52..., dimensions={0} | all-to-all | bytes 393216 | tf_op jit(solution)/shard_map/all_to_all | solution.py:425
  79.8 0.3 panel.1
  80.1 10.9 %all_to_all.27.mine = f32[4,272,128]{2,1,0:T(8,128)S(1)} all-to-all(f32[4,272,128]{2,1,0:T(8,128)S(1)} %panel.1), channel_id=1, replica_groups={{0,128,256,384},{4,132,260,388},{8,136,264,392},{12,140,268,396},{16,14..., dimensions={0} | all-to-all | bytes 1114112 | tf_op jit(solution)/shard_map/all_to_all | solution.py:425
  90.9 9.6 %collective-permute-start.3 = (f32[4,272,128]{2,1,0:T(8,128)S(1)}, f32[4,272,128]{2,1,0:T(8,128)S(1)}, u32[]{:S(2)}, u32[]{:S(2)}) collective-permute-start(f32[4,272,128]{2,1,0:T(8,128)S(1)} %all_to_all.27.mine), channel_id=1, source_target_pairs={{4,0},{0,4},{12,8},{8,12},{20,16},{16,20},{28,24},{24,28},{36,32},... | collective-permute-start | bytes 1671176 | tf_op jit(solution)/shard_map/ppermute | solution.py:435
  100.5 1.6 %collective-permute-done.3.theirs = f32[4,272,128]{2,1,0:T(8,128)S(1)} collective-permute-done((f32[4,272,128]{2,1,0:T(8,128)S(1)}, f32[4,272,128]{2,1,0:T(8,128)S(1)}, u32[]{:S(2)}, u32[]{:S(2)}) %collective-permute-start.3) | collective-permute-done | bytes 557088 | tf_op jit(solution)/shard_map/ppermute | solution.py:435
  102.1 15.0 %solve.1 = f32[4,32]{1,0:T(4,128)} custom-call(s32[1]{0:T(128)} %bitcast.pos, f32[4,272,128]{2,1,0:T(8,128)S(1)} %all_to_all.27.mine, f32[4,272,128]{2,1,0:T(8,128)S(1)} %collective-permute-done.3.theirs), custom_call_target="tpu_custom_call" | custom-call | tf_op jit(solution)/shard_map/solve/pallas_call | solution.py:404
  (5 shorter events, 0.0 us)
Async XLA Ops:
  0.0 14.9 %copy-start = (s32[4]{0:T(128)S(1)}, s32[4]{0:T(128)}, u32[]{:S(2)}) copy-start(s32[4]{0:T(128)} %tlen.1) | copy-start | bytes 52
  4.2 10.7 %all-to-all-start = ((f32[4,160,128]{2,1,0:T(8,128)}), f32[4,160,128]{2,1,0:T(8,128)S(1)}, u32[]{:S(2)}, u32[]{:S(2)}) async-start(f32[4,160,128]{2,1,0:T(8,128)} %project.1), calls=%async_computation | async-start | bytes 655360 | tf_op jit(solution)/shard_map/all_to_all | solution.py:448
  16.6 32.2 %all-to-all-start.1 = ((f32[16,32,128]{2,1,0:T(8,128)}), f32[16,32,128]{2,1,0:T(8,128)S(1)}, u32[]{:S(2)}, u32[]{:S(2)}) async-start(f32[16,32,128]{2,1,0:T(8,128)} %get-tuple-element.7), calls=%async_computation.1 | async-start | bytes 524288 | tf_op jit(solution)/shard_map/all_to_all | solution.py:425
  31.8 5.2 %collective-permute-start = (f32[40,128]{1,0:T(8,128)S(1)}, f32[40,128]{1,0:T(8,128)S(1)}, u32[]{:S(2)}, u32[]{:S(2)}) collective-permute-start(f32[40,128]{1,0:T(8,128)S(1)} %get-tuple-element.8), channel_id=1, source_target_pairs={{4,0},{0,4},{12,8},{8,12},{20,16},{16,20},{28,24},{24,28},{36,32},... | collective-permute-start | bytes 61448 | tf_op jit(solution)/shard_map/ppermute | solution.py:435
  37.0 5.0 %collective-permute-start.1 = (f32[80,128]{1,0:T(8,128)S(1)}, f32[80,128]{1,0:T(8,128)S(1)}, u32[]{:S(2)}, u32[]{:S(2)}) collective-permute-start(f32[80,128]{1,0:T(8,128)S(1)} %pad_maximum_fusion), channel_id=1, source_target_pairs={{128,0},{132,4},{136,8},{140,12},{144,16},{148,20},{152,24},{156,2... | collective-permute-start | bytes 122888 | tf_op jit(solution)/shard_map/ppermute | solution.py:435
  42.1 6.8 %collective-permute-start.2 = (f32[160,128]{1,0:T(8,128)S(1)}, f32[160,128]{1,0:T(8,128)S(1)}, u32[]{:S(2)}, u32[]{:S(2)}) collective-permute-start(f32[160,128]{1,0:T(8,128)S(1)} %constant_dynamic-update-slice_fusion.near), channel_id=1, source_target_pairs={{384,0},{388,4},{392,8},{396,12},{400,16},{404,20},{408,24},{412,2... | collective-permute-start | bytes 245768 | tf_op jit(solution)/shard_map/ppermute | solution.py:435
  90.9 11.2 %collective-permute-start.3 = (f32[4,272,128]{2,1,0:T(8,128)S(1)}, f32[4,272,128]{2,1,0:T(8,128)S(1)}, u32[]{:S(2)}, u32[]{:S(2)}) collective-permute-start(f32[4,272,128]{2,1,0:T(8,128)S(1)} %all_to_all.27.mine), channel_id=1, source_target_pairs={{4,0},{0,4},{12,8},{8,12},{20,16},{16,20},{28,24},{24,28},{36,32},... | collective-permute-start | bytes 1671176 | tf_op jit(solution)/shard_map/ppermute | solution.py:435

commit v7 on v6

--- a/solution.py
+++ b/solution.py
@@ -37,7 +37,7 @@
 CHUNKS = 4
 
 
-def project_kernel(tg, ta, qg, qa, of, inf, out, g, a, fo, fi, acc, sem):
+def project_kernel(tg, ta, qg, qa, of, inf, out, g, a, fo, fi, acc, packed, sem):
     copies = []
 
     def start(src, dst):
@@ -69,14 +69,16 @@
         copies[7 + 2 * j].wait()
         s = slice(j * width, (j + 1) * width)
         acc[...] += dot(g[:, :, s].reshape(320, width), fo[:, s], 1, 1, None)
-    for low, high, to, n in ((0, 128, 0, 128), (256, 288, 128, 32)):
-        left = lanes(n, 128) < 64
-        first = acc[low : low + n, :]
-        second = acc[high : high + n, :]
-        for p in range(4):
-            one = pltpu.roll(first, (128 - 32 * p) % 128, 1) if p else first
-            two = pltpu.roll(second, (64 - 32 * p) % 128, 1) if p != 2 else second
-            out[p, to : to + n, :] = jnp.where(left, one, two)
+    for p in range(4):
+        for low, high, to, n in ((0, 128, 0, 128), (256, 288, 128, 32)):
+            one = acc[low : low + n, :]
+            two = acc[high : high + n, :]
+            one = pltpu.roll(one, (128 - 32 * p) % 128, 1) if p else one
+            two = pltpu.roll(two, (64 - 32 * p) % 128, 1) if p != 2 else two
+            packed[p, to : to + n, :] = jnp.where(lanes(n, 128) < 64, one, two)
+        start(packed.at[p], out.at[p])
+    for copy in copies[6 + 2 * CHUNKS :]:
+        copy.wait()
 
 
 def project(tg, ta, qg, qa, of, inf):
@@ -85,21 +87,22 @@
         project_kernel,
         out_shape=shape(4, 160, 128),
         in_specs=[ANY] * 6,
-        out_specs=VM,
+        out_specs=ANY,
         scratch_shapes=[
             pltpu.VMEM((5, 64, kg), jnp.bfloat16),
             pltpu.VMEM((5, 64, ka), jnp.bfloat16),
             pltpu.VMEM((128, kg), jnp.bfloat16),
             pltpu.VMEM((128, ka), jnp.bfloat16),
             pltpu.VMEM((320, 128), F32),
-            pltpu.SemaphoreType.DMA((6 + 2 * CHUNKS,)),
+            pltpu.VMEM((4, 160, 128), F32),
+            pltpu.SemaphoreType.DMA((10 + 2 * CHUNKS,)),
         ],
         compiler_params=params(56 * MB),
         name="project",
     )(tg, ta, qg, qa, of, inf)
 
 
-def sketch_kernel(tlen, qlen, parts, zcopies, own, square):
+def sketch_kernel(tlen, qlen, parts, zcopies, own, square, trains, sem):
     lane = lanes(8, 128)
 
     def fold(row, col):
@@ -113,10 +116,9 @@
         return total
 
     def emit(e, tile):
-        for t in range(NZ):
-            if e < 4:
-                zcopies[t, 8 * e : 8 * e + 8, :] = tile
         own[8 * e : 8 * e + 8, :] = tile
+        if e < 4:
+            trains[8 * e : 8 * e + 8, :] = tile
 
     def outer(low, n, weight):
         s = slice(low, low + n)
@@ -131,9 +133,16 @@
         outer(64 * e, 64, weight)
         emit(e, fold(0, 32))
         emit(e + 2, fold(64, 96))
+    copies = [
+        pltpu.make_async_copy(trains, zcopies.at[t], sem.at[t]) for t in range(NZ)
+    ]
+    for copy in copies:
+        copy.start()
     token = token[0:32] + jnp.where(left[0:32], 0, 32)
     outer(128, 32, (token < qlen[0]).astype(F32))
     emit(4, fold(0, 32) + fold(64, 96))
+    for copy in copies:
+        copy.wait()
 
 
 def sketch(tlen, qlen, parts):
@@ -141,8 +150,12 @@
         sketch_kernel,
         out_shape=(shape(NZ, 32, 128), shape(40, 128)),
         in_specs=[SM] * 2 + [VM],
-        out_specs=(VM, VM),
-        scratch_shapes=[pltpu.VMEM((128, 128), F32)],
+        out_specs=(ANY, VM),
+        scratch_shapes=[
+            pltpu.VMEM((128, 128), F32),
+            pltpu.VMEM((32, 128), F32),
+            pltpu.SemaphoreType.DMA((NZ,)),
+        ],
         compiler_params=params(),
         name="sketch",
     )(tlen, qlen, parts)
@@ -397,7 +410,9 @@
 
     lax.fori_loop(0, 4, step, 0)
     right = full[:, 512:640]
-    out[...] = stacked(right.T[32:40, :], right, 1, 0)[0:4, 0:32]
+    for i in range(4):
+        one = jnp.sum(right * right[:, 32 + i : 33 + i], axis=0, keepdims=True)
+        out[i : i + 1, :] = one[:, 0:32]
 
 
 def solve(pos, mine, theirs):

time: 118 us -> 118 us (level)
  no operation moved by 1% of the time
where the time goes in v7:
time: 118 us; the launch traced here: 117 us
  starting transfers between devices  41.8 us (35%)
  blocking collectives  41.2 us (35%)
  Pallas kernels  22 us (19%)
  waiting for transfers between devices  11.5 us (10%)
    all_to_all x2, blocking collectives, exchange(): lax.all_to_all(value, 'dp', 0, 0, axis_index_groups=groups, tiled=True)  34.4 us
    ppermute x4, starting transfers between devices, swap(): return lax.ppermute(value, 'dp', pairs)  21.8 us
    all_to_all x1, starting transfers between devices, exchange(): lax.all_to_all(value, 'dp', 0, 0, axis_index_groups=groups, tiled=True)  15.2 us
    pallas_call x1, Pallas kernels, solve(): pl.pallas_call(solve_kernel, out_shape=shape(4, 32), in_specs=[SM] + [VM]...  15.1 us
    all_to_all x1, blocking collectives, shards(): tiles = lax.all_to_all(tile(pos, line, near, away), 'mp', 0, 0, tiled=True)  6.75 us
    ppermute x4, waiting for transfers between devices, swap(): return lax.ppermute(value, 'dp', pairs)  6.29 us
    all_to_all x1, waiting for transfers between devices, shards(): parts = lax.all_to_all(parts, 'mp', 0, 0, tiled=True)  5.23 us
    all_to_all x1, starting transfers between devices, shards(): parts = lax.all_to_all(parts, 'mp', 0, 0, tiled=True)  4.85 us
  transfers between devices with their start and end apart: 6, of which 5 were waited for; matrix products, arithmetic and copies ran while one was open for 0% of the time, Pallas kernels for 0%

profile of v7, /device:TPU:1, one launch (start us, length us, event | category | flops | bytes accessed | tf_op | source)
XLA Modules:
  0.0 117.3 jit_solution(10571097535469137845)
XLA Ops:
  0.0 0.0 copy-start
  0.0 4.2 %project.1 = f32[4,160,128]{2,1,0:T(8,128)} custom-call(bf16[4,64,3584]{2,1,0:T(8,128)(2,1)} %tg.1, bf16[4,64,1024]{2,1,0:T(8,128)(2,1)} %ta.1, bf16[1,64,3584]{2,1,0:T(8,128)(2,1)} %qg.1, bf16[1,64,1024]{2,1,0:T(8,128)(2,1)} %qa.1, bf16[64,3584]{1,0:T(8,128)(2,1)} %of.1, bf16[64,1024]{1,0:T(8,128)(2,1)} %inf.1), custom_call_target="tpu_custom_call" | custom-call | tf_op jit(solution)/shard_map/project/pallas_call | solution.py:86
  4.2 4.9 %all-to-all-start = ((f32[4,160,128]{2,1,0:T(8,128)}), f32[4,160,128]{2,1,0:T(8,128)S(1)}, u32[]{:S(2)}, u32[]{:S(2)}) async-start(f32[4,160,128]{2,1,0:T(8,128)} %project.1), calls=%async_computation | async-start | bytes 655360 | tf_op jit(solution)/shard_map/all_to_all | solution.py:463
  9.7 5.2 %all-to-all-done.parts = f32[4,160,128]{2,1,0:T(8,128)S(1)} async-done(((f32[4,160,128]{2,1,0:T(8,128)}), f32[4,160,128]{2,1,0:T(8,128)S(1)}, u32[]{:S(2)}, u32[]{:S(2)}) %all-to-all-start) | async-done | bytes 327712 | tf_op jit(solution)/shard_map/all_to_all | solution.py:463
  15.0 0.0 copy-done
  15.0 1.8 %sketch.1 = (f32[16,32,128]{2,1,0:T(8,128)}, f32[40,128]{1,0:T(8,128)S(1)}) custom-call(s32[4]{0:T(128)S(1)} %copy-done, s32[1]{0:T(128)S(6)} %copy.11.qlen, f32[4,160,128]{2,1,0:T(8,128)S(1)} %all-to-all-done.parts), custom_call_target="tpu_custom_call" | custom-call | tf_op jit(solution)/shard_map/sketch/pallas_call | solution.py:149
  16.8 15.2 %all-to-all-start.1 = ((f32[16,32,128]{2,1,0:T(8,128)}), f32[16,32,128]{2,1,0:T(8,128)S(1)}, u32[]{:S(2)}, u32[]{:S(2)}) async-start(f32[16,32,128]{2,1,0:T(8,128)} %get-tuple-element.7), calls=%async_computation.1 | async-start | bytes 524288 | tf_op jit(solution)/shard_map/all_to_all | solution.py:440
  32.0 4.3 %collective-permute-start = (f32[40,128]{1,0:T(8,128)S(1)}, f32[40,128]{1,0:T(8,128)S(1)}, u32[]{:S(2)}, u32[]{:S(2)}) collective-permute-start(f32[40,128]{1,0:T(8,128)S(1)} %get-tuple-element.8), channel_id=1, source_target_pairs={{4,0},{0,4},{12,8},{8,12},{20,16},{16,20},{28,24},{24,28},{36,32},... | collective-permute-start | bytes 61448 | tf_op jit(solution)/shard_map/ppermute | solution.py:450
  36.4 0.8 collective-permute-done
  37.2 3.2 %collective-permute-start.1 = (f32[80,128]{1,0:T(8,128)S(1)}, f32[80,128]{1,0:T(8,128)S(1)}, u32[]{:S(2)}, u32[]{:S(2)}) collective-permute-start(f32[80,128]{1,0:T(8,128)S(1)} %pad_maximum_fusion), channel_id=1, source_target_pairs={{128,0},{132,4},{136,8},{140,12},{144,16},{148,20},{152,24},{156,2... | collective-permute-start | bytes 122888 | tf_op jit(solution)/shard_map/ppermute | solution.py:450
  40.4 1.8 %collective-permute-done.1 = f32[80,128]{1,0:T(8,128)S(1)} collective-permute-done((f32[80,128]{1,0:T(8,128)S(1)}, f32[80,128]{1,0:T(8,128)S(1)}, u32[]{:S(2)}, u32[]{:S(2)}) %collective-permute-start.1) | collective-permute-done | bytes 40992 | tf_op jit(solution)/shard_map/ppermute | solution.py:450
  42.2 4.6 %collective-permute-start.2 = (f32[160,128]{1,0:T(8,128)S(1)}, f32[160,128]{1,0:T(8,128)S(1)}, u32[]{:S(2)}, u32[]{:S(2)}) collective-permute-start(f32[160,128]{1,0:T(8,128)S(1)} %constant_dynamic-update-slice_fusion.near), channel_id=1, source_target_pairs={{384,0},{388,4},{392,8},{396,12},{400,16},{404,20},{408,24},{412,2... | collective-permute-start | bytes 245768 | tf_op jit(solution)/shard_map/ppermute | solution.py:450
  46.9 2.1 %collective-permute-done.2.away = f32[160,128]{1,0:T(8,128)S(1)} collective-permute-done((f32[160,128]{1,0:T(8,128)S(1)}, f32[160,128]{1,0:T(8,128)S(1)}, u32[]{:S(2)}, u32[]{:S(2)}) %collective-permute-start.2) | collective-permute-done | bytes 81952 | tf_op jit(solution)/shard_map/ppermute | solution.py:450
  49.0 0.0 all-to-all-done.1
  49.0 0.7 tile.1
  49.7 6.7 %all_to_all.25.parts = f32[4,24,128]{2,1,0:T(8,128)S(1)} all-to-all(f32[4,24,128]{2,1,0:T(8,128)S(1)} %tile.1), channel_id=1, replica_groups=mesh['dp'=128,'mp'=4] {'mp'}, dimensions={0} | all-to-all | bytes 98304 | tf_op jit(solution)/shard_map/all_to_all | solution.py:469
  56.4 23.6 %all_to_all.26.parts = f32[16,24,128]{2,1,0:T(8,128)S(1)} all-to-all(f32[16,24,128]{2,1,0:T(8,128)S(1)} %add.1), channel_id=1, replica_groups={{0,8,16,24,32,40,48,56,64,72,80,88,96,104,112,120},{4,12,20,28,36,44,52..., dimensions={0} | all-to-all | bytes 393216 | tf_op jit(solution)/shard_map/all_to_all | solution.py:440
  80.0 0.3 panel.1
  80.3 10.8 %all_to_all.27.mine = f32[4,272,128]{2,1,0:T(8,128)S(1)} all-to-all(f32[4,272,128]{2,1,0:T(8,128)S(1)} %panel.1), channel_id=1, replica_groups={{0,128,256,384},{4,132,260,388},{8,136,264,392},{12,140,268,396},{16,14..., dimensions={0} | all-to-all | bytes 1114112 | tf_op jit(solution)/shard_map/all_to_all | solution.py:440
  91.1 9.6 %collective-permute-start.3 = (f32[4,272,128]{2,1,0:T(8,128)S(1)}, f32[4,272,128]{2,1,0:T(8,128)S(1)}, u32[]{:S(2)}, u32[]{:S(2)}) collective-permute-start(f32[4,272,128]{2,1,0:T(8,128)S(1)} %all_to_all.27.mine), channel_id=1, source_target_pairs={{4,0},{0,4},{12,8},{8,12},{20,16},{16,20},{28,24},{24,28},{36,32},... | collective-permute-start | bytes 1671176 | tf_op jit(solution)/shard_map/ppermute | solution.py:450
  100.7 1.6 %collective-permute-done.3.theirs = f32[4,272,128]{2,1,0:T(8,128)S(1)} collective-permute-done((f32[4,272,128]{2,1,0:T(8,128)S(1)}, f32[4,272,128]{2,1,0:T(8,128)S(1)}, u32[]{:S(2)}, u32[]{:S(2)}) %collective-permute-start.3) | collective-permute-done | bytes 557088 | tf_op jit(solution)/shard_map/ppermute | solution.py:450
  102.3 15.1 %solve.1 = f32[4,32]{1,0:T(4,128)} custom-call(s32[1]{0:T(128)} %bitcast.pos, f32[4,272,128]{2,1,0:T(8,128)S(1)} %all_to_all.27.mine, f32[4,272,128]{2,1,0:T(8,128)S(1)} %collective-permute-done.3.theirs), custom_call_target="tpu_custom_call" | custom-call | tf_op jit(solution)/shard_map/solve/pallas_call | solution.py:419
  (5 shorter events, 0.0 us)
Async XLA Ops:
  0.0 15.0 %copy-start = (s32[4]{0:T(128)S(1)}, s32[4]{0:T(128)}, u32[]{:S(2)}) copy-start(s32[4]{0:T(128)} %tlen.1) | copy-start | bytes 52
  4.2 10.7 %all-to-all-start = ((f32[4,160,128]{2,1,0:T(8,128)}), f32[4,160,128]{2,1,0:T(8,128)S(1)}, u32[]{:S(2)}, u32[]{:S(2)}) async-start(f32[4,160,128]{2,1,0:T(8,128)} %project.1), calls=%async_computation | async-start | bytes 655360 | tf_op jit(solution)/shard_map/all_to_all | solution.py:463
  16.8 32.2 %all-to-all-start.1 = ((f32[16,32,128]{2,1,0:T(8,128)}), f32[16,32,128]{2,1,0:T(8,128)S(1)}, u32[]{:S(2)}, u32[]{:S(2)}) async-start(f32[16,32,128]{2,1,0:T(8,128)} %get-tuple-element.7), calls=%async_computation.1 | async-start | bytes 524288 | tf_op jit(solution)/shard_map/all_to_all | solution.py:440
  32.0 5.2 %collective-permute-start = (f32[40,128]{1,0:T(8,128)S(1)}, f32[40,128]{1,0:T(8,128)S(1)}, u32[]{:S(2)}, u32[]{:S(2)}) collective-permute-start(f32[40,128]{1,0:T(8,128)S(1)} %get-tuple-element.8), channel_id=1, source_target_pairs={{4,0},{0,4},{12,8},{8,12},{20,16},{16,20},{28,24},{24,28},{36,32},... | collective-permute-start | bytes 61448 | tf_op jit(solution)/shard_map/ppermute | solution.py:450
  37.2 5.0 %collective-permute-start.1 = (f32[80,128]{1,0:T(8,128)S(1)}, f32[80,128]{1,0:T(8,128)S(1)}, u32[]{:S(2)}, u32[]{:S(2)}) collective-permute-start(f32[80,128]{1,0:T(8,128)S(1)} %pad_maximum_fusion), channel_id=1, source_target_pairs={{128,0},{132,4},{136,8},{140,12},{144,16},{148,20},{152,24},{156,2... | collective-permute-start | bytes 122888 | tf_op jit(solution)/shard_map/ppermute | solution.py:450
  42.2 6.8 %collective-permute-start.2 = (f32[160,128]{1,0:T(8,128)S(1)}, f32[160,128]{1,0:T(8,128)S(1)}, u32[]{:S(2)}, u32[]{:S(2)}) collective-permute-start(f32[160,128]{1,0:T(8,128)S(1)} %constant_dynamic-update-slice_fusion.near), channel_id=1, source_target_pairs={{384,0},{388,4},{392,8},{396,12},{400,16},{404,20},{408,24},{412,2... | collective-permute-start | bytes 245768 | tf_op jit(solution)/shard_map/ppermute | solution.py:450
  91.1 11.2 %collective-permute-start.3 = (f32[4,272,128]{2,1,0:T(8,128)S(1)}, f32[4,272,128]{2,1,0:T(8,128)S(1)}, u32[]{:S(2)}, u32[]{:S(2)}) collective-permute-start(f32[4,272,128]{2,1,0:T(8,128)S(1)} %all_to_all.27.mine), channel_id=1, source_target_pairs={{4,0},{0,4},{12,8},{8,12},{20,16},{16,20},{28,24},{24,28},{36,32},... | collective-permute-start | bytes 1671176 | tf_op jit(solution)/shard_map/ppermute | solution.py:450

commit v8 on v6

--- a/solution.py
+++ b/solution.py
@@ -99,7 +99,7 @@
     )(tg, ta, qg, qa, of, inf)
 
 
-def sketch_kernel(tlen, qlen, parts, zcopies, own, square):
+def sketch_kernel(tlen, qlen, parts, own, square):
     lane = lanes(8, 128)
 
     def fold(row, col):
@@ -113,9 +113,6 @@
         return total
 
     def emit(e, tile):
-        for t in range(NZ):
-            if e < 4:
-                zcopies[t, 8 * e : 8 * e + 8, :] = tile
         own[8 * e : 8 * e + 8, :] = tile
 
     def outer(low, n, weight):
@@ -139,9 +136,9 @@
 def sketch(tlen, qlen, parts):
     return pl.pallas_call(
         sketch_kernel,
-        out_shape=(shape(NZ, 32, 128), shape(40, 128)),
+        out_shape=shape(40, 128),
         in_specs=[SM] * 2 + [VM],
-        out_specs=(VM, VM),
+        out_specs=VM,
         scratch_shapes=[pltpu.VMEM((128, 128), F32)],
         compiler_params=params(),
         name="sketch",
@@ -446,7 +443,8 @@
     pos = lax.axis_index("dp").astype(jnp.int32).reshape(1)
     parts = project(tg, ta, qg, qa, of, inf)
     parts = lax.all_to_all(parts, "mp", 0, 0, tiled=True)
-    zcopies, own = sketch(tlen, qlen, parts)
+    own = sketch(tlen, qlen, parts)
+    zcopies = jnp.broadcast_to(own[None, :32], (NZ, 32, 128))
     pair = jnp.concatenate([own, swap(own, other_core)], axis=0)
     line = exchange(zcopies, line_groups).reshape(NZ * 32, 128)
     near = jnp.concatenate([pair, swap(pair, lambda y, z, c: (y ^ 1, z, c))], axis=0)

time: 118 us -> 118 us (level)
  no operation moved by 1% of the time
where the time goes in v8:
time: 118 us; the launch traced here: 117 us
  starting transfers between devices  41.8 us (35%)
  blocking collectives  41.2 us (35%)
  Pallas kernels  21.2 us (18%)
  waiting for transfers between devices  11.5 us (10%)
    all_to_all x2, blocking collectives, exchange(): lax.all_to_all(value, 'dp', 0, 0, axis_index_groups=groups, tiled=True)  34.4 us
    ppermute x4, starting transfers between devices, swap(): return lax.ppermute(value, 'dp', pairs)  21.8 us
    all_to_all x1, starting transfers between devices, exchange(): lax.all_to_all(value, 'dp', 0, 0, axis_index_groups=groups, tiled=True)  15.2 us
    pallas_call x1, Pallas kernels, solve(): pl.pallas_call(solve_kernel, out_shape=shape(4, 32), in_specs=[SM] + [VM]...  15.1 us
    all_to_all x1, blocking collectives, shards(): tiles = lax.all_to_all(tile(pos, line, near, away), 'mp', 0, 0, tiled=True)  6.75 us
    ppermute x4, waiting for transfers between devices, swap(): return lax.ppermute(value, 'dp', pairs)  6.32 us
    all_to_all x1, waiting for transfers between devices, shards(): parts = lax.all_to_all(parts, 'mp', 0, 0, tiled=True)  5.23 us
    all_to_all x1, starting transfers between devices, shards(): parts = lax.all_to_all(parts, 'mp', 0, 0, tiled=True)  4.85 us
  transfers between devices with their start and end apart: 6, of which 5 were waited for; matrix products, arithmetic and copies ran while one was open for 0% of the time, Pallas kernels for 0%

profile of v8, /device:TPU:1, one launch (start us, length us, event | category | flops | bytes accessed | tf_op | source)
XLA Modules:
  0.0 117.2 jit_solution(12808822494765825740)
XLA Ops:
  0.0 0.0 copy-start
  0.0 4.2 %project.1 = f32[4,160,128]{2,1,0:T(8,128)} custom-call(bf16[4,64,3584]{2,1,0:T(8,128)(2,1)} %tg.1, bf16[4,64,1024]{2,1,0:T(8,128)(2,1)} %ta.1, bf16[1,64,3584]{2,1,0:T(8,128)(2,1)} %qg.1, bf16[1,64,1024]{2,1,0:T(8,128)(2,1)} %qa.1, bf16[64,3584]{1,0:T(8,128)(2,1)} %of.1, bf16[64,1024]{1,0:T(8,128)(2,1)} %inf.1), custom_call_target="tpu_custom_call" | custom-call | tf_op jit(solution)/shard_map/project/pallas_call | solution.py:84
  4.2 4.9 %all-to-all-start = ((f32[4,160,128]{2,1,0:T(8,128)}), f32[4,160,128]{2,1,0:T(8,128)S(1)}, u32[]{:S(2)}, u32[]{:S(2)}) async-start(f32[4,160,128]{2,1,0:T(8,128)} %project.1), calls=%async_computation | async-start | bytes 655360 | tf_op jit(solution)/shard_map/all_to_all | solution.py:445
  9.7 5.2 %all-to-all-done.parts = f32[4,160,128]{2,1,0:T(8,128)S(1)} async-done(((f32[4,160,128]{2,1,0:T(8,128)}), f32[4,160,128]{2,1,0:T(8,128)S(1)}, u32[]{:S(2)}, u32[]{:S(2)}) %all-to-all-start) | async-done | bytes 327712 | tf_op jit(solution)/shard_map/all_to_all | solution.py:445
  14.9 0.0 copy-done
  14.9 1.0 sketch.1
  15.9 0.7 broadcast_in_dim.2
  16.7 15.2 %all-to-all-start.1 = ((f32[16,32,128]{2,1,0:T(8,128)}), f32[16,32,128]{2,1,0:T(8,128)S(1)}, u32[]{:S(2)}, u32[]{:S(2)}) async-start(f32[16,32,128]{2,1,0:T(8,128)} %broadcast_in_dim.2), calls=%async_computation.1 | async-start | bytes 524288 | tf_op jit(solution)/shard_map/all_to_all | solution.py:422
  31.9 4.3 %collective-permute-start = (f32[40,128]{1,0:T(8,128)S(1)}, f32[40,128]{1,0:T(8,128)S(1)}, u32[]{:S(2)}, u32[]{:S(2)}) collective-permute-start(f32[40,128]{1,0:T(8,128)S(1)} %sketch.1), channel_id=1, source_target_pairs={{4,0},{0,4},{12,8},{8,12},{20,16},{16,20},{28,24},{24,28},{36,32},... | collective-permute-start | bytes 61448 | tf_op jit(solution)/shard_map/ppermute | solution.py:432
  36.2 0.8 collective-permute-done
  37.0 3.2 %collective-permute-start.1 = (f32[80,128]{1,0:T(8,128)S(1)}, f32[80,128]{1,0:T(8,128)S(1)}, u32[]{:S(2)}, u32[]{:S(2)}) collective-permute-start(f32[80,128]{1,0:T(8,128)S(1)} %pad_maximum_fusion.1), channel_id=1, source_target_pairs={{128,0},{132,4},{136,8},{140,12},{144,16},{148,20},{152,24},{156,2... | collective-permute-start | bytes 122888 | tf_op jit(solution)/shard_map/ppermute | solution.py:432
  40.3 1.8 %collective-permute-done.1 = f32[80,128]{1,0:T(8,128)S(1)} collective-permute-done((f32[80,128]{1,0:T(8,128)S(1)}, f32[80,128]{1,0:T(8,128)S(1)}, u32[]{:S(2)}, u32[]{:S(2)}) %collective-permute-start.1) | collective-permute-done | bytes 40992 | tf_op jit(solution)/shard_map/ppermute | solution.py:432
  42.1 4.6 %collective-permute-start.2 = (f32[160,128]{1,0:T(8,128)S(1)}, f32[160,128]{1,0:T(8,128)S(1)}, u32[]{:S(2)}, u32[]{:S(2)}) collective-permute-start(f32[160,128]{1,0:T(8,128)S(1)} %pad_maximum_fusion.near), channel_id=1, source_target_pairs={{384,0},{388,4},{392,8},{396,12},{400,16},{404,20},{408,24},{412,2... | collective-permute-start | bytes 245768 | tf_op jit(solution)/shard_map/ppermute | solution.py:432
  46.7 2.1 %collective-permute-done.2.away = f32[160,128]{1,0:T(8,128)S(1)} collective-permute-done((f32[160,128]{1,0:T(8,128)S(1)}, f32[160,128]{1,0:T(8,128)S(1)}, u32[]{:S(2)}, u32[]{:S(2)}) %collective-permute-start.2) | collective-permute-done | bytes 81952 | tf_op jit(solution)/shard_map/ppermute | solution.py:432
  48.8 0.0 all-to-all-done.1
  48.8 0.7 tile.1
  49.5 6.7 %all_to_all.25.parts = f32[4,24,128]{2,1,0:T(8,128)S(1)} all-to-all(f32[4,24,128]{2,1,0:T(8,128)S(1)} %tile.1), channel_id=1, replica_groups=mesh['dp'=128,'mp'=4] {'mp'}, dimensions={0} | all-to-all | bytes 98304 | tf_op jit(solution)/shard_map/all_to_all | solution.py:452
  56.3 23.6 %all_to_all.26.parts = f32[16,24,128]{2,1,0:T(8,128)S(1)} all-to-all(f32[16,24,128]{2,1,0:T(8,128)S(1)} %add.1), channel_id=1, replica_groups={{0,8,16,24,32,40,48,56,64,72,80,88,96,104,112,120},{4,12,20,28,36,44,52..., dimensions={0} | all-to-all | bytes 393216 | tf_op jit(solution)/shard_map/all_to_all | solution.py:422
  79.8 0.3 panel.1
  80.1 10.9 %all_to_all.27.mine = f32[4,272,128]{2,1,0:T(8,128)S(1)} all-to-all(f32[4,272,128]{2,1,0:T(8,128)S(1)} %panel.1), channel_id=1, replica_groups={{0,128,256,384},{4,132,260,388},{8,136,264,392},{12,140,268,396},{16,14..., dimensions={0} | all-to-all | bytes 1114112 | tf_op jit(solution)/shard_map/all_to_all | solution.py:422
  91.0 9.6 %collective-permute-start.3 = (f32[4,272,128]{2,1,0:T(8,128)S(1)}, f32[4,272,128]{2,1,0:T(8,128)S(1)}, u32[]{:S(2)}, u32[]{:S(2)}) collective-permute-start(f32[4,272,128]{2,1,0:T(8,128)S(1)} %all_to_all.27.mine), channel_id=1, source_target_pairs={{4,0},{0,4},{12,8},{8,12},{20,16},{16,20},{28,24},{24,28},{36,32},... | collective-permute-start | bytes 1671176 | tf_op jit(solution)/shard_map/ppermute | solution.py:432
  100.6 1.6 %collective-permute-done.3.theirs = f32[4,272,128]{2,1,0:T(8,128)S(1)} collective-permute-done((f32[4,272,128]{2,1,0:T(8,128)S(1)}, f32[4,272,128]{2,1,0:T(8,128)S(1)}, u32[]{:S(2)}, u32[]{:S(2)}) %collective-permute-start.3) | collective-permute-done | bytes 557088 | tf_op jit(solution)/shard_map/ppermute | solution.py:432
  102.1 15.1 %solve.1 = f32[4,32]{1,0:T(4,128)} custom-call(s32[1]{0:T(128)} %bitcast.pos, f32[4,272,128]{2,1,0:T(8,128)S(1)} %all_to_all.27.mine, f32[4,272,128]{2,1,0:T(8,128)S(1)} %collective-permute-done.3.theirs), custom_call_target="tpu_custom_call" | custom-call | tf_op jit(solution)/shard_map/solve/pallas_call | solution.py:401
  (4 shorter events, 0.0 us)
Async XLA Ops:
  0.0 14.9 %copy-start = (s32[4]{0:T(128)S(1)}, s32[4]{0:T(128)}, u32[]{:S(2)}) copy-start(s32[4]{0:T(128)} %tlen.1) | copy-start | bytes 52
  4.2 10.7 %all-to-all-start = ((f32[4,160,128]{2,1,0:T(8,128)}), f32[4,160,128]{2,1,0:T(8,128)S(1)}, u32[]{:S(2)}, u32[]{:S(2)}) async-start(f32[4,160,128]{2,1,0:T(8,128)} %project.1), calls=%async_computation | async-start | bytes 655360 | tf_op jit(solution)/shard_map/all_to_all | solution.py:445
  16.7 32.2 %all-to-all-start.1 = ((f32[16,32,128]{2,1,0:T(8,128)}), f32[16,32,128]{2,1,0:T(8,128)S(1)}, u32[]{:S(2)}, u32[]{:S(2)}) async-start(f32[16,32,128]{2,1,0:T(8,128)} %broadcast_in_dim.2), calls=%async_computation.1 | async-start | bytes 524288 | tf_op jit(solution)/shard_map/all_to_all | solution.py:422
  31.9 5.2 %collective-permute-start = (f32[40,128]{1,0:T(8,128)S(1)}, f32[40,128]{1,0:T(8,128)S(1)}, u32[]{:S(2)}, u32[]{:S(2)}) collective-permute-start(f32[40,128]{1,0:T(8,128)S(1)} %sketch.1), channel_id=1, source_target_pairs={{4,0},{0,4},{12,8},{8,12},{20,16},{16,20},{28,24},{24,28},{36,32},... | collective-permute-start | bytes 61448 | tf_op jit(solution)/shard_map/ppermute | solution.py:432
  37.0 5.0 %collective-permute-start.1 = (f32[80,128]{1,0:T(8,128)S(1)}, f32[80,128]{1,0:T(8,128)S(1)}, u32[]{:S(2)}, u32[]{:S(2)}) collective-permute-start(f32[80,128]{1,0:T(8,128)S(1)} %pad_maximum_fusion.1), channel_id=1, source_target_pairs={{128,0},{132,4},{136,8},{140,12},{144,16},{148,20},{152,24},{156,2... | collective-permute-start | bytes 122888 | tf_op jit(solution)/shard_map/ppermute | solution.py:432
  42.1 6.8 %collective-permute-start.2 = (f32[160,128]{1,0:T(8,128)S(1)}, f32[160,128]{1,0:T(8,128)S(1)}, u32[]{:S(2)}, u32[]{:S(2)}) collective-permute-start(f32[160,128]{1,0:T(8,128)S(1)} %pad_maximum_fusion.near), channel_id=1, source_target_pairs={{384,0},{388,4},{392,8},{396,12},{400,16},{404,20},{408,24},{412,2... | collective-permute-start | bytes 245768 | tf_op jit(solution)/shard_map/ppermute | solution.py:432
  91.0 11.2 %collective-permute-start.3 = (f32[4,272,128]{2,1,0:T(8,128)S(1)}, f32[4,272,128]{2,1,0:T(8,128)S(1)}, u32[]{:S(2)}, u32[]{:S(2)}) collective-permute-start(f32[4,272,128]{2,1,0:T(8,128)S(1)} %all_to_all.27.mine), channel_id=1, source_target_pairs={{4,0},{0,4},{12,8},{8,12},{20,16},{16,20},{28,24},{24,28},{36,32},... | collective-permute-start | bytes 1671176 | tf_op jit(solution)/shard_map/ppermute | solution.py:432
